TPU v7x, 32 devices: a whole 2x2x4 slice. The times are simulated.
32 devices in a mesh: dp: 16 (over z, x, core), seq: 2 (over y).
Axes of the slice: x: 2, y: 2, z: 4, core: 2. Of those that a mesh axis runs over, the one named last changes fastest.
Arguments:
- block_input: bfloat16 [16, 1024, 1024], P('dp', 'seq'), may hold values from -6 to 6
- doc_starts: int32 [16, 6], P('dp'), may hold values from 1 to 1023, as said below
- norm_in: bfloat16 [1024], P(('dp', 'seq')), may hold values from 0.5 to 1.5
- w_mix: bfloat16 [1024, 6144], P(('dp', 'seq')), may hold values from -0.1875 to 0.1875
- w_small: bfloat16 [1024, 24], P(('dp', 'seq')), may hold values from -0.1875 to 0.1875
- conv_w: bfloat16 [4, 5120], P(None, ('dp', 'seq')), may hold values from -3 to 3
- decay_log: bfloat16 [8], replicated, may hold values from -8 to -2.5
- norm_out: bfloat16 [128], replicated, may hold values from 0.5 to 1.5
- w_out: bfloat16 [1024, 1024], P(('dp', 'seq')), may hold values from -0.25 to 0.25
- norm_mlp: bfloat16 [1024], P(('dp', 'seq')), may hold values from 0.5 to 1.5
- w_gu: bfloat16 [1024, 5632], P(('dp', 'seq')), may hold values from -0.1875 to 0.1875
- w_down: bfloat16 [2816, 1024], P(('dp', 'seq')), may hold values from -0.15625 to 0.15625
- cotangent: bfloat16 [16, 1024, 1024], P('dp', 'seq'), may hold values from -6 to 6
Outputs:
- block_output: bfloat16 [16, 1024, 1024], P('dp', 'seq')
- input_grad: bfloat16 [16, 1024, 1024], P('dp', 'seq')
- grad_norm_in: float32 [1024], P(('dp', 'seq'))
- grad_mix: float32 [1024, 6144], P(('dp', 'seq'))
- grad_small: float32 [1024, 24], P(('dp', 'seq'))
- grad_conv: float32 [4, 5120], P(None, ('dp', 'seq'))
- grad_decay: float32 [8], replicated
- grad_norm_out: float32 [128], replicated
- grad_out: float32 [1024, 1024], P(('dp', 'seq'))
- grad_norm_mlp: float32 [1024], P(('dp', 'seq'))
- grad_gu: float32 [1024, 5632], P(('dp', 'seq'))
- grad_down: float32 [2816, 1024], P(('dp', 'seq'))
Inputs may be any that keep to these rules, and one draw needn't show every extreme that they name: `doc_starts`: each row's starts are strictly increasing; three lie among the row's first 512 positions and three among its last 512, so that one document covers the middle of every row.
All inputs are finite; a program needn't handle non-finite values.
Results may differ from a plain program's by a relative error of at most 0.012.
Values may be sent and summed in bfloat16 or wider, within the bound.
A program may use at most 320 MiB of HBM per device.

v0:
```python
from functools import partial

import jax
import jax.numpy as jnp
from jax import lax
from jax.sharding import PartitionSpec as P

H = 8
DK = 128
DV = 128
NH = 2
GROUP = 64


EPSILON = 1e-06
HIGHEST = lax.Precision.HIGHEST


def from_behind(block, axis, distance):
    devices = range(lax.axis_size(axis))
    route = [(i - distance, i) for i in devices if i - distance in devices]
    return lax.ppermute(block, axis, route)


def rms_scale(values, scale_gain):
    return (
        values * lax.rsqrt(jnp.mean(values * values, axis=-1, keepdims=True) + EPSILON) * scale_gain
    )


def swiglu(gate_up):
    half_width = gate_up.shape[-1] // 2
    return jax.nn.silu(gate_up[:, :half_width]) * gate_up[:, half_width:]


def segment_of(positions, starts):
    counted = jnp.sum((positions[:, :, None] >= starts[:, None, :]).astype(jnp.int32), axis=2)
    return jnp.where(positions < 0, -1, counted)


def gated_norm(mixed_out, out_gate, scale_gain):
    gated_out = rms_scale(mixed_out, scale_gain) * jax.nn.silu(out_gate.reshape(mixed_out.shape))
    return gated_out.reshape(mixed_out.shape[0], -1)


def matmul_heads(left_mat, right_mat):
    return jnp.einsum("rhab,rhbc->rhac", left_mat, right_mat, precision=HIGHEST)


def block_terms(seg_ext, channels_ext, gates_raw, decay_log, conv_taps):
    row_count, ext_len, channel_count = channels_ext.shape
    tap_count = conv_taps.shape[0]
    seg_len = ext_len - (tap_count - 1)
    seg_now = seg_ext[:, tap_count - 1 :]
    convolved = jnp.zeros((row_count, seg_len, channel_count), jnp.float32)
    for tap_index in range(tap_count):
        offset = tap_count - 1 - tap_index
        same_doc = (seg_ext[:, offset : offset + seg_len] == seg_now).astype(jnp.float32)
        convolved = (
            convolved
            + channels_ext[:, offset : offset + seg_len]
            * conv_taps[tap_index]
            * same_doc[:, :, None]
        )
    convolved = jax.nn.silu(convolved)
    key_width = H * DK
    queries = convolved[:, :, :key_width].reshape(row_count, seg_len, H, DK)
    queries = (
        queries
        * lax.rsqrt(jnp.sum(queries * queries, axis=-1, keepdims=True) + EPSILON)
        * DK ** (-0.5)
    )
    key_tok = convolved[:, :, key_width : 3 * key_width].reshape(row_count, seg_len, NH, H, DK)
    key_tok = key_tok * lax.rsqrt(jnp.sum(key_tok * key_tok, axis=-1, keepdims=True) + EPSILON)
    value_tok = convolved[:, :, 3 * key_width :].reshape(row_count, seg_len, NH, H, DV)
    beta_tok = jax.nn.sigmoid(gates_raw[:, :, : NH * H]).reshape(row_count, seg_len, NH, H)
    decay_tok = -jnp.exp(decay_log) * jax.nn.softplus(gates_raw[:, :, NH * H :])
    block_count = seg_len // GROUP
    span = NH * GROUP
    key_rows = key_tok.transpose(0, 3, 1, 2, 4).reshape(row_count, H, block_count, span, DK)
    value_rows = value_tok.transpose(0, 3, 1, 2, 4).reshape(row_count, H, block_count, span, DV)
    beta_rows = beta_tok.transpose(0, 3, 1, 2).reshape(row_count, H, block_count, span)
    gate_tok = jnp.concatenate(
        [decay_tok[..., None], jnp.zeros(decay_tok.shape + (NH - 1,), jnp.float32)], axis=-1
    )
    gate_rows = gate_tok.transpose(0, 2, 1, 3).reshape(row_count, H, block_count, span)
    query_rows = queries.transpose(0, 2, 1, 3).reshape(row_count, H, block_count, GROUP, DK)
    seg_rows = jnp.repeat(seg_now, NH, axis=1).reshape(row_count, block_count, span)
    seg_before = jnp.concatenate(
        [seg_ext[:, tap_count - 2 : tap_count - 1], seg_rows[:, :-1, -1]], axis=1
    )
    log_decay = jnp.cumsum(gate_rows, axis=-1)
    offsets = jnp.arange(span)
    causal = offsets[:, None] >= offsets[None, :]
    linked = ((seg_rows[:, :, :, None] == seg_rows[:, :, None, :]) & causal)[:, None]
    log_gap = log_decay[..., :, None] - log_decay[..., None, :]
    carried = jnp.where(linked, jnp.exp(jnp.where(linked, log_gap, 0.0)), 0.0)
    unbroken = (seg_rows == seg_before[..., None]).astype(jnp.float32)[:, None]
    carry_scale = jnp.exp(log_decay) * unbroken
    key_gram = jnp.einsum("rhcik,rhcjk->rhcij", key_rows, key_rows, precision=HIGHEST)
    strict = (offsets[:, None] > offsets[None, :]).astype(jnp.float32)
    lower_part = beta_rows[..., :, None] * carried * key_gram * strict
    right_side = jnp.concatenate(
        [beta_rows[..., None] * value_rows, (beta_rows * carry_scale)[..., None] * key_rows],
        axis=-1,
    )
    solved = jax.scipy.linalg.solve_triangular(
        lower_part, right_side, lower=True, unit_diagonal=True
    )
    value_part = solved[..., :DV]
    key_part = solved[..., DV:]
    reading = carried[..., NH - 1 :: NH, :] * jnp.einsum(
        "rhctk,rhcjk->rhctj", query_rows, key_rows, precision=HIGHEST
    )
    out_values = jnp.einsum("rhctj,rhcjv->rhctv", reading, value_part, precision=HIGHEST)
    out_keys = carry_scale[..., NH - 1 :: NH, None] * query_rows - jnp.einsum(
        "rhctj,rhcjk->rhctk", reading, key_part, precision=HIGHEST
    )
    tail_weight = carried[..., -1, :]
    transfer = carry_scale[..., -1][..., None, None] * jnp.eye(DK, dtype=jnp.float32) - jnp.einsum(
        "rhcjk,rhcj,rhcjl->rhckl", key_part, tail_weight, key_rows, precision=HIGHEST
    )
    inject = jnp.einsum(
        "rhcjv,rhcj,rhcjk->rhcvk", value_part, tail_weight, key_rows, precision=HIGHEST
    )
    return (out_values, out_keys, transfer, inject)


def chain_forward(transfer, inject, entry_state):

    def advance(state_now, pair_item):
        return (matmul_heads(state_now, pair_item[0]) + pair_item[1], state_now)

    final_state, entries = lax.scan(
        advance, entry_state, (jnp.moveaxis(transfer, 2, 0), jnp.moveaxis(inject, 2, 0))
    )
    return (final_state, entries)


def chain_backward(transfer, entries, local_grad, exit_grad):

    def retreat(grad_next, triple):
        matrix, entry_state, own_grad = triple
        grad_matrix = jnp.einsum("rhvk,rhvl->rhkl", entry_state, grad_next, precision=HIGHEST)
        grad_here = own_grad + jnp.einsum("rhvl,rhkl->rhvk", grad_next, matrix, precision=HIGHEST)
        return (grad_here, (grad_matrix, grad_next))

    grad_entry, (grad_transfer, grad_inject) = lax.scan(
        retreat,
        exit_grad,
        (jnp.moveaxis(transfer, 2, 0), entries, jnp.moveaxis(local_grad, 2, 0)),
        reverse=True,
    )
    return (grad_entry, jnp.moveaxis(grad_transfer, 0, 2), jnp.moveaxis(grad_inject, 0, 2))


def on_device(
    block_input,
    doc_starts,
    norm_in,
    w_mix,
    w_small,
    conv_w,
    decay_log,
    norm_out,
    w_out,
    norm_mlp,
    w_gu,
    w_down,
    cotangent,
):
    row_count, seg_len, model_width = block_input.shape
    tokens = row_count * seg_len
    tap_count = conv_w.shape[0]
    key_width = H * DK
    block_count = seg_len // GROUP
    norm_in_all, mix_all, small_all, conv_all, out_all = (
        lax.all_gather(norm_in, ("dp", "seq"), axis=0, tiled=True),
        lax.all_gather(w_mix, ("dp", "seq"), axis=0, tiled=True),
        lax.all_gather(w_small, ("dp", "seq"), axis=0, tiled=True),
        lax.all_gather(conv_w, ("dp", "seq"), axis=1, tiled=True),
        lax.all_gather(w_out, ("dp", "seq"), axis=0, tiled=True),
    )
    residual_in = block_input.astype(jnp.float32).reshape(tokens, model_width)
    normed, norm_in_back = jax.vjp(rms_scale, residual_in, norm_in_all.astype(jnp.float32))
    normed_low = normed.astype(jnp.bfloat16)
    projected = jnp.dot(normed_low, mix_all, preferred_element_type=jnp.float32)
    gates_raw = jnp.dot(normed_low, small_all, preferred_element_type=jnp.float32)
    channels = projected[:, : 5 * key_width].reshape(row_count, seg_len, 5 * key_width)
    out_gate = projected[:, 5 * key_width :]
    border = from_behind(channels[:, seg_len - tap_count + 1 :], "seq", 1)
    channels_ext = jnp.concatenate([border, channels], axis=1)
    positions = lax.axis_index("seq") * seg_len + jnp.arange(
        -(tap_count - 1), seg_len, dtype=jnp.int32
    )
    seg_ext = segment_of(
        jnp.broadcast_to(positions, (row_count, seg_len + tap_count - 1)), doc_starts
    )
    block_parts, terms_back = jax.vjp(
        partial(block_terms, seg_ext),
        channels_ext,
        gates_raw.reshape(row_count, seg_len, -1),
        decay_log.astype(jnp.float32),
        conv_all.astype(jnp.float32),
    )
    out_values, out_keys, transfer, inject = block_parts
    eye_block = jnp.broadcast_to(jnp.eye(DK, dtype=jnp.float32), (row_count, H, DK, DK))
    zero_state = jnp.zeros((row_count, H, DV, DK), jnp.float32)

    def compose_step(product, matrix):
        return (matmul_heads(product, matrix), None)

    device_transfer, unused = lax.scan(compose_step, eye_block, jnp.moveaxis(transfer, 2, 0))
    device_inject, unused_entries = chain_forward(transfer, inject, zero_state)

    def relay_state(turn_index, incoming):
        return from_behind(
            (matmul_heads(incoming, device_transfer) + device_inject).astype(jnp.bfloat16), "seq", 1
        ).astype(jnp.float32)

    entry_state = lax.fori_loop(0, lax.axis_size("seq") - 1, relay_state, zero_state)
    final_state, entries = chain_forward(transfer, inject, entry_state)
    entries_heads = jnp.moveaxis(entries, 0, 2)
    mixed_heads = out_values + jnp.einsum(
        "rhctk,rhcvk->rhctv", out_keys, entries_heads, precision=HIGHEST
    )
    mixed_tokens = mixed_heads.transpose(0, 2, 3, 1, 4).reshape(tokens, H, DV)
    normed_out, gated_back = jax.vjp(
        gated_norm, mixed_tokens, out_gate, norm_out.astype(jnp.float32)
    )
    normed_out_low = normed_out.astype(jnp.bfloat16)
    hidden = residual_in + jnp.dot(normed_out_low, out_all, preferred_element_type=jnp.float32)
    norm_mlp_all, gu_all, down_all = (
        lax.all_gather(norm_mlp, ("dp", "seq"), axis=0, tiled=True),
        lax.all_gather(w_gu, ("dp", "seq"), axis=0, tiled=True),
        lax.all_gather(w_down, ("dp", "seq"), axis=0, tiled=True),
    )
    mlp_in, norm_mlp_back = jax.vjp(rms_scale, hidden, norm_mlp_all.astype(jnp.float32))
    mlp_in_low = mlp_in.astype(jnp.bfloat16)
    gate_up = jnp.dot(mlp_in_low, gu_all, preferred_element_type=jnp.float32)
    activated, act_back = jax.vjp(swiglu, gate_up)
    activated_low = activated.astype(jnp.bfloat16)
    result = hidden + jnp.dot(activated_low, down_all, preferred_element_type=jnp.float32)
    block_output = result.astype(jnp.bfloat16).reshape(row_count, seg_len, model_width)
    gu_use, down_use = (
        lax.all_gather(w_gu, ("dp", "seq"), axis=0, tiled=True),
        lax.all_gather(w_down, ("dp", "seq"), axis=0, tiled=True),
    )
    d_result = cotangent.astype(jnp.float32).reshape(tokens, model_width)
    d_result_low = d_result.astype(jnp.bfloat16)
    grad_down = jnp.einsum(
        "nf,nd->fd", activated_low, d_result_low, preferred_element_type=jnp.float32
    )
    d_activated = jnp.einsum(
        "nd,fd->nf", d_result_low, down_use, preferred_element_type=jnp.float32
    )
    (d_gate_up,) = act_back(d_activated)
    d_gate_low = d_gate_up.astype(jnp.bfloat16)
    grad_gu = jnp.einsum("nd,nf->df", mlp_in_low, d_gate_low, preferred_element_type=jnp.float32)
    d_mlp_in = jnp.einsum("nf,df->nd", d_gate_low, gu_use, preferred_element_type=jnp.float32)
    d_hidden_norm, grad_norm_mlp = norm_mlp_back(d_mlp_in)
    d_hidden = d_result + d_hidden_norm
    grad_norm_mlp, grad_gu, grad_down = (
        lax.psum_scatter(grad_norm_mlp, ("dp", "seq"), scatter_dimension=0, tiled=True),
        lax.psum_scatter(grad_gu, ("dp", "seq"), scatter_dimension=0, tiled=True),
        lax.psum_scatter(grad_down, ("dp", "seq"), scatter_dimension=0, tiled=True),
    )
    mix_use, small_use, out_use = (
        lax.all_gather(w_mix, ("dp", "seq"), axis=0, tiled=True),
        lax.all_gather(w_small, ("dp", "seq"), axis=0, tiled=True),
        lax.all_gather(w_out, ("dp", "seq"), axis=0, tiled=True),
    )
    d_mixer_low = d_hidden.astype(jnp.bfloat16)
    grad_out = jnp.einsum(
        "nh,nd->hd", normed_out_low, d_mixer_low, preferred_element_type=jnp.float32
    )
    d_normed_out = jnp.einsum("nd,hd->nh", d_mixer_low, out_use, preferred_element_type=jnp.float32)
    d_mixed, d_out_gate, grad_norm_out = gated_back(d_normed_out)
    d_heads = d_mixed.reshape(row_count, block_count, GROUP, H, DV).transpose(0, 3, 1, 2, 4)
    d_out_keys = jnp.einsum("rhctv,rhcvk->rhctk", d_heads, entries_heads, precision=HIGHEST)
    local_grad = jnp.einsum("rhctv,rhctk->rhcvk", d_heads, out_keys, precision=HIGHEST)
    own_entry, unused_mats, unused_adds = chain_backward(transfer, entries, local_grad, zero_state)
    flipped = jnp.swapaxes(device_transfer, 2, 3)

    def relay_grad(turn_index, incoming):
        return from_behind(
            (matmul_heads(incoming, flipped) + own_entry).astype(jnp.bfloat16), "seq", -1
        ).astype(jnp.float32)

    exit_grad = lax.fori_loop(0, lax.axis_size("seq") - 1, relay_grad, zero_state)
    grad_entry, grad_transfer, grad_inject = chain_backward(
        transfer, entries, local_grad, exit_grad
    )
    d_channels_ext, d_gates_raw, grad_decay, grad_conv = terms_back(
        (d_heads, d_out_keys, grad_transfer, grad_inject)
    )
    returned = from_behind(
        d_channels_ext[:, : tap_count - 1].astype(jnp.bfloat16), "seq", -1
    ).astype(jnp.float32)
    d_channels = d_channels_ext[:, tap_count - 1 :]
    d_channels = jnp.concatenate(
        [
            d_channels[:, : seg_len - tap_count + 1],
            d_channels[:, seg_len - tap_count + 1 :] + returned,
        ],
        axis=1,
    )
    d_projected = jnp.concatenate([d_channels.reshape(tokens, -1), d_out_gate], axis=1).astype(
        jnp.bfloat16
    )
    d_gates_low = d_gates_raw.reshape(tokens, -1).astype(jnp.bfloat16)
    grad_mix = jnp.einsum("nd,nc->dc", normed_low, d_projected, preferred_element_type=jnp.float32)
    grad_small = jnp.einsum(
        "nd,nc->dc", normed_low, d_gates_low, preferred_element_type=jnp.float32
    )
    d_normed = jnp.einsum("nc,dc->nd", d_projected, mix_use, preferred_element_type=jnp.float32)
    d_normed = d_normed + jnp.einsum(
        "nc,dc->nd", d_gates_low, small_use, preferred_element_type=jnp.float32
    )
    d_input_norm, grad_norm_in = norm_in_back(d_normed)
    input_grad = (
        (d_hidden + d_input_norm).astype(jnp.bfloat16).reshape(row_count, seg_len, model_width)
    )
    grad_norm_in, grad_mix, grad_small, grad_conv, grad_out = (
        lax.psum_scatter(grad_norm_in, ("dp", "seq"), scatter_dimension=0, tiled=True),
        lax.psum_scatter(grad_mix, ("dp", "seq"), scatter_dimension=0, tiled=True),
        lax.psum_scatter(grad_small, ("dp", "seq"), scatter_dimension=0, tiled=True),
        lax.psum_scatter(grad_conv, ("dp", "seq"), scatter_dimension=1, tiled=True),
        lax.psum_scatter(grad_out, ("dp", "seq"), scatter_dimension=0, tiled=True),
    )
    grad_decay, grad_norm_out = lax.psum((grad_decay, grad_norm_out), ("dp", "seq"))
    return (
        block_output,
        input_grad,
        grad_norm_in,
        grad_mix,
        grad_small,
        grad_conv,
        grad_decay,
        grad_norm_out,
        grad_out,
        grad_norm_mlp,
        grad_gu,
        grad_down,
    )


def solution(mesh):
    in_specs = (
        P("dp", "seq", None),
        P("dp", None),
        P(("dp", "seq")),
        P(("dp", "seq"), None),
        P(("dp", "seq"), None),
        P(None, ("dp", "seq")),
        P(),
        P(),
        P(("dp", "seq"), None),
        P(("dp", "seq")),
        P(("dp", "seq"), None),
        P(("dp", "seq"), None),
        P("dp", "seq", None),
    )
    out_specs = (
        P("dp", "seq", None),
        P("dp", "seq", None),
        P(("dp", "seq")),
        P(("dp", "seq"), None),
        P(("dp", "seq"), None),
        P(None, ("dp", "seq")),
        P(),
        P(),
        P(("dp", "seq"), None),
        P(("dp", "seq")),
        P(("dp", "seq"), None),
        P(("dp", "seq"), None),
    )
    return jax.shard_map(
        on_device, mesh=mesh, in_specs=in_specs, out_specs=out_specs, check_vma=False
    )
```

profile of v0, /device:TPU:0, one launch (start us, length us, event | category | flops | bytes accessed | tf_op | source)
XLA Modules:
  0.0 2984.6 jit_solution(14332174423550219644)
XLA Ops:
  14.0 43.0 %all-reduce.27 = (bf16[1024]{0:T(1024)(128)(2,1)S(1)}, bf16[1024]{0:T(1024)(128)(2,1)S(1)}) all-reduce(bf16[1024]{0:T(1024)(128)(2,1)S(1)} %dynamic-update-slice, bf16[1024]{0:T(1024)(128)(2,1)S(1)} %dynamic-update-slice.1), channel_id=1, replica_groups=mesh['dp'=16,'seq'=2] {'dp','seq'}, use_global_device_ids=true, to_apply=%add.22 | all-reduce | flops 2048 | bytes 8192
  58.6 68.9 %all-gather = bf16[32,32,24]{1,2,0:T(8,128)(2,1)S(1)} all-gather(bf16[1,32,24]{1,2,0:T(8,128)(2,1)} %bitcast.735), channel_id=1, replica_groups=mesh['dp'=16,'seq'=2] {'dp','seq'}, dimensions={0}, use_global_device_ids=true | all-gather | bytes 50688 | tf_op jit(solution)/shard_map/all_gather | solution.py:180
  135.7 9.8 slice.124
  146.6 64.4 %all-gather.1 = bf16[32,160,4]{1,2,0:T(4,128)(2,1)S(1)} all-gather(bf16[1,160,4]{1,2,0:T(4,128)(2,1)S(1)} %bitcast.736), channel_id=1, replica_groups=mesh['dp'=16,'seq'=2] {'dp','seq'}, dimensions={0}, use_global_device_ids=true | all-gather | bytes 42240 | tf_op jit(solution)/shard_map/all_gather | solution.py:181
  215.8 9.5 fusion.221
  239.4 19.6 fusion.39
  288.8 9.1 fusion.230
  304.2 630.2 %custom-call.10 = f32[8,8,1,128,128]{3,4,2,1,0:T(8,128)} custom-call(f32[8,8,1,128,128]{4,3,2,1,0:T(8,128)} %add_bitcast_fusion.2), custom_call_target="InvertDiagBlocksLowerTriangular" | custom-call | tf_op jit(solution)/shard_map/jvp(jit(_solve_triangular))/vmap(vmap())/triangular_solve | solution.py:107
  942.2 11.7 fusion.40
  953.9 10.5 subtract_bitcast_fusion
  977.4 11.1 fusion.106
  994.0 15.3 while.73
  1010.3 14.3 while.72
  1030.8 13.2 bitcast_multiply_fusion.12
  1054.9 22.1 while.74
  1103.6 12.6 fusion.219
  1116.2 13.0 fusion.173
  1129.2 14.5 multiply_reduce_fusion.9
  1169.4 9.6 multiply_reduce_fusion.11
  1179.0 9.6 fusion.84
  1194.8 29.8 while.75
  1228.5 11.8 fusion.150
  1256.7 32.5 %pad.78 = f32[1,8,8,128,128]{4,3,2,1,0:T(8,128)} pad(f32[1,8,8,64,128]{4,3,2,1,0:T(8,128)} %multiply_bitcast_fusion.1, f32[]{:T(128)} %constant.182.clone.1), padding=0_0_0x0_0_0x0_0_0x1_0_1x0_0_0 | pad | bytes 6291460 | tf_op jit(solution)/shard_map/transpose(jvp())/pad | solution.py:112
  1290.3 9.9 fusion.129
  1305.3 46.4 %while.76 = (s32[]{:T(128)}, f32[1,8,128,128]{2,3,1,0:T(8,128)S(1)}, f32[8,1,8,128,128]{4,3,2,1,0:T(8,128)}, f32[8,1,8,128,128]{3,4,2,1,0:T(8,128)}, f32[8,1,8,1...) while((s32[]{:T(128)}, ...), condition=%wide.region_18.19_spmd, body=%wide.region_17.18_spmd.sunk | while | flops 402784256 | bytes 5769333 | solution.py:148
  1351.7 11.2 fusion.73
  1392.5 16.9 fusion.43
  1409.4 16.0 fusion.94
  1425.4 12.1 fusion.71
  1437.5 11.5 multiply_reduce_fusion.4
  1449.3 8.8 multiply_reduce_fusion.6
  1458.5 12.4 fusion.59
  1471.0 13.3 fusion.144
  1490.0 9.9 reduce_window_sum.23
  1500.5 13.1 fusion.58
  1543.7 28.6 multiply_reduce_fusion.3
  1581.2 9.5 fusion.165
  1591.5 14.8 multiply_multiply_fusion.2
  1606.3 15.1 fusion.226
  1631.6 11.9 fusion.69
  1644.2 15.7 fusion.171
  1670.2 14.3 fusion.110
  1684.6 37.2 %all-reduce.26 = (f32[1024]{0:T(1024)S(1)}, f32[8]{0:T(128)}, f32[128]{0:T(128)}, f32[1024]{0:T(1024)S(1)}) all-reduce(f32[1024]{0:T(1024)S(1)} %get-tuple-element.486, f32[8]{0:T(128)S(1)} %negate_multiply_fusion, f32[128]{0:T(128)S(1)} %copy-done.110, f32[1024]{0:T(1024)S(1)} %copy-done.106), channel_id=2, replica_groups=mesh['dp'=16,'seq'=2] {'dp','seq'}, use_global_device_ids=true, to_apply=%region_31.32.clone | all-reduce | flops 2184 | bytes 17472
  1727.6 116.3 %reduce-scatter.19.cloned.1.call-done = f32[32,24]{1,0:T(8,128)} async-done(((f32[1024,24]{1,0:T(8,128)}), f32[32,24]{1,0:T(8,128)}) %reduce-scatter.19.cloned.1.call-update) | async-done | bytes 3088
  1845.3 139.1 %reduce-scatter.13.cloned.1.call-done = f32[32,1024]{1,0:T(8,128)} async-done(((f32[1024,1024]{1,0:T(8,128)}), f32[32,1024]{1,0:T(8,128)}) %reduce-scatter.13.cloned.1.call-update) | async-done | bytes 131088 | tf_op jit(solution)/shard_map/reduce_scatter | solution.py:329
  1984.4 248.4 %reduce-scatter.17.cloned.1.call-done = f32[88,1024]{1,0:T(8,128)} async-done(((f32[2816,1024]{1,0:T(8,128)}), f32[88,1024]{1,0:T(8,128)}) %reduce-scatter.17.cloned.1.call-update) | async-done | bytes 360464 | tf_op jit(solution)/shard_map/reduce_scatter | solution.py:266
  2232.8 254.4 %reduce-scatter.11.cloned.1.call-done = f32[32,6144]{1,0:T(8,128)} async-done(((f32[1024,6144]{1,0:T(8,128)}), f32[32,6144]{1,0:T(8,128)}) %reduce-scatter.11.cloned.1.call-update) | async-done | bytes 786448 | tf_op jit(solution)/shard_map/reduce_scatter | solution.py:326
  2487.1 490.4 %reduce-scatter.15.cloned.1.call-done = f32[32,5632]{1,0:T(8,128)} async-done(((f32[1024,5632]{1,0:T(8,128)}), f32[32,5632]{1,0:T(8,128)}) %reduce-scatter.15.cloned.1.call-update) | async-done | bytes 720912 | tf_op jit(solution)/shard_map/reduce_scatter | solution.py:265
  (538 shorter events, 431.7 us)
Async XLA Ops:
  7.2 122.5 %copy-start.113 = (bf16[8]{0:T(256)(128)(2,1)S(1)}, bf16[8]{0:T(256)(128)(2,1)}, u32[]{:S(2)}) copy-start(bf16[8]{0:T(256)(128)(2,1)} %param.29) | copy-start | bytes 52
  7.2 208.6 %all-gather.7.cloned.1.call-start = ((), (), s32[]{:S(2)}) async-start(), calls=%async_computation.6 | async-start | bytes 12976128 | tf_op jit(solution)/shard_map/all_gather | solution.py:179
  7.9 1090.8 %all-gather.9.cloned.1.call-start = ((), (), s32[]{:S(2)}) async-start(), calls=%async_computation.7 | async-start | bytes 2162688 | tf_op jit(solution)/shard_map/all_gather | solution.py:182
  8.7 1094.9 %all-gather.11.cloned.1.call-start = ((), (), s32[]{:S(2)}) async-start(), calls=%async_computation.8 | async-start | bytes 11894784 | tf_op jit(solution)/shard_map/all_gather | solution.py:235
  9.4 1106.8 %all-gather.13.cloned.1.call-start = ((), (), s32[]{:S(2)}) async-start(), calls=%async_computation.9 | async-start | bytes 5947392 | tf_op jit(solution)/shard_map/all_gather | solution.py:236
  10.0 1716.1 %reduce-scatter.21.cloned.1.call-start = ((), (), s32[]{:S(2)}) async-start(), calls=%async_computation.15 | async-start | bytes 2703360
  10.9 228.4 %copy-start.96 = (f32[1,512]{1,0:T(1,128)}, f32[1,512]{1,0:T(1,128)S(1)}, u32[]{:S(2)}) copy-start(f32[1,512]{1,0:T(1,128)S(1)} %get-tuple-element.571) | copy-start | bytes 6148
  10.9 228.4 %copy-start.98 = (f32[1,512]{1,0:T(1,128)}, f32[1,512]{1,0:T(1,128)S(1)}, u32[]{:S(2)}) copy-start(f32[1,512]{1,0:T(1,128)S(1)} %get-tuple-element.572) | copy-start | bytes 6148
  10.9 228.4 %copy-start.100 = (f32[1,512]{1,0:T(1,128)}, f32[1,512]{1,0:T(1,128)S(1)}, u32[]{:S(2)}) copy-start(f32[1,512]{1,0:T(1,128)S(1)} %get-tuple-element.573) | copy-start | bytes 6148
  57.0 158.8 %copy-start.67 = (f32[1024]{0:T(1024)}, f32[1024]{0:T(1024)S(1)}, u32[]{:S(2)}) copy-start(f32[1024]{0:T(1024)S(1)} %convert_element_type.132) | copy-start | bytes 12292
  58.5 68.9 %copy-start.102 = (f32[512]{0:T(512)}, f32[512]{0:T(512)S(1)}, u32[]{:S(2)}) copy-start(f32[512]{0:T(512)S(1)} %fusion.111) | copy-start | bytes 6148
  58.6 157.3 %copy-start.79 = (f32[512]{0:T(512)}, f32[512]{0:T(512)S(1)}, u32[]{:S(2)}) copy-start(f32[512]{0:T(512)S(1)} %fusion.203) | copy-start | bytes 6148
  129.7 15.8 copy-start.107
  132.7 165.2 %copy-start.48 = (f32[1,8,8,128]{3,2,1,0:T(8,128)}, f32[1,8,8,128]{3,2,1,0:T(8,128)S(1)}, u32[]{:S(2)}) copy-start(f32[1,8,8,128]{3,2,1,0:T(8,128)S(1)} %reduce_window_sum.22) | copy-start | bytes 98308
  132.9 165.0 %copy-start.50 = (pred[8,128,128]{2,1,0:T(8,128)(4,1)}, pred[8,128,128]{2,1,0:T(8,128)(4,1)S(1)}, u32[]{:S(2)}) copy-start(pred[8,128,128]{2,1,0:T(8,128)(4,1)S(1)} %compare_and_fusion) | copy-start | bytes 393220
  135.7 80.2 %copy-start.44 = (bf16[1,512,1024]{2,1,0:T(8,128)(2,1)S(1)}, bf16[1,512,1024]{2,1,0:T(8,128)(2,1)}, u32[]{:S(2)}) copy-start(bf16[1,512,1024]{2,1,0:T(8,128)(2,1)} %param.23) | copy-start | bytes 3145732
  146.5 807.4 %copy-start.60 = (f32[128,128]{1,0:T(8,128)}, f32[128,128]{1,0:T(8,128)S(1)}, u32[]{:S(2)}) copy-start(f32[128,128]{1,0:T(8,128)S(1)} %fusion.185) | copy-start | bytes 196612
  146.5 67.4 %copy-start.104 = (f32[128]{0:T(128)}, f32[128]{0:T(128)S(1)}, u32[]{:S(2)}) copy-start(f32[128]{0:T(128)S(1)} %convert_element_type.140) | copy-start | bytes 1540
  211.1 28.2 copy-start.85
  211.2 28.2 copy-start.87
  211.2 28.2 copy-start.89
  211.2 28.2 copy-start.91
  211.6 722.8 %copy-start.58 = (f32[8,8,128]{2,1,0:T(8,128)}, f32[8,8,128]{2,1,0:T(8,128)S(1)}, u32[]{:S(2)}) copy-start(f32[8,8,128]{2,1,0:T(8,128)S(1)} %copy.405) | copy-start | bytes 98308
  212.5 721.9 %copy-start.71 = (f32[8,8,128]{2,1,0:T(8,128)}, f32[8,8,128]{2,1,0:T(8,128)S(1)}, u32[]{:S(2)}) copy-start(f32[8,8,128]{2,1,0:T(8,128)S(1)} %multiply_multiply_fusion.5) | copy-start | bytes 98308
  212.6 85.4 %copy-start.56 = (f32[128,128]{1,0:T(8,128)}, f32[128,128]{1,0:T(8,128)S(1)}, u32[]{:S(2)}) copy-start(f32[128,128]{1,0:T(8,128)S(1)} %get-tuple-element.588) | copy-start | bytes 196612
  212.6 85.4 %copy-start.65 = (pred[128,128]{1,0:T(8,128)(4,1)}, pred[128,128]{1,0:T(8,128)(4,1)S(1)}, u32[]{:S(2)}) copy-start(pred[128,128]{1,0:T(8,128)(4,1)S(1)} %get-tuple-element.587) | copy-start | bytes 49156
  213.9 929.9 %copy-start.63 = (f32[1024]{0:T(1024)}, f32[1024]{0:T(1024)S(1)}, u32[]{:S(2)}) copy-start(f32[1024]{0:T(1024)S(1)} %convert_element_type.142) | copy-start | bytes 12292
  231.5 7.9 collective-permute-start
  239.3 19.7 copy-start.69
  993.9 16.3 copy-start.76
  1025.8 25.6 collective-permute-start.1
  1103.5 40.3 %copy-start.77 = (f32[512]{0:T(512)}, f32[512]{0:T(512)S(1)}, u32[]{:S(2)}) copy-start(f32[512]{0:T(512)S(1)} %fusion.204) | copy-start | bytes 6148
  1160.8 18.2 copy-start.19
  1160.8 18.2 slice-start
  1227.2 73.0 %collective-permute-start.2 = (bf16[1,8,128,128]{3,2,1,0:T(8,128)(2,1)}, bf16[1,8,128,128]{3,2,1,0:T(8,128)(2,1)S(1)}, u32[]{:S(2)}, u32[]{:S(2)}) collective-permute-start(bf16[1,8,128,128]{3,2,1,0:T(8,128)(2,1)} %fusion.159), channel_id=1, source_target_pairs={{1,0},{3,2},{5,4},{7,6},{9,8},{11,10},{13,12},{15,14},{17,16},{19,... | collective-permute-start | bytes 786440 | tf_op jit(solution)/shard_map/while/body/eval_jaxpr/ppermute | solution.py:22
  1256.7 33.6 %copy-start.15 = (f32[1,8,512,128]{3,2,1,0:T(8,128)S(1)}, f32[1,8,512,128]{3,2,1,0:T(8,128)}, u32[]{:S(2)}) copy-start(f32[1,8,512,128]{3,2,1,0:T(8,128)} %copy.400) | copy-start | bytes 6291460
  1409.4 16.0 copy-start.23
  1409.4 28.1 copy-start.49
  1409.4 28.1 copy-start.51
  1409.4 28.1 copy-start.57
  1409.4 28.1 copy-start.66
  1574.7 269.3 %reduce-scatter.19.cloned.1.call-start = ((), (), s32[]{:S(2)}) async-start(), calls=%async_computation.14 | async-start | bytes 540672
  1576.2 408.2 %reduce-scatter.13.cloned.1.call-start = ((), (), s32[]{:S(2)}) async-start(), calls=%async_computation.11 | async-start | bytes 4325376 | tf_op jit(solution)/shard_map/reduce_scatter | solution.py:329
  1581.1 651.6 %reduce-scatter.17.cloned.1.call-start = ((), (), s32[]{:S(2)}) async-start(), calls=%async_computation.13 | async-start | bytes 11894784 | tf_op jit(solution)/shard_map/reduce_scatter | solution.py:266
  1590.8 896.4 %reduce-scatter.11.cloned.1.call-start = ((), (), s32[]{:S(2)}) async-start(), calls=%async_computation.10 | async-start | bytes 25952256 | tf_op jit(solution)/shard_map/reduce_scatter | solution.py:326
  1621.4 6.5 collective-permute-start.3
  1643.6 1334.0 %reduce-scatter.15.cloned.1.call-start = ((), (), s32[]{:S(2)}) async-start(), calls=%async_computation.12 | async-start | bytes 23789568 | tf_op jit(solution)/shard_map/reduce_scatter | solution.py:265
  1670.2 52.7 %copy-start.103 = (f32[512]{0:T(512)S(1)}, f32[512]{0:T(512)}, u32[]{:S(2)}) copy-start(f32[512]{0:T(512)} %copy-done.102) | copy-start | bytes 6148
  (83 other events, 539.0 us)
Sparse Core Ops, SparseCore 0:
  10.9 101.9 all-gather.6
  116.0 54.8 all-gather.8
  173.7 89.9 all-gather.10
  266.5 68.5 all-gather.12
  1574.8 136.5 reduce-scatter.20
  1713.5 130.3 reduce-scatter.18
  1846.9 137.4 reduce-scatter.12
  1987.4 245.3 reduce-scatter.16
  2240.9 246.1 reduce-scatter.10
  2489.8 487.6 reduce-scatter.14
where the time goes:
time: 3000 us; the launch traced here: 2980 us
  waiting for transfers between devices  1260 us (42%)
  other arithmetic  803 us (27%)
  matrix products  493 us (16%)
  blocking collectives  213 us (7%)
  local copies, waits for them, and re-layouts  187 us (6%)
    another operation x5, other arithmetic, block_terms(): jax.scipy.linalg.solve_triangular(lower_part, right_side, lower=True, uni...  635 us
    reduce_scatter x1, waiting for transfers between devices, on_device(): lax.psum_scatter(grad_gu, ('dp', 'seq'), scatter_dimension=0, tiled=True)  490 us
    reduce_scatter x1, waiting for transfers between devices, on_device(): lax.psum_scatter(grad_mix, ('dp', 'seq'), scatter_dimension=0, tiled=True)  254 us
    reduce_scatter x1, waiting for transfers between devices, on_device(): lax.psum_scatter(grad_down, ('dp', 'seq'), scatter_dimension=0, tiled=True)  248 us
    reduce_scatter x1, waiting for transfers between devices, on_device(): lax.psum_scatter(grad_out, ('dp', 'seq'), scatter_dimension=0, tiled=True)  139 us
    unnamed x12, waiting for transfers between devices  119 us
    unnamed x2, blocking collectives  80.2 us
    all_gather x1, blocking collectives, on_device(): lax.all_gather(w_small, ('dp', 'seq'), axis=0, tiled=True)  68.9 us
  transfers between devices with their start and end apart: 14, of which 7 were waited for; matrix products, arithmetic and copies ran while one was open for 36% of the time, Pallas kernels for 0%

commit v1 on v0

v1 whole, which is shorter than its diff:
```python
from functools import partial

import jax
import jax.numpy as jnp
from jax import lax
from jax.experimental import pallas as pl
from jax.experimental.pallas import tpu as pltpu
from jax.sharding import PartitionSpec as P

H = 8
DK = 128
DV = 128
NH = 2
GROUP = 64
SPAN = NH * GROUP
LEVELS = 6
EPSILON = 1e-06
HIGHEST = lax.Precision.HIGHEST
LIMIT = 50 * 1024 * 1024


def mm(left, right, left_dim=1, right_dim=0):
    return lax.dot_general(
        left.astype(jnp.bfloat16),
        right.astype(jnp.bfloat16),
        (((left_dim,), (right_dim,)), ((), ())),
        preferred_element_type=jnp.float32,
    )


def iotas(rows, columns):
    return (
        lax.broadcasted_iota(jnp.int32, (rows, columns), 0),
        lax.broadcasted_iota(jnp.int32, (rows, columns), 1),
    )


def order_masks():
    row, column = iotas(SPAN, SPAN)
    row_tok, column_tok = row % GROUP, column % GROUP
    row_step, column_step = row // GROUP, column // GROUP
    pair = (row_tok == column_tok) & (row_step > column_step)
    strict = (row_tok > column_tok) | pair
    levels = []
    for level in range(LEVELS):
        row_half, column_half = row_tok >> level, column_tok >> level
        levels.append((row_half == column_half + 1) & (row_half % 2 == 1))
    eye = jnp.where(row == column, 1.0, 0.0)
    return strict, pair, levels, eye


def unit_inverses(lowers, pair, levels, eye):
    inverses = [eye - jnp.where(pair, lower, 0.0) for lower in lowers]
    for level in levels:
        parts = [mm(jnp.where(level, lower, 0.0), inv) for lower, inv in zip(lowers, inverses)]
        inverses = [inv - mm(inv, part) for part, inv in zip(parts, inverses)]
    return inverses


def silu_pair(values):
    sig = jax.nn.sigmoid(values)
    return values * sig, sig


def conv_block(channel_ref, border_ref, tap_ref, mask_ref, ext_ref):
    length = channel_ref.shape[0]
    ext_ref[0:8, :] = border_ref[...]
    ext_ref[8 : 8 + length, :] = channel_ref[...]
    summed = channel_ref[...] * tap_ref[0:1, :]
    for tap in range(1, 4):
        summed = summed + ext_ref[8 - tap : 8 - tap + length, :] * tap_ref[tap : tap + 1, :] * mask_ref[tap - 1]
    return summed


def unit_rows(values):
    inv = lax.rsqrt(jnp.sum(values * values, axis=1, keepdims=True) + EPSILON)
    return values * inv, inv


def chunk_vectors(vec_ref, chunk):
    rows = vec_ref[0, chunk]
    columns = jnp.transpose(rows)
    return rows, columns


def link_matrix(rows, columns):
    row, column = iotas(GROUP, SPAN)
    linked = (columns[:GROUP, 2:3] == rows[2:3, :]) & (row >= column % GROUP)
    return jnp.exp(jnp.where(linked, columns[:GROUP, 0:1] - rows[0:1, :], -1e30))


def twice(values):
    return jnp.concatenate([values, values], axis=0)


def forward_kernel(
    q_in, k0_in, k1_in, v0_in, v1_in,
    bq, bk0, bk1, bv0, bv1,
    tq, tk0, tk1, tv0, tv1,
    mask_ref, vec_ref, start_ref,
    x_out, w_out, u_out, t_out, i_out, ok_out, o_out, state_out,
    ext_ref, q_ref, k_ref, v_ref,
):
    length = q_in.shape[0]
    chunks = length // GROUP
    conv = []
    for channel, border, tap in (
        (q_in, bq, tq), (k0_in, bk0, tk0), (k1_in, bk1, tk1), (v0_in, bv0, tv0), (v1_in, bv1, tv1),
    ):
        conv.append(silu_pair(conv_block(channel, border, tap, mask_ref, ext_ref))[0])
    q_ref[...] = unit_rows(conv[0])[0] * DK ** (-0.5)
    for step in range(NH):
        k_ref[step] = unit_rows(conv[1 + step])[0]
        v_ref[step] = conv[1 + NH + step]
    strict, pair, levels, eye = order_masks()
    items = []
    lowers = []
    for chunk in range(chunks):
        here = slice(chunk * GROUP, (chunk + 1) * GROUP)
        rows, columns = chunk_vectors(vec_ref, chunk)
        keys = k_ref[:, here, :].reshape(SPAN, DK)
        values = v_ref[:, here, :].reshape(SPAN, DV)
        queries = q_ref[here, :]
        link = link_matrix(rows, columns)
        lower = jnp.where(strict, columns[:, 1:2] * twice(link) * mm(keys, keys, 1, 1), 0.0)
        reading = link * mm(queries, keys, 1, 1)
        lowers.append(lower)
        items.append((rows, columns, keys, values, queries, reading))
    inverses = unit_inverses(lowers, pair, levels, eye)
    state = start_ref[0]
    for chunk in range(chunks):
        rows, columns, keys, values, queries, reading = items[chunk]
        inverse = inverses[chunk]
        here = slice(chunk * GROUP, (chunk + 1) * GROUP)
        beta, scale, tail = columns[:, 1:2], columns[:, 3:4], columns[:, 4:5]
        key_part = mm(inverse, beta * scale * keys)
        value_part = mm(inverse, beta * values)
        tail_keys = tail * keys
        transfer = mm(key_part, tail_keys, 0, 0)
        inject = mm(value_part, tail_keys, 0, 0)
        x_out[0, chunk] = inverse.astype(x_out.dtype)
        w_out[0, chunk] = key_part.astype(w_out.dtype)
        u_out[0, chunk] = value_part.astype(u_out.dtype)
        t_out[0, chunk] = transfer.astype(t_out.dtype)
        i_out[0, chunk] = inject
        ok_out[0, chunk] = (columns[:GROUP, 3:4] * queries - mm(reading, key_part)).astype(ok_out.dtype)
        o_out[0, chunk] = mm(reading, value_part)
        state = rows[3:4, GROUP - 1 : GROUP] * state - mm(state, transfer) + inject
    state_out[0] = state


def chain_kernel(vec_ref, t_in, start_ref, state_out):
    chunks = t_in.shape[1]
    state = start_ref[0]
    for chunk in range(chunks):
        state = vec_ref[0, chunk, 3:4, GROUP - 1 : GROUP] * state - mm(state, t_in[0, chunk])
    state_out[0] = state


def readout_kernel(vec_ref, w_in, u_in, t_in, i_in, ok_in, o_in, entry_ref, gate_ref, gain_ref, gated_out, mixed_out, u_out, s_out):
    chunks = w_in.shape[1]
    state = entry_ref[0]
    states = []
    for chunk in range(chunks):
        states.append(state)
        state = vec_ref[0, chunk, 3:4, GROUP - 1 : GROUP] * state - mm(state, t_in[0, chunk]) + i_in[0, chunk]
    for chunk in range(chunks):
        here = slice(chunk * GROUP, (chunk + 1) * GROUP)
        state = states[chunk].astype(jnp.bfloat16)
        s_out[0, chunk] = state
        u_out[0, chunk] = (u_in[0, chunk].astype(jnp.float32) - mm(w_in[0, chunk], state, 1, 1)).astype(u_out.dtype)
        mixed = o_in[0, chunk] + mm(ok_in[0, chunk], state, 1, 1)
        mixed_out[here, :] = mixed
        inv = lax.rsqrt(jnp.mean(mixed * mixed, axis=1, keepdims=True) + EPSILON)
        gate = silu_pair(gate_ref[here, :])[0]
        gated_out[here, :] = (mixed * inv * gain_ref[0:1, :] * gate).astype(gated_out.dtype)


def readout_back_kernel(vec_ref, t_in, ok_in, mixed_in, gate_ref, gain_ref, d_ref, start_ref, d_mixed_out, d_gate_out, local_out, state_out, gain_out):
    chunks = t_in.shape[1]
    gain = gain_ref[0:1, :]
    gain_grad = jnp.zeros((1, DV), jnp.float32)
    locals_ = []
    for chunk in range(chunks):
        here = slice(chunk * GROUP, (chunk + 1) * GROUP)
        mixed = mixed_in[here, :]
        inv = lax.rsqrt(jnp.mean(mixed * mixed, axis=1, keepdims=True) + EPSILON)
        unit = mixed * inv
        gate = gate_ref[here, :]
        open_, sig = silu_pair(gate)
        d_gated = d_ref[here, :]
        d_scaled = d_gated * open_
        d_gate_out[here, :] = (d_gated * unit * gain * sig * (1.0 + gate * (1.0 - sig))).astype(d_gate_out.dtype)
        gain_grad = gain_grad + jnp.sum(d_scaled * unit, axis=0, keepdims=True)
        d_unit = d_scaled * gain
        d_mixed = inv * (d_unit - unit * jnp.mean(d_unit * unit, axis=1, keepdims=True))
        d_mixed_low = d_mixed.astype(jnp.bfloat16)
        d_mixed_out[here, :] = d_mixed_low
        local = mm(d_mixed_low, ok_in[0, chunk], 0, 0)
        local_out[0, chunk] = local
        locals_.append(local)
    gain_out[0] = jnp.broadcast_to(gain_grad, (8, DV))
    state = start_ref[0]
    for chunk in reversed(range(chunks)):
        state = vec_ref[0, chunk, 3:4, GROUP - 1 : GROUP] * state - mm(state, t_in[0, chunk], 1, 1) + locals_[chunk]
    state_out[0] = state


def backward_kernel(
    q_in, k0_in, k1_in, v0_in, v1_in,
    bq, bk0, bk1, bv0, bv1,
    tq, tk0, tk1, tv0, tv1,
    mask_ref, vec_ref, t_in, x_in, u_in, s_in, d_mixed_in, local_in, exit_ref,
    dq_out, dk0_out, dk1_out, dv0_out, dv1_out,
    eq_out, ek0_out, ek1_out, ev0_out, ev1_out,
    gq_out, gk0_out, gk1_out, gv0_out, gv1_out,
    d_vec_out,
    ext_ref, pre_ref, q_ref, k_ref, v_ref, inv_ref, d_ref, z_ref,
):
    length = q_in.shape[0]
    chunks = length // GROUP
    channels = (q_in, k0_in, k1_in, v0_in, v1_in)
    taps = (tq, tk0, tk1, tv0, tv1)
    for part, (channel, border, tap) in enumerate(zip(channels, (bq, bk0, bk1, bv0, bv1), taps)):
        pre = conv_block(channel, border, tap, mask_ref, ext_ref.at[part])
        pre_ref[part] = pre
        value = silu_pair(pre)[0]
        if part == 0:
            unit, inv = unit_rows(value)
            q_ref[...] = unit * DK ** (-0.5)
            inv_ref[0] = jnp.broadcast_to(inv, (length, DK))
        elif part <= NH:
            unit, inv = unit_rows(value)
            k_ref[part - 1] = unit
            inv_ref[part] = jnp.broadcast_to(inv, (length, DK))
        else:
            v_ref[part - 1 - NH] = value
    strict, pair, levels, eye = order_masks()
    column_index = iotas(SPAN, 8)[1]
    exit_grads = [None] * chunks
    grad = exit_ref[0]
    for chunk in reversed(range(chunks)):
        exit_grads[chunk] = grad
        grad = vec_ref[0, chunk, 3:4, GROUP - 1 : GROUP] * grad - mm(grad, t_in[0, chunk], 1, 1) + local_in[0, chunk]
    for chunk in reversed(range(chunks)):
        here = slice(chunk * GROUP, (chunk + 1) * GROUP)
        rows, columns = chunk_vectors(vec_ref, chunk)
        beta, scale, tail = columns[:, 1:2], columns[:, 3:4], columns[:, 4:5]
        keys = k_ref[:, here, :].reshape(SPAN, DK)
        values = v_ref[:, here, :].reshape(SPAN, DV)
        queries = q_ref[here, :]
        link = link_matrix(rows, columns)
        link_gram = jnp.where(strict, twice(link) * mm(keys, keys, 1, 1), 0.0)
        reading = link * mm(queries, keys, 1, 1)
        d_exit = exit_grads[chunk]
        solved = u_in[0, chunk]
        entry = s_in[0, chunk]
        d_mixed = d_mixed_in[here, :]
        tail_keys = tail * keys
        d_solved = mm(reading, d_mixed, 0, 0) + mm(tail_keys, d_exit, 1, 1)
        d_right = mm(x_in[0, chunk], d_solved, 0, 0)
        d_lower = jnp.where(strict, -mm(d_right, solved, 1, 1), 0.0)
        d_tail_keys = mm(solved, d_exit)
        d_right_entry = mm(d_right, entry)
        d_reading = mm(d_mixed, solved, 1, 1)
        d_query_entry = mm(d_mixed, entry)
        both_scale = -jnp.sum(d_right_entry * keys, axis=1, keepdims=True)
        lower_weight = d_lower * link_gram
        d_beta = (
            jnp.sum(d_right * values, axis=1, keepdims=True)
            + scale * both_scale
            + jnp.sum(lower_weight, axis=1, keepdims=True)
        )
        lower_moment = lower_weight * beta
        reading_moment = d_reading * reading
        d_gram = beta * twice(link) * d_lower
        d_gram = d_gram + jnp.transpose(d_gram)
        d_query_gram = link * d_reading
        d_keys = (
            tail * d_tail_keys
            - beta * scale * d_right_entry
            + mm(d_gram, keys)
            + mm(d_query_gram, queries, 0, 0)
        )
        d_queries = mm(d_query_gram, keys) + scale[:GROUP] * d_query_entry
        d_values = beta * d_right
        none = jnp.zeros((GROUP, 1), jnp.float32)
        d_gap = jnp.sum(lower_moment, axis=1, keepdims=True) + jnp.concatenate(
            [jnp.sum(reading_moment, axis=1, keepdims=True), none], axis=0
        )
        last = jnp.sum(jnp.sum(d_exit * entry.astype(jnp.float32), axis=1, keepdims=True), axis=0, keepdims=True)
        own_scale = jnp.sum(d_query_entry * queries, axis=1, keepdims=True)
        own_scale = own_scale + jnp.where(iotas(GROUP, 1)[0] == GROUP - 1, last, 0.0)
        d_scale = beta * both_scale + jnp.concatenate([own_scale, none], axis=0)
        d_tail = jnp.sum(d_tail_keys * keys, axis=1, keepdims=True)
        grads = jnp.where(
            column_index == 0,
            d_gap,
            jnp.where(
                column_index == 1,
                d_beta,
                jnp.where(column_index == 3, d_scale, jnp.where(column_index == 4, d_tail, 0.0)),
            ),
        )
        grads = jnp.transpose(grads)
        sums = jnp.sum(lower_moment, axis=0, keepdims=True) + jnp.sum(reading_moment, axis=0, keepdims=True)
        grads = grads - jnp.where(iotas(8, SPAN)[0] == 0, sums, 0.0)
        d_vec_out[0, chunk] = grads
        d_ref[0, here, :] = d_queries
        for step in range(NH):
            mine = slice(step * GROUP, (step + 1) * GROUP)
            d_ref[1 + step, here, :] = d_keys[mine]
            d_ref[1 + NH + step, here, :] = d_values[mine]
    outs = (dq_out, dk0_out, dk1_out, dv0_out, dv1_out)
    edges = (eq_out, ek0_out, ek1_out, ev0_out, ev1_out)
    tap_grads = (gq_out, gk0_out, gk1_out, gv0_out, gv1_out)
    z_ref[0:8, :] = jnp.zeros((8, DK), jnp.float32)
    z_ref[8 + length : 16 + length, :] = jnp.zeros((8, DK), jnp.float32)
    for part in range(1 + 2 * NH):
        grad = d_ref[part]
        if part <= NH:
            unit = q_ref[...] * DK ** 0.5 if part == 0 else k_ref[part - 1]
            if part == 0:
                grad = grad * DK ** (-0.5)
            grad = inv_ref[part] * (grad - unit * jnp.sum(grad * unit, axis=1, keepdims=True))
        pre = pre_ref[part]
        sig = jax.nn.sigmoid(pre)
        grad = grad * sig * (1.0 + pre * (1.0 - sig))
        tap = taps[part]
        total = grad * tap[0:1, :]
        edge = jnp.zeros((8, DK), jnp.float32)
        tap_rows = [jnp.sum(grad * channels[part][...], axis=0, keepdims=True)]
        for index in range(1, 4):
            shifted = grad * mask_ref[index - 1]
            tap_rows.append(
                jnp.sum(shifted * ext_ref[part, 8 - index : 8 - index + length, :], axis=0, keepdims=True)
            )
            z_ref[8 : 8 + length, :] = shifted * tap[index : index + 1, :]
            total = total + z_ref[8 + index : 8 + index + length, :]
            edge = edge + z_ref[index : index + 8, :]
        outs[part][...] = total.astype(outs[part].dtype)
        edges[part][0:8, :] = edge
        edges[part][8:16, :] = total[length - 8 :, :]
        tap_grads[part][...] = jnp.concatenate(tap_rows + [jnp.zeros((4, DK), jnp.float32)], axis=0)


MESH = pl.DeviceIdType.MESH
ZS = 4
STACK = (ZS, 2, 2, 2)
STAGES = 6


def place():
    dp, seq = lax.axis_index("dp"), lax.axis_index("seq")
    return dp // 4, (dp // 2) % 2, dp % 2, seq


def device_at(z, x, core, y):
    return (z * 4 + x * 2 + core, y)


def peers():
    z, x, core, y = place()
    ring = [device_at((z + step) % ZS, x, core, y) for step in range(1, ZS)]
    return ring + [device_at(z, 1 - x, core, y), device_at(z, x, core, 1 - y), device_at(z, x, 1 - core, y)]


def meet(devices):
    barrier = pltpu.get_barrier_semaphore()
    for device in devices:
        pl.semaphore_signal(barrier, inc=1, device_id=device, device_id_type=MESH)
    pl.semaphore_wait(barrier, len(devices))


class Gather:
    def __init__(self, source, target, x_first, sems, index):
        self.source, self.target, self.x_first = source, target, x_first
        self.send, self.recv, self.local = sems
        self.index = index
        self.copies = []

    def remote(self, source, target, slot):
        copy = pltpu.make_async_remote_copy(
            src_ref=source, dst_ref=target,
            send_sem=self.send.at[self.index, slot], recv_sem=self.recv.at[self.index, slot],
            device_id=peers()[slot], device_id_type=MESH,
        )
        copy.start()
        self.copies.append(copy)
        return copy

    def begin(self):
        z, x, core, y = place()
        mine = self.target(z, x, core, y)
        self.own = pltpu.make_async_copy(self.source, mine, self.local.at[self.index])
        self.own.start()
        self.waiting = [self.remote(self.source, mine, slot) for slot in range(ZS - 1)]

    def second(self):
        z, x, core, y = place()
        self.own.wait()
        for copy in self.waiting:
            copy.wait_recv()
        block = self.target(slice(None), x, core, y)
        self.waiting = [self.remote(block, block, ZS - 1 if self.x_first else ZS)]

    def third(self):
        z, x, core, y = place()
        self.waiting[0].wait_recv()
        every = slice(None)
        block = self.target(every, every, core, y) if self.x_first else self.target(every, x, core, every)
        self.waiting = [self.remote(block, block, ZS if self.x_first else ZS - 1)]

    def fourth(self):
        z, x, core, y = place()
        self.waiting[0].wait_recv()
        every = slice(None)
        block = self.target(every, every, core, every)
        self.waiting = [self.remote(block, block, ZS + 1)]

    def finish(self):
        self.waiting[0].wait_recv()
        for copy in self.copies:
            copy.wait_send()


def columns_of(ref, first, width):
    return lambda z, x, core, y: ref.at[z, x, core, y, :, pl.ds(first, width)]


def gather_project_kernel(
    x_ref, small_in, mix_in, out_in,
    mix_out, out_out, small_out, normed_ref, projected_out, gates_ref,
    mix_ref, small_ref, slab_ref,
    send, recv, local, store_mix, store_slab, store_small,
):
    sems = (send, recv, local)
    chunk = 1024
    half = chunk // 2
    items = []

    def add(source, first, width, ref, x_first):
        items.append(
            Gather(source.at[:, pl.ds(first, width)], columns_of(ref, first, width), x_first, sems, len(items))
        )
        return items[-1]

    ticks = []
    chunks = mix_in.shape[1] // chunk
    small = add(small_in, 0, small_in.shape[1], small_ref, True)
    for index in range(chunks):
        ticks.append([add(mix_in, index * chunk + part * half, half, mix_ref, part == 0) for part in range(2)])
    ticks.append([add(out_in, part * half, half, out_out, part == 0) for part in range(2)])
    ticks[0].insert(0, small)
    meet(peers())
    steps = (Gather.begin, Gather.second, Gather.third, Gather.fourth, Gather.finish)
    values = x_ref[...].astype(jnp.float32)
    scaled = values * lax.rsqrt(jnp.mean(values * values, axis=1, keepdims=True) + EPSILON)
    stores = []
    for tick in range(len(ticks) + len(steps) - 1):
        for step, action in reversed(list(enumerate(steps))):
            if 0 <= tick - step < len(ticks):
                for item in ticks[tick - step]:
                    action(item)
        done = tick - len(steps) + 1
        if done == 0:
            smalls = small_ref[...].reshape(-1, small_in.shape[1])
            gain = jnp.transpose(smalls.astype(jnp.float32))[24:25, :]
            normed_ref[...] = (scaled * gain).astype(jnp.bfloat16)
            gates_ref[...] = mm(normed_ref[...], smalls)
            stores.append(pltpu.make_async_copy(small_ref, small_out, store_small))
            stores[-1].start()
        if 0 <= done < chunks:
            here = pl.ds(done * chunk, chunk)
            keep = pltpu.make_async_copy(
                mix_ref.at[:, :, :, :, :, here], mix_out.at[:, :, :, :, :, here], store_mix.at[done]
            )
            keep.start()
            stores.append(keep)
            weights = mix_ref[:, :, :, :, :, done * chunk : (done + 1) * chunk].reshape(-1, chunk)
            slab = done % 2
            if done >= 2:
                slab_stores[done - 2].wait()
            else:
                slab_stores = [] if done == 0 else slab_stores
            slab_ref[slab] = mm(normed_ref[...], weights)
            slab_stores.append(
                pltpu.make_async_copy(slab_ref.at[slab], projected_out.at[:, here], store_slab.at[slab])
            )
            slab_stores[-1].start()
    for store in stores + slab_stores[-2:]:
        store.wait()


def gather_project_call(x, small, mix, out):
    length = x.shape[0]
    rows, width = mix.shape
    everywhere = pl.BlockSpec(memory_space=pl.ANY)
    held = pl.BlockSpec(memory_space=pltpu.VMEM)
    items = 3 + 2 * (width // 1024)
    full = STACK + (rows,)
    outs = pl.pallas_call(
        gather_project_kernel,
        out_shape=[
            jax.ShapeDtypeStruct(full + (width,), jnp.bfloat16),
            jax.ShapeDtypeStruct(full + (out.shape[1],), jnp.bfloat16),
            jax.ShapeDtypeStruct(full + (small.shape[1],), jnp.bfloat16),
            jax.ShapeDtypeStruct(x.shape, jnp.bfloat16),
            jax.ShapeDtypeStruct((length, width), jnp.float32),
            jax.ShapeDtypeStruct((length, small.shape[1]), jnp.float32),
        ],
        in_specs=[held, everywhere, everywhere, everywhere],
        out_specs=[everywhere, everywhere, everywhere, held, everywhere, held],
        scratch_shapes=[
            pltpu.VMEM(full + (width,), jnp.bfloat16),
            pltpu.VMEM(full + (small.shape[1],), jnp.bfloat16),
            pltpu.VMEM((2, length, 1024), jnp.float32),
            pltpu.SemaphoreType.DMA((items, STAGES)),
            pltpu.SemaphoreType.DMA((items, STAGES)),
            pltpu.SemaphoreType.DMA((items,)),
            pltpu.SemaphoreType.DMA((width // 1024,)),
            pltpu.SemaphoreType.DMA((2,)),
            pltpu.SemaphoreType.DMA,
        ],
        compiler_params=pltpu.CompilerParams(collective_id=1, has_side_effects=True, vmem_limit_bytes=LIMIT),
        cost_estimate=pl.CostEstimate(flops=2 * length * width * 1024, bytes_accessed=60_000_000, transcendentals=0),
    )(x, small, mix, out)
    return [part.reshape((-1,) + part.shape[5:]) if part.ndim == 6 else part for part in outs]


def from_behind(block, axis, distance):
    devices = range(lax.axis_size(axis))
    route = [(i - distance, i) for i in devices if i - distance in devices]
    return lax.ppermute(block, axis, route)


def rms_scale(values, scale_gain):
    return (
        values * lax.rsqrt(jnp.mean(values * values, axis=-1, keepdims=True) + EPSILON) * scale_gain
    )


def swiglu(gate_up):
    half_width = gate_up.shape[-1] // 2
    return jax.nn.silu(gate_up[:, :half_width]) * gate_up[:, half_width:]


def exchange(block, axis, bit):
    route = [(i, i ^ (1 << bit)) for i in range(lax.axis_size(axis))]
    return lax.ppermute(block, axis, route)


def axis_bits(axis):
    return lax.axis_size(axis).bit_length() - 1


def bit_orders():
    dp_bits = [("dp", bit) for bit in range(axis_bits("dp"))]
    seq_bits = [("seq", bit) for bit in range(axis_bits("seq"))]
    first, rest = dp_bits[:1], dp_bits[1:]
    inner = rest[:1] + seq_bits[:1]
    outer = rest[1:] + seq_bits[1:]
    return first + inner + outer, first + inner[::-1] + outer


def scatter_sum(part, order):
    dp_bits, seq_bits = axis_bits("dp"), axis_bits("seq")
    dims = [("dp", bit) for bit in reversed(range(dp_bits))] + [("seq", bit) for bit in reversed(range(seq_bits))]
    rows = part.shape[0] >> len(dims)
    part = part.reshape((2,) * len(dims) + (rows, part.shape[1]))
    for axis, bit in order:
        place = dims.index((axis, bit))
        dims.pop(place)
        mine = (lax.axis_index(axis) >> bit) & 1
        sent = lax.dynamic_index_in_dim(part, 1 - mine, place, keepdims=False)
        kept = lax.dynamic_index_in_dim(part, mine, place, keepdims=False)
        got = exchange(sent.astype(jnp.bfloat16), axis, bit)
        part = kept.astype(jnp.float32) + got.astype(jnp.float32)
    return part


def scatter_halves(part):
    half = part.shape[1] // 2
    orders = bit_orders()
    return jnp.concatenate(
        [scatter_sum(part[:, :half], orders[0]), scatter_sum(part[:, half:], orders[1])], axis=1
    )


def total_sum(block):
    for axis in ("dp", "seq"):
        for bit in range(axis_bits(axis)):
            block = block + exchange(block, axis, bit)
    return block


def gate_vectors(seg_now, seg_prev, gates_raw, decay_log):
    length = gates_raw.shape[0]
    chunks = length // GROUP
    beta = jax.nn.sigmoid(gates_raw[:, : NH * H]).reshape(chunks, GROUP, NH, H)
    rate = -jnp.exp(decay_log) * jax.nn.softplus(gates_raw[:, NH * H :])
    lower = jnp.tril(jnp.ones((GROUP, GROUP), jnp.float32))
    total = jnp.einsum("ts,csh->cth", lower, rate.reshape(chunks, GROUP, H), precision=HIGHEST)
    seg = seg_now.reshape(chunks, GROUP)
    before = jnp.concatenate([seg_prev.reshape(1), seg[:-1, -1]])
    scale = jnp.exp(total) * (seg == before[:, None]).astype(jnp.float32)[:, :, None]
    tail = jnp.exp(total[:, -1:, :] - total) * (seg == seg[:, -1:]).astype(jnp.float32)[:, :, None]

    def both(values):
        moved = jnp.moveaxis(values, 2, 0)
        return jnp.concatenate([moved, moved], axis=-1)

    beta_rows = beta.transpose(3, 0, 2, 1).reshape(H, chunks, SPAN)
    seg_rows = jnp.broadcast_to(jnp.concatenate([seg, seg], axis=1).astype(jnp.float32), (H, chunks, SPAN))
    none = jnp.zeros((H, chunks, SPAN), jnp.float32)
    return jnp.stack([both(total), beta_rows, seg_rows, both(scale), both(tail), none, none, none], axis=2)


def head_spec(shape):
    rank = len(shape)
    return pl.BlockSpec((1,) + shape, lambda head: (head,) + (0,) * rank)


def column_spec(rows, first):
    return pl.BlockSpec((rows, DK), lambda head: (0, first + head))


def whole_spec(shape):
    rank = len(shape)
    return pl.BlockSpec(shape, lambda head: (0,) * rank)


def per_head(shape, dtype=jnp.float32):
    return jax.ShapeDtypeStruct((H,) + shape, dtype)


def call(kernel, out_shape, in_specs, out_specs, scratch, flops, bytes_accessed):
    return pl.pallas_call(
        kernel,
        grid=(H,),
        out_shape=out_shape,
        in_specs=in_specs,
        out_specs=out_specs,
        scratch_shapes=scratch,
        compiler_params=pltpu.CompilerParams(
            dimension_semantics=("arbitrary",), vmem_limit_bytes=LIMIT
        ),
        cost_estimate=pl.CostEstimate(flops=flops, bytes_accessed=bytes_accessed, transcendentals=0),
    )


def conv_specs(length):
    return (
        [column_spec(length, H * part) for part in range(1 + 2 * NH)]
        + [column_spec(8, H * part) for part in range(1 + 2 * NH)] * 2
        + [whole_spec((3, length, DK))]
    )


def forward_call(projected, border, taps, masks, vec, start):
    length = projected.shape[0]
    chunks = length // GROUP
    square = (chunks, SPAN, DK)
    outs = [
        (square, jnp.bfloat16),
        (square, jnp.bfloat16),
        (square, jnp.float32),
        (square, jnp.bfloat16),
        (square, jnp.float32),
        ((chunks, GROUP, DK), jnp.bfloat16),
        ((chunks, GROUP, DV), jnp.float32),
        ((DV, DK), jnp.float32),
    ]
    parts = 1 + 2 * NH
    return call(
        forward_kernel,
        [per_head(*out) for out in outs],
        conv_specs(length) + [head_spec((chunks, 8, SPAN)), head_spec((DV, DK))],
        [head_spec(out[0]) for out in outs],
        [
            pltpu.VMEM((length + 8, DK), jnp.float32),
            pltpu.VMEM((length, DK), jnp.float32),
            pltpu.VMEM((NH, length, DK), jnp.float32),
            pltpu.VMEM((NH, length, DK), jnp.float32),
        ],
        H * chunks * 20 * 2 * SPAN**3 * 4,
        H * chunks * 8 * SPAN * DK * 4,
    )(*[projected] * parts, *[border] * parts, *[taps] * parts, masks, vec, start)


def chain_call(vec, transfer, start):
    chunks = transfer.shape[1]
    return call(
        chain_kernel,
        per_head((DV, DK)),
        [head_spec((chunks, 8, SPAN)), head_spec((chunks, SPAN, DK)), head_spec((DV, DK))],
        head_spec((DV, DK)),
        [],
        H * chunks * 2 * SPAN**3,
        H * chunks * SPAN * DK * 4,
    )(vec, transfer, start)


def readout_call(vec, key_part, value_part, transfer, inject, out_keys, out_values, entry, projected, gain):
    length = projected.shape[0]
    chunks = length // GROUP
    square = head_spec((chunks, SPAN, DK))
    half = head_spec((chunks, GROUP, DK))
    return call(
        readout_kernel,
        [
            jax.ShapeDtypeStruct((length, H * DV), jnp.bfloat16),
            jax.ShapeDtypeStruct((length, H * DV), jnp.float32),
            per_head((chunks, SPAN, DK), jnp.bfloat16),
            per_head((chunks, SPAN, DK), jnp.bfloat16),
        ],
        [
            head_spec((chunks, 8, SPAN)), square, square, square, square, half, half,
            head_spec((DV, DK)), column_spec(length, (1 + 2 * NH) * H), whole_spec((8, DV)),
        ],
        [column_spec(length, 0), column_spec(length, 0), square, square],
        [],
        H * chunks * 4 * 2 * SPAN**3 * 4,
        H * chunks * 8 * SPAN * DK * 4,
    )(vec, key_part, value_part, transfer, inject, out_keys, out_values, entry, projected, gain)


def readout_back_call(vec, transfer, out_keys, mixed, projected, gain, d_gated, start):
    length = projected.shape[0]
    chunks = length // GROUP
    square = head_spec((chunks, SPAN, DK))
    return call(
        readout_back_kernel,
        [
            jax.ShapeDtypeStruct((length, H * DV), jnp.bfloat16),
            jax.ShapeDtypeStruct((length, H * DV), jnp.bfloat16),
            per_head((chunks, SPAN, DK)),
            per_head((DV, DK)),
            per_head((8, DV)),
        ],
        [
            head_spec((chunks, 8, SPAN)), square, head_spec((chunks, GROUP, DK)),
            column_spec(length, 0), column_spec(length, (1 + 2 * NH) * H), whole_spec((8, DV)),
            column_spec(length, 0), head_spec((DV, DK)),
        ],
        [column_spec(length, 0), column_spec(length, 0), square, head_spec((DV, DK)), head_spec((8, DV))],
        [],
        H * chunks * 4 * 2 * SPAN**3 * 4,
        H * chunks * 8 * SPAN * DK * 4,
    )(vec, transfer, out_keys, mixed, projected, gain, d_gated, start)


def backward_call(projected, border, taps, masks, vec, transfer, inverse, solved, entries, d_mixed, local, exit_grad):
    length = projected.shape[0]
    chunks = length // GROUP
    parts = 1 + 2 * NH
    square = head_spec((chunks, SPAN, DK))
    outs = (
        [jax.ShapeDtypeStruct((length, H * DK), jnp.bfloat16)] * parts
        + [jax.ShapeDtypeStruct((16, H * DK), jnp.float32)] * parts
        + [jax.ShapeDtypeStruct((8, H * DK), jnp.float32)] * parts
        + [per_head((chunks, 8, SPAN))]
    )
    out_specs = (
        [column_spec(length, 0)] * parts
        + [column_spec(16, 0)] * parts
        + [column_spec(8, 0)] * parts
        + [head_spec((chunks, 8, SPAN))]
    )
    tall = pltpu.VMEM((parts, length, DK), jnp.float32)
    return call(
        backward_kernel,
        outs,
        conv_specs(length)
        + [head_spec((chunks, 8, SPAN)), square, square, square, square, column_spec(length, 0), square, head_spec((DV, DK))],
        out_specs,
        [
            pltpu.VMEM((parts, length + 8, DK), jnp.float32),
            tall,
            pltpu.VMEM((length, DK), jnp.float32),
            pltpu.VMEM((NH, length, DK), jnp.float32),
            pltpu.VMEM((NH, length, DK), jnp.float32),
            pltpu.VMEM((1 + NH, length, DK), jnp.float32),
            tall,
            pltpu.VMEM((length + 16, DK), jnp.float32),
        ],
        H * chunks * 14 * 2 * SPAN**3 * 4,
        H * chunks * 16 * SPAN * DK * 4,
    )(*[projected] * parts, *[border] * parts, *[taps] * parts, masks, vec, transfer, inverse, solved, entries, d_mixed, local, exit_grad)


def gather(block, dim=0):
    return lax.all_gather(block, ("dp", "seq"), axis=dim, tiled=True)


def on_device(
    block_input, doc_starts, norm_in, w_mix, w_small, conv_w, decay_log, norm_out,
    w_out, norm_mlp, w_gu, w_down, cotangent,
):
    row_count, seg_len, width = block_input.shape
    tap_count = conv_w.shape[0]
    key_width = H * DK
    parts = 1 + 2 * NH
    seqs = lax.axis_size("seq")
    residual_in = block_input.astype(jnp.float32).reshape(seg_len, width)
    smalls, rows = w_small.shape[1], w_mix.shape[0]
    fast = lax.axis_size("dp") == 4 * ZS and seqs == 2 and rows % 16 == 0
    if fast:
        small = jnp.concatenate(
            [w_small, norm_in[:, None], norm_mlp[:, None], conv_w.reshape(tap_count, rows, -1).transpose(1, 2, 0).reshape(rows, -1)], axis=1
        )
        small = jnp.concatenate([small, jnp.zeros((rows, DK - small.shape[1]), small.dtype)], axis=1)
        mix_all, out_all, small_pack, normed_low, projected, gates_raw = gather_project_call(
            block_input.reshape(seg_len, width), small, w_mix, w_out
        )
        small_all = small_pack[:, :smalls]
        gates_raw = gates_raw[:, :smalls]
        norm_in_all = small_pack[:, smalls].astype(jnp.float32)
        norm_mlp_all = small_pack[:, smalls + 1].astype(jnp.float32)
        per_row = conv_w.shape[1] // rows
        conv_all = small_pack[:, smalls + 2 : smalls + 2 + per_row * tap_count]
        conv_all = conv_all.reshape(-1, tap_count).transpose(1, 0)
        normed, norm_in_back = jax.vjp(rms_scale, residual_in, norm_in_all)
    else:
        mix_all, small_all, conv_all, out_all = gather(w_mix), gather(w_small), gather(conv_w, 1), gather(w_out)
        norm_in_all = gather(norm_in).astype(jnp.float32)
        norm_mlp_all = gather(norm_mlp).astype(jnp.float32)
        normed, norm_in_back = jax.vjp(rms_scale, residual_in, norm_in_all)
        normed_low = normed.astype(jnp.bfloat16)
        projected = jnp.dot(normed_low, mix_all, preferred_element_type=jnp.float32)
        gates_raw = jnp.dot(normed_low, small_all, preferred_element_type=jnp.float32)
    gu_all, down_all = gather(w_gu), gather(w_down)
    border = from_behind(projected[seg_len - tap_count + 1 :, : parts * key_width], "seq", 1)
    border = jnp.concatenate([jnp.zeros((9 - tap_count, parts * key_width), jnp.float32), border], axis=0)
    positions = lax.axis_index("seq") * seg_len + jnp.arange(1 - tap_count, seg_len, dtype=jnp.int32)
    seg_ext = jnp.sum((positions[:, None] >= doc_starts[0][None, :]).astype(jnp.int32), axis=1)
    seg_ext = jnp.where(positions < 0, -1, seg_ext)
    seg_now = seg_ext[tap_count - 1 :]
    masks = jnp.stack(
        [seg_ext[tap_count - 1 - tap : tap_count - 1 - tap + seg_len] == seg_now for tap in range(1, tap_count)]
    ).astype(jnp.float32)
    masks = jnp.broadcast_to(masks[:, :, None], (tap_count - 1, seg_len, DK))
    taps = jnp.concatenate([conv_all.astype(jnp.float32), jnp.zeros((8 - tap_count, parts * key_width), jnp.float32)], axis=0)
    vec, vec_back = jax.vjp(
        partial(gate_vectors, seg_now, seg_ext[tap_count - 2]), gates_raw, decay_log.astype(jnp.float32)
    )
    zero_state = jnp.zeros((H, DV, DK), jnp.float32)
    inverse, key_part, value_part, transfer, inject, out_keys, out_values, final_state = forward_call(
        projected, border, taps, masks, vec, zero_state
    )
    entry = zero_state
    device_transfer = None
    if seqs > 2:
        eye = jnp.broadcast_to(jnp.eye(DK, dtype=jnp.float32), (H, DK, DK))
        device_transfer = chain_call(vec, transfer, eye)
    for turn in range(seqs - 1):
        leaving = final_state
        if turn > 0:
            leaving = leaving + jnp.einsum("hvk,hkl->hvl", entry, device_transfer, precision=HIGHEST)
        entry = from_behind(leaving.astype(jnp.bfloat16), "seq", 1).astype(jnp.float32)
    gain = jnp.broadcast_to(norm_out.astype(jnp.float32)[None, :], (8, DV))
    normed_out_low, mixed, solved, entries = readout_call(
        vec, key_part, value_part, transfer, inject, out_keys, out_values, entry, projected, gain
    )
    hidden = residual_in + jnp.dot(normed_out_low, out_all, preferred_element_type=jnp.float32)
    mlp_in, norm_mlp_back = jax.vjp(rms_scale, hidden, norm_mlp_all)
    mlp_in_low = mlp_in.astype(jnp.bfloat16)
    gate_up = jnp.dot(mlp_in_low, gu_all, preferred_element_type=jnp.float32)
    activated, act_back = jax.vjp(swiglu, gate_up)
    activated_low = activated.astype(jnp.bfloat16)
    result = hidden + jnp.dot(activated_low, down_all, preferred_element_type=jnp.float32)
    block_output = result.astype(jnp.bfloat16).reshape(block_input.shape)

    d_result_low = cotangent.reshape(seg_len, width)
    d_result = d_result_low.astype(jnp.float32)
    grad_down = jnp.einsum("nf,nd->fd", activated_low, d_result_low, preferred_element_type=jnp.float32)
    d_activated = jnp.einsum("nd,fd->nf", d_result_low, down_all, preferred_element_type=jnp.float32)
    (d_gate_up,) = act_back(d_activated)
    d_gate_low = d_gate_up.astype(jnp.bfloat16)
    grad_gu = jnp.einsum("nd,nf->df", mlp_in_low, d_gate_low, preferred_element_type=jnp.float32)
    d_mlp_in = jnp.einsum("nf,df->nd", d_gate_low, gu_all, preferred_element_type=jnp.float32)
    d_hidden_norm, grad_norm_mlp = norm_mlp_back(d_mlp_in)
    d_hidden = d_result + d_hidden_norm
    grad_gu = scatter_halves(grad_gu.astype(jnp.bfloat16))
    grad_down = scatter_halves(grad_down.astype(jnp.bfloat16))

    d_mixer_low = d_hidden.astype(jnp.bfloat16)
    grad_out = jnp.einsum("nh,nd->hd", normed_out_low, d_mixer_low, preferred_element_type=jnp.float32)
    grad_out = scatter_halves(grad_out.astype(jnp.bfloat16))
    d_normed_out = jnp.einsum("nd,hd->nh", d_mixer_low, out_all, preferred_element_type=jnp.float32)
    d_mixed, d_out_gate, local, own_entry, gain_parts = readout_back_call(
        vec, transfer, out_keys, mixed, projected, gain, d_normed_out, zero_state
    )
    grad_norm_out = jnp.sum(gain_parts[:, 0, :], axis=0)
    exit_grad = zero_state
    for turn in range(seqs - 1):
        leaving = own_entry
        if turn > 0:
            leaving = leaving + jnp.einsum("hvl,hkl->hvk", exit_grad, device_transfer, precision=HIGHEST)
        exit_grad = from_behind(leaving.astype(jnp.bfloat16), "seq", -1).astype(jnp.float32)
    backs = backward_call(
        projected, border, taps, masks, vec, transfer, inverse, solved, entries, d_mixed, local, exit_grad
    )
    d_columns, edges, tap_grads, d_vec = backs[:parts], backs[parts : 2 * parts], backs[2 * parts : 3 * parts], backs[-1]
    edge = jnp.concatenate(edges, axis=1)
    returned = from_behind(edge[9 - tap_count : 8].astype(jnp.bfloat16), "seq", -1).astype(jnp.float32)
    fixed = (edge[17 - tap_count :] + returned).astype(jnp.bfloat16)
    d_projected = jnp.concatenate(list(d_columns) + [d_out_gate], axis=1)
    d_projected = lax.dynamic_update_slice(d_projected, fixed, (seg_len - tap_count + 1, 0))
    d_gates_raw, grad_decay = vec_back(d_vec)
    d_gates_low = d_gates_raw.astype(jnp.bfloat16)
    grad_mix = jnp.einsum("nd,nc->dc", normed_low, d_projected, preferred_element_type=jnp.float32)
    grad_mix = scatter_halves(grad_mix.astype(jnp.bfloat16))
    grad_small = jnp.einsum("nd,nc->dc", normed_low, d_gates_low, preferred_element_type=jnp.float32)
    d_normed = jnp.einsum("nc,dc->nd", d_projected, mix_all, preferred_element_type=jnp.float32)
    d_normed = d_normed + jnp.einsum("nc,dc->nd", d_gates_low, small_all, preferred_element_type=jnp.float32)
    d_input_norm, grad_norm_in = norm_in_back(d_normed)
    input_grad = (d_hidden + d_input_norm).astype(jnp.bfloat16).reshape(block_input.shape)

    grad_conv = jnp.concatenate(tap_grads, axis=1)[:tap_count]
    devices = lax.axis_size("dp") * seqs
    conv_rows = grad_conv.reshape(tap_count, devices, -1).transpose(1, 0, 2).reshape(width, -1)
    packed = jnp.concatenate([grad_small, grad_norm_in[:, None], grad_norm_mlp[:, None], conv_rows], axis=1)
    packed = jnp.concatenate([packed, jnp.zeros((width, 128 - packed.shape[1]), jnp.float32)], axis=1)
    packed = scatter_sum(packed, bit_orders()[0])
    smalls = grad_small.shape[1]
    grad_small = packed[:, :smalls]
    grad_norm_in, grad_norm_mlp = packed[:, smalls], packed[:, smalls + 1]
    grad_conv = packed[:, smalls + 2 : smalls + 2 + conv_rows.shape[1]].reshape(tap_count, -1)
    sums = total_sum(jnp.concatenate([grad_norm_out, grad_decay]))
    grad_norm_out, grad_decay = sums[:DV], sums[DV:]
    return (
        block_output, input_grad, grad_norm_in, grad_mix, grad_small, grad_conv, grad_decay,
        grad_norm_out, grad_out, grad_norm_mlp, grad_gu, grad_down,
    )


def solution(mesh):
    sharded = ("dp", "seq")
    in_specs = (
        P("dp", "seq", None), P("dp", None), P(sharded), P(sharded, None), P(sharded, None),
        P(None, sharded), P(), P(), P(sharded, None), P(sharded), P(sharded, None),
        P(sharded, None), P("dp", "seq", None),
    )
    out_specs = (
        P("dp", "seq", None), P("dp", "seq", None), P(sharded), P(sharded, None), P(sharded, None),
        P(None, sharded), P(), P(), P(sharded, None), P(sharded), P(sharded, None), P(sharded, None),
    )
    return jax.shard_map(
        on_device, mesh=mesh, in_specs=in_specs, out_specs=out_specs, check_vma=False
    )
```

time: 3000 us -> 789 us (0.26)
  waiting for transfers between devices: 1260 us -> 190 us
  other arithmetic: 803 us -> 43.8 us
  matrix products: 493 us -> 96.7 us
  Pallas kernels: 0 us -> 267 us
  blocking collectives: 213 us -> 0 us
  local copies, waits for them, and re-layouts: 187 us -> 96.4 us
  starting transfers between devices: 13.2 us -> 72.1 us
    reduce_scatter x4 -> x0, waiting for transfers between devices: 1130 us -> none  [the longest x1 490 us: on_device(): lax.psum_scatter(grad_gu, ('dp', 'seq'), scatter_dimension=0, tiled=True)]
    another operation x11 -> x0, other arithmetic: 669 us -> none  [the longest x5 635 us: block_terms(): jax.scipy.linalg.solve_triangular(lower_part, right_side, lower=True, uni...]
    dot_general x79 -> x7, matrix products: 385 us -> 43.9 us  [the longest x1 14 us: on_device(): jnp.einsum('nf,df->nd', d_gate_low, gu_all, preferred_element_type=jnp.fl...]
    pallas_call x0 -> x5, Pallas kernels: none -> 267 us  [the longest x1 115 us: gather_project_call(): pl.pallas_call(gather_project_kernel, out_shape=[jax.ShapeDtypeStruct(ful...]
    ppermute x0 -> x50, waiting for transfers between devices: none -> 184 us  [exchange(): return lax.ppermute(block, axis, route)]
    all_gather x2 -> x0, blocking collectives: 133 us -> none  [the longest x1 68.9 us: on_device(): lax.all_gather(w_small, ('dp', 'seq'), axis=0, tiled=True)]
    unnamed x12 -> x2, waiting for transfers between devices: 119 us -> 1.38 us
    unnamed x2 -> x0, blocking collectives: 80.2 us -> none
  transfers between devices with their start and end apart: 14 -> 56, of which waited for: 7 -> 34; matrix products, arithmetic and copies ran while one was open for 36% -> 22% of each run, Pallas kernels for 0% -> 32%
where the time goes in v1:
time: 789 us; the launch traced here: 782 us
  Pallas kernels  267 us (34%)
  waiting for transfers between devices  190 us (24%)
  matrix products  96.7 us (12%)
  local copies, waits for them, and re-layouts  96.4 us (12%)
  starting transfers between devices  72.1 us (9%)
  other arithmetic  43.8 us (6%)
  between operations  16.1 us (2%)
    ppermute x50, waiting for transfers between devices, exchange(): return lax.ppermute(block, axis, route)  184 us
    pallas_call x1, Pallas kernels, gather_project_call(): pl.pallas_call(gather_project_kernel, out_shape=[jax.ShapeDtypeStruct(ful...  115 us
    pallas_call x1, Pallas kernels, backward_call(): call(backward_kernel, outs, conv_specs(length) + [head_spec((chunks, 8, S...  78.4 us
    ppermute x50, starting transfers between devices, exchange(): return lax.ppermute(block, axis, route)  63.1 us
    pallas_call x1, Pallas kernels, forward_call(): call(forward_kernel, [per_head(*out) for out in outs], conv_specs(length)...  45.1 us
    add x45, other arithmetic, scatter_sum(): part = kept.astype(jnp.float32) + got.astype(jnp.float32)  26.2 us
    unnamed x187, local copies, waits for them, and re-layouts  22.9 us
    slice x4, local copies, waits for them, and re-layouts, scatter_halves(): part[:, :half]  17.2 us
  transfers between devices with their start and end apart: 56, of which 34 were waited for; matrix products, arithmetic and copies ran while one was open for 22% of the time, Pallas kernels for 32%

profile of v1, /device:TPU:0, one launch (start us, length us, event | category | flops | bytes accessed | tf_op | source)
XLA Modules:
  0.0 782.1 jit_solution(10381587356949497121)
XLA Ops:
  15.1 115.2 %shard_map.220 = (bf16[4,2,2,2,32,6144]{5,4,3,2,1,0:T(8,128)(2,1)}, bf16[4,2,2,2,32,1024]{5,4,3,2,1,0:T(8,128)(2,1)}, bf16[4,2,2,2,32,128]{5,4,3,2,1,0:T(8,128)(...) custom-call(bf16[512,1024]{1,0:T(8,128)(2,1)S(1)} %bitcast.360, ...), custom_call_target="tpu_custom_call" | custom-call | flops 6442450944 | bytes 60000000 | tf_op jit(solution)/shard_map/pallas_call | solution.py:502
  132.4 4.1 collective-permute-start
  144.9 45.1 %shard_map.221 = (bf16[8,8,128,128]{3,2,1,0:T(8,128)(2,1)}, bf16[8,8,128,128]{3,2,1,0:T(8,128)(2,1)}, f32[8,8,128,128]{3,2,1,0:T(8,128)}, bf16[8,8,128,128]{3,2,...) custom-call(f32[512,6144]{1,0:T(8,128)} %get-tuple-element.52.q_in.k, ...), custom_call_target="tpu_custom_call" | custom-call | flops 21474836480 | bytes 33554432 | tf_op jit(solution)/shard_map/pallas_call | solution.py:675
  197.0 4.3 collective-permute-done.1
  202.3 14.7 %shard_map.222 = (bf16[512,1024]{1,0:T(8,128)(2,1)S(1)}, f32[512,1024]{1,0:T(8,128)}, bf16[8,8,128,128]{3,2,1,0:T(8,128)(2,1)}, bf16[8,8,128,128]{3,2,1,0:T(8,128)(2,1)}) custom-call(f32[8,8,8,128]{3,2,1,0:T(8,128)S(1)} %stack.31.vec_ref, bf16[8,8,128,128]{3,2,1,0:T(8,128)(2,1)} %get-tuple-element.54.w_in, f32[8,8,128,128]{3,2,1,0:T(8,128)} %get-tuple-element.55.u_in, ...), custom_call_target="tpu_custom_call" | custom-call | flops 4294967296 | bytes 33554432 | tf_op jit(solution)/shard_map/pallas_call | solution.py:709
  219.6 12.3 %fusion.100 = f32[512,5632]{1,0:T(8,128)} fusion(bf16[1024,5632]{1,0:T(8,128)(2,1)} %all-gather.3.cloned.1.call-done, f32[512,1024]{1,0:T(8,128)} %get-tuple-element.188, f32[1024]{0:T(1024)S(1)} %bitcast.377, f32[512]{0:T(512)S(1)} %fusion.89), kind=kOutput, calls=%fused_computation.310 | convolution fusion | flops 5907152896 | bytes 25171968 | tf_op jit(solution)/shard_map/dot_general | solution.py:868
  231.9 12.7 %fusion.26 = (f32[512,2816]{1,0:T(8,128)}, f32[512,2816]{1,0:T(8,128)}, bf16[512,2816]{1,0:T(8,128)(2,1)}) fusion(f32[512,5632]{1,0:T(8,128)} %fusion.100, bf16[2816,1024]{1,0:T(8,128)(2,1)} %all-gather.5.cloned.1.call-done, bf16[1,512,1024]{2,1,0:T(8,128)(2,1)S(1)} %copy-done.57), kind=kOutput, calls=%fused_computation.105 | convolution fusion | flops 2972975104 | bytes 32768000 | tf_op jit(solution)/shard_map/nd,fd->nf/dot_general | solution.py:877
  244.6 14.0 %multiply_reduce_fusion = (f32[1024]{0:T(1024)S(1)}, f32[512]{0:T(512)S(1)}, f32[512,1024]{1,0:T(8,128)}) fusion(f32[512,1024]{1,0:T(8,128)} %get-tuple-element.188, f32[512]{0:T(512)S(1)} %fusion.89, f32[1024]{0:T(1024)S(1)} %bitcast.378, bf16[1024,5632]{1,0:T(8,128)(2,1)} %all-gather.3.cloned.1.call-done, f32[512,2816]{1,0:T(8,128)} %get-tuple-element.145, ...), kind=kOutput, calls=%fused_computation.46 | convolution fusion | flops 5914491392 | bytes 27275264 | tf_op jit(solution)/shard_map/nf,df->nd/dot_general | solution.py:881
  258.6 2.9 fusion.3
  261.5 2.7 fusion.28.d_ref
  266.8 13.6 %convolution_convert_fusion = bf16[1024,5632]{1,0:T(8,128)(2,1)} fusion(f32[512,2816]{1,0:T(8,128)} %get-tuple-element.145, f32[512,2816]{1,0:T(8,128)} %get-tuple-element.144, f32[512,1024]{1,0:T(8,128)S(1)} %copy-done.42, f32[1024]{0:T(1024)S(1)} %bitcast.380, f32[512]{0:T(512)S(1)} %fusion.89), kind=kOutput, calls=%fused_computation.1 | convolution fusion | flops 5918687232 | bytes 25171968 | tf_op jit(solution)/shard_map/nd,nf->df/dot_general | solution.py:880
  280.4 14.0 %shard_map.223 = (bf16[512,1024]{1,0:T(8,128)(2,1)S(1)}, bf16[512,1024]{1,0:T(8,128)(2,1)S(1)}, f32[8,8,128,128]{3,2,1,0:T(8,128)}, f32[8,128,128]{2,1,0:T(8,128)S(1)}, f32[8,8,128]{2,1,0:T(8,128)S(1)}) custom-call(f32[8,8,8,128]{3,2,1,0:T(8,128)S(1)} %stack.31.vec_ref, bf16[8,8,128,128]{3,2,1,0:T(8,128)(2,1)} %get-tuple-element.56.t_in, ...), custom_call_target="tpu_custom_call" | custom-call | flops 4294967296 | bytes 33554432 | tf_op jit(solution)/shard_map/pallas_call | solution.py:732
  304.5 9.2 %fusion.102 = (bf16[1024,2816]{1,0:T(8,128)(2,1)}, bf16[1024,2816]{1,0:T(8,128)(2,1)}) fusion(bf16[1024,5632]{1,0:T(8,128)(2,1)} %convolution_convert_fusion), kind=kLoop, calls=%fused_computation.312 | loop fusion | bytes 23068672 | tf_op jit(solution)/shard_map/slice | solution.py:586
  313.8 4.9 constant_dynamic-slice_fusion.5
  325.7 3.8 convolution_convert_fusion.2
  333.7 4.1 fusion.14
  340.4 78.4 %shard_map.224 = (bf16[512,1024]{1,0:T(8,128)(2,1)S(1)}, bf16[512,1024]{1,0:T(8,128)(2,1)}, bf16[512,1024]{1,0:T(8,128)(2,1)}, bf16[512,1024]{1,0:T(8,128)(2,1)}...) custom-call(f32[512,6144]{1,0:T(8,128)} %get-tuple-element.52.q_in.k, ...), custom_call_target="tpu_custom_call" | custom-call | flops 15032385536 | bytes 67108864 | tf_op jit(solution)/shard_map/pallas_call | solution.py:771
  442.7 3.3 collective-permute-start.22
  455.7 12.6 %convolution_convert_fusion.1 = bf16[1024,6144]{1,0:T(8,128)(2,1)} fusion(bf16[512,1024]{1,0:T(8,128)(2,1)S(1)} %copy-done.15, bf16[512,6144]{1,0:T(8,128)(2,1)} %dynamic_update_slice.3), kind=kOutput, calls=%fused_computation.2 | convolution fusion | flops 6448742400 | bytes 19922944 | tf_op jit(solution)/shard_map/nd,nc->dc/dot_general | solution.py:912
  468.2 12.0 %fusion.9 = (f32[1024]{0:T(1024)S(1)}, f32[512]{0:T(512)S(1)}, f32[512,1024]{1,0:T(8,128)S(1)}) fusion(f32[512]{0:T(512)S(1)} %copy-done.72, bf16[1,512,1024]{2,1,0:T(8,128)(2,1)S(1)} %copy-done.6, f32[1024]{0:T(1024)S(1)} %bitcast.394, f32[512,1024]{1,0:T(8,128)S(1)} %copy-done.49, bf16[512,6144]{1,0:T(8,128)(2,1)} %dynamic_update_slice.3, ...), kind=kOutput, calls=%fused_computation.45 | convolution fusion | flops 6446643712 | bytes 24129536 | tf_op jit(solution)/shard_map/nc,dc->nd/dot_general | solution.py:915
  482.3 2.7 concatenate.82
  486.5 5.9 fusion.101
  498.6 2.9 collective-permute-done.5
  515.1 3.0 collective-permute-start.8
  523.2 3.9 collective-permute-done.30
  529.3 4.9 collective-permute-done.25
  535.4 3.7 collective-permute-done.31
  539.4 4.8 collective-permute-done.26
  552.7 3.0 collective-permute-start.33
  557.6 3.0 collective-permute-start.28
  566.9 14.1 %collective-permute-done.50 = bf16[2,2,2,88,512]{4,3,0,1,2:T(8,128)(2,1)S(1)} collective-permute-done((bf16[2,2,2,88,512]{4,3,0,1,2:T(8,128)(2,1)S(1)}, bf16[2,2,2,88,512]{4,3,0,1,2:T(8,128)(2,1)S(1)}, u32[]{:S(2)}, u32[]{:S(2)}) %collective-permute-start.50) | collective-permute-done | bytes 720928 | tf_op jit(solution)/shard_map/ppermute | solution.py:550
  584.7 8.1 %collective-permute-done.51 = bf16[2,2,88,512]{3,2,0,1:T(8,128)(2,1)S(1)} collective-permute-done((bf16[2,2,88,512]{3,2,0,1:T(8,128)(2,1)S(1)}, bf16[2,2,88,512]{3,2,0,1:T(8,128)(2,1)S(1)}, u32[]{:S(2)}, u32[]{:S(2)}) %collective-permute-start.51) | collective-permute-done | bytes 360480 | tf_op jit(solution)/shard_map/ppermute | solution.py:550
  594.5 6.9 collective-permute-done.46
  603.6 4.2 collective-permute-done.52
  610.2 4.4 collective-permute-done.47
  614.7 6.3 collective-permute-done.53
  621.0 6.0 collective-permute-done.48
  633.2 2.7 convert_add_fusion.3
  640.0 3.0 convert_add_fusion
  644.9 3.0 convert_add_fusion.1
  649.1 17.3 %collective-permute-done.40 = bf16[2,2,2,32,2816]{4,3,0,1,2:T(8,128)(2,1)} collective-permute-done((bf16[2,2,2,32,2816]{4,3,0,1,2:T(8,128)(2,1)}, bf16[2,2,2,32,2816]{4,3,0,1,2:T(8,128)(2,1)}, u32[]{:S(2)}, u32[]{:S(2)}) %collective-permute-start.40) | collective-permute-done | bytes 1441824 | tf_op jit(solution)/shard_map/ppermute | solution.py:550
  675.1 25.0 %collective-permute-done.15 = bf16[2,2,2,32,3072]{4,3,0,1,2:T(8,128)(2,1)} collective-permute-done((bf16[2,2,2,32,3072]{4,3,0,1,2:T(8,128)(2,1)S(1)}, bf16[2,2,2,32,3072]{4,3,0,1,2:T(8,128)(2,1)}, u32[]{:S(2)}, u32[]{:S(2)}) %collective-permute-start.15) | collective-permute-done | bytes 1572896 | tf_op jit(solution)/shard_map/ppermute | solution.py:550
  707.2 11.2 %collective-permute-done.41 = bf16[2,2,32,2816]{3,2,0,1:T(8,128)(2,1)S(1)} collective-permute-done((bf16[2,2,32,2816]{3,2,0,1:T(8,128)(2,1)S(1)}, bf16[2,2,32,2816]{3,2,0,1:T(8,128)(2,1)S(1)}, u32[]{:S(2)}, u32[]{:S(2)}) %collective-permute-start.41) | collective-permute-done | bytes 720928 | tf_op jit(solution)/shard_map/ppermute | solution.py:550
  721.0 8.4 %collective-permute-done.42 = bf16[2,32,2816]{2,1,0:T(8,128)(2,1)S(1)} collective-permute-done((bf16[2,32,2816]{2,1,0:T(8,128)(2,1)S(1)}, bf16[2,32,2816]{2,1,0:T(8,128)(2,1)S(1)}, u32[]{:S(2)}, u32[]{:S(2)}) %collective-permute-start.42) | collective-permute-done | bytes 360480 | tf_op jit(solution)/shard_map/ppermute | solution.py:550
  731.0 9.4 %collective-permute-done.37 = bf16[2,32,2816]{2,1,0:T(8,128)(2,1)S(1)} collective-permute-done((bf16[2,32,2816]{2,1,0:T(8,128)(2,1)S(1)}, bf16[2,32,2816]{2,1,0:T(8,128)(2,1)S(1)}, u32[]{:S(2)}, u32[]{:S(2)}) %collective-permute-start.37) | collective-permute-done | bytes 360480 | tf_op jit(solution)/shard_map/ppermute | solution.py:550
  742.6 9.4 %collective-permute-done.38 = bf16[32,2816]{1,0:T(8,128)(2,1)S(1)} collective-permute-done((bf16[32,2816]{1,0:T(8,128)(2,1)S(1)}, bf16[32,2816]{1,0:T(8,128)(2,1)S(1)}, u32[]{:S(2)}, u32[]{:S(2)}) %collective-permute-start.38) | collective-permute-done | bytes 180256 | tf_op jit(solution)/shard_map/ppermute | solution.py:550
  755.6 5.4 collective-permute-done.17
  769.9 4.2 collective-permute-done.13
  (484 shorter events, 195.4 us)
Async XLA Ops:
  7.2 212.4 %all-gather.3.cloned.1.call-start = ((), (), s32[]{:S(2)}) async-start(), calls=%async_computation | async-start | bytes 11894784 | tf_op jit(solution)/shard_map/all_gather | solution.py:793
  7.9 224.0 %all-gather.5.cloned.1.call-start = ((), (), s32[]{:S(2)}) async-start(), calls=%async_computation.1 | async-start | bytes 5947392 | tf_op jit(solution)/shard_map/all_gather | solution.py:793
  132.4 12.1 %collective-permute-start = (f32[3,5120]{1,0:T(4,128)S(1)}, f32[3,5120]{1,0:T(4,128)S(1)}, u32[]{:S(2)}, u32[]{:S(2)}) collective-permute-start(f32[3,5120]{1,0:T(4,128)S(1)} %slice.119), channel_id=1, source_target_pairs={{0,1},{2,3},{4,5},{6,7},{8,9},{10,11},{12,13},{14,15},{16,17},{18,... | collective-permute-start | bytes 184328 | tf_op jit(solution)/shard_map/ppermute | solution.py:534
  190.8 10.4 %collective-permute-start.1 = (bf16[8,128,128]{2,1,0:T(8,128)(2,1)}, bf16[8,128,128]{2,1,0:T(8,128)(2,1)}, u32[]{:S(2)}, u32[]{:S(2)}) collective-permute-start(bf16[8,128,128]{2,1,0:T(8,128)(2,1)} %convert_element_type.529), channel_id=1, source_target_pairs={{0,1},{2,3},{4,5},{6,7},{8,9},{10,11},{12,13},{14,15},{16,17},{18,... | collective-permute-start | bytes 786440 | tf_op jit(solution)/shard_map/ppermute | solution.py:534
  296.5 43.9 %collective-permute-start.2 = (bf16[8,128,128]{2,1,0:T(8,128)(2,1)S(1)}, bf16[8,128,128]{2,1,0:T(8,128)(2,1)S(1)}, u32[]{:S(2)}, u32[]{:S(2)}) collective-permute-start(bf16[8,128,128]{2,1,0:T(8,128)(2,1)S(1)} %convert_element_type.540), channel_id=1, source_target_pairs={{1,0},{3,2},{5,4},{7,6},{9,8},{11,10},{13,12},{15,14},{17,16},{19,... | collective-permute-start | bytes 786440 | tf_op jit(solution)/shard_map/ppermute | solution.py:534
  302.3 206.9 %collective-permute-start.29 = (bf16[2,2,2,2,32,512]{5,4,0,1,2,3:T(8,128)(2,1)}, bf16[2,2,2,2,32,512]{5,4,0,1,2,3:T(8,128)(2,1)}, u32[]{:S(2)}, u32[]{:S(2)}) collective-permute-start(bf16[2,2,2,2,32,512]{5,4,0,1,2,3:T(8,128)(2,1)} %bitcast.351), channel_id=1, source_target_pairs={{0,2},{2,0},{4,6},{6,4},{8,10},{10,8},{12,14},{14,12},{16,18},{18,... | collective-permute-start | bytes 1572872 | tf_op jit(solution)/shard_map/ppermute | solution.py:550
  304.0 207.0 %collective-permute-start.24 = (bf16[2,2,2,2,32,512]{5,4,0,1,3,2:T(8,128)(2,1)}, bf16[2,2,2,2,32,512]{5,4,0,1,3,2:T(8,128)(2,1)}, u32[]{:S(2)}, u32[]{:S(2)}) collective-permute-start(bf16[2,2,2,2,32,512]{5,4,0,1,3,2:T(8,128)(2,1)} %bitcast.352), channel_id=1, source_target_pairs={{0,2},{2,0},{4,6},{6,4},{8,10},{10,8},{12,14},{14,12},{16,18},{18,... | collective-permute-start | bytes 1572872 | tf_op jit(solution)/shard_map/ppermute | solution.py:550
  320.4 307.4 %collective-permute-start.39 = (bf16[2,2,2,2,32,2816]{5,4,0,1,2,3:T(8,128)(2,1)}, bf16[2,2,2,2,32,2816]{5,4,0,1,2,3:T(8,128)(2,1)}, u32[]{:S(2)}, u32[]{:S(2)}) collective-permute-start(bf16[2,2,2,2,32,2816]{5,4,0,1,2,3:T(8,128)(2,1)} %bitcast.347), channel_id=1, source_target_pairs={{0,2},{2,0},{4,6},{6,4},{8,10},{10,8},{12,14},{14,12},{16,18},{18,... | collective-permute-start | bytes 8650760 | tf_op jit(solution)/shard_map/ppermute | solution.py:550
  430.5 22.3 %collective-permute-start.3 = (bf16[3,5120]{1,0:T(4,128)(2,1)S(1)}, bf16[3,5120]{1,0:T(4,128)(2,1)S(1)}, u32[]{:S(2)}, u32[]{:S(2)}) collective-permute-start(bf16[3,5120]{1,0:T(4,128)(2,1)S(1)} %slice.207), channel_id=1, source_target_pairs={{1,0},{3,2},{5,4},{7,6},{9,8},{11,10},{13,12},{15,14},{17,16},{19,... | collective-permute-start | bytes 92168 | tf_op jit(solution)/shard_map/ppermute | solution.py:534
  442.7 4.8 collective-permute-start.22
  451.7 181.4 %collective-permute-start.34 = (bf16[2,2,2,2,32,2816]{5,4,0,1,3,2:T(8,128)(2,1)}, bf16[2,2,2,2,32,2816]{5,4,0,1,3,2:T(8,128)(2,1)}, u32[]{:S(2)}, u32[]{:S(2)}) collective-permute-start(bf16[2,2,2,2,32,2816]{5,4,0,1,3,2:T(8,128)(2,1)} %bitcast.373), channel_id=1, source_target_pairs={{0,2},{2,0},{4,6},{6,4},{8,10},{10,8},{12,14},{14,12},{16,18},{18,... | collective-permute-start | bytes 8650760 | tf_op jit(solution)/shard_map/ppermute | solution.py:550
  486.0 11.1 %collective-permute-start.4 = (bf16[2,2,2,2,32,128]{5,4,3,2,1,0:T(8,128)(2,1)S(1)}, bf16[2,2,2,2,32,128]{5,4,3,2,1,0:T(8,128)(2,1)S(1)}, u32[]{:S(2)}, u32[]{:S(2)}) collective-permute-start(bf16[2,2,2,2,32,128]{5,4,3,2,1,0:T(8,128)(2,1)S(1)} %fusion.51), channel_id=1, source_target_pairs={{0,2},{2,0},{4,6},{6,4},{8,10},{10,8},{12,14},{14,12},{16,18},{18,... | collective-permute-start | bytes 393224 | tf_op jit(solution)/shard_map/ppermute | solution.py:550
  501.5 7.7 collective-permute-start.6
  509.2 48.4 %collective-permute-start.49 = (bf16[2,2,2,2,88,512]{5,4,0,1,2,3:T(8,128)(2,1)}, bf16[2,2,2,2,88,512]{5,4,0,1,2,3:T(8,128)(2,1)}, u32[]{:S(2)}, u32[]{:S(2)}) collective-permute-start(bf16[2,2,2,2,88,512]{5,4,0,1,2,3:T(8,128)(2,1)} %bitcast.349), channel_id=1, source_target_pairs={{0,2},{2,0},{4,6},{6,4},{8,10},{10,8},{12,14},{14,12},{16,18},{18,... | collective-permute-start | bytes 4325384 | tf_op jit(solution)/shard_map/ppermute | solution.py:550
  509.2 53.5 %collective-permute-start.44 = (bf16[2,2,2,2,88,512]{5,4,0,1,3,2:T(8,128)(2,1)}, bf16[2,2,2,2,88,512]{5,4,0,1,3,2:T(8,128)(2,1)}, u32[]{:S(2)}, u32[]{:S(2)}) collective-permute-start(bf16[2,2,2,2,88,512]{5,4,0,1,3,2:T(8,128)(2,1)} %bitcast.350), channel_id=1, source_target_pairs={{0,2},{2,0},{4,6},{6,4},{8,10},{10,8},{12,14},{14,12},{16,18},{18,... | collective-permute-start | bytes 4325384 | tf_op jit(solution)/shard_map/ppermute | solution.py:550
  515.1 4.6 collective-permute-start.8
  519.7 7.4 collective-permute-start.30
  527.1 7.1 collective-permute-start.25
  534.2 5.0 collective-permute-start.31
  539.2 5.0 collective-permute-start.26
  552.7 4.9 collective-permute-start.33
  557.6 80.7 %collective-permute-start.14 = (bf16[2,2,2,2,32,3072]{5,4,0,1,2,3:T(8,128)(2,1)S(1)}, bf16[2,2,2,2,32,3072]{5,4,0,1,2,3:T(8,128)(2,1)S(1)}, u32[]{:S(2)}, u32[]{:S(2)}) collective-permute-start(bf16[2,2,2,2,32,3072]{5,4,0,1,2,3:T(8,128)(2,1)S(1)} %bitcast.372), channel_id=1, source_target_pairs={{0,2},{2,0},{4,6},{6,4},{8,10},{10,8},{12,14},{14,12},{16,18},{18,... | collective-permute-start | bytes 9437192 | tf_op jit(solution)/shard_map/ppermute | solution.py:550
  557.6 7.4 collective-permute-start.28
  562.7 18.3 %collective-permute-start.50 = (bf16[2,2,2,88,512]{4,3,0,1,2:T(8,128)(2,1)S(1)}, bf16[2,2,2,88,512]{4,3,0,1,2:T(8,128)(2,1)S(1)}, u32[]{:S(2)}, u32[]{:S(2)}) collective-permute-start(bf16[2,2,2,88,512]{4,3,0,1,2:T(8,128)(2,1)S(1)} %fusion.25), channel_id=1, source_target_pairs={{0,1},{1,0},{2,3},{3,2},{4,5},{5,4},{6,7},{7,6},{8,9},{9,8},{10,11... | collective-permute-start | bytes 2162696 | tf_op jit(solution)/shard_map/ppermute | solution.py:550
  565.1 18.2 %collective-permute-start.45 = (bf16[2,2,2,88,512]{4,3,0,1,2:T(8,128)(2,1)S(1)}, bf16[2,2,2,88,512]{4,3,0,1,2:T(8,128)(2,1)S(1)}, u32[]{:S(2)}, u32[]{:S(2)}) collective-permute-start(bf16[2,2,2,88,512]{4,3,0,1,2:T(8,128)(2,1)S(1)} %fusion.24), channel_id=1, source_target_pairs={{0,4},{2,6},{4,0},{6,2},{8,12},{10,14},{12,8},{14,10},{16,20},{18,... | collective-permute-start | bytes 2162696 | tf_op jit(solution)/shard_map/ppermute | solution.py:550
  581.0 63.3 %collective-permute-start.9 = (bf16[2,2,2,2,32,3072]{5,4,0,1,3,2:T(8,128)(2,1)S(1)}, bf16[2,2,2,2,32,3072]{5,4,0,1,3,2:T(8,128)(2,1)}, u32[]{:S(2)}, u32[]{:S(2)}) collective-permute-start(bf16[2,2,2,2,32,3072]{5,4,0,1,3,2:T(8,128)(2,1)S(1)} %bitcast.371), channel_id=1, source_target_pairs={{0,2},{2,0},{4,6},{6,4},{8,10},{10,8},{12,14},{14,12},{16,18},{18,... | collective-permute-start | bytes 9437192 | tf_op jit(solution)/shard_map/ppermute | solution.py:550
  583.2 9.6 %collective-permute-start.51 = (bf16[2,2,88,512]{3,2,0,1:T(8,128)(2,1)S(1)}, bf16[2,2,88,512]{3,2,0,1:T(8,128)(2,1)S(1)}, u32[]{:S(2)}, u32[]{:S(2)}) collective-permute-start(bf16[2,2,88,512]{3,2,0,1:T(8,128)(2,1)S(1)} %fusion.35), channel_id=1, source_target_pairs={{0,4},{2,6},{4,0},{6,2},{8,12},{10,14},{12,8},{14,10},{16,20},{18,... | collective-permute-start | bytes 1081352 | tf_op jit(solution)/shard_map/ppermute | solution.py:550
  592.8 8.6 %collective-permute-start.46 = (bf16[2,2,88,512]{3,2,0,1:T(8,128)(2,1)S(1)}, bf16[2,2,88,512]{3,2,0,1:T(8,128)(2,1)S(1)}, u32[]{:S(2)}, u32[]{:S(2)}) collective-permute-start(bf16[2,2,88,512]{3,2,0,1:T(8,128)(2,1)S(1)} %fusion.34), channel_id=1, source_target_pairs={{0,1},{1,0},{2,3},{3,2},{4,5},{5,4},{6,7},{7,6},{8,9},{9,8},{10,11... | collective-permute-start | bytes 1081352 | tf_op jit(solution)/shard_map/ppermute | solution.py:550
  601.4 6.4 collective-permute-start.52
  607.8 6.8 collective-permute-start.47
  614.6 6.4 collective-permute-start.53
  621.0 6.0 collective-permute-start.48
  631.6 34.8 %collective-permute-start.40 = (bf16[2,2,2,32,2816]{4,3,0,1,2:T(8,128)(2,1)}, bf16[2,2,2,32,2816]{4,3,0,1,2:T(8,128)(2,1)}, u32[]{:S(2)}, u32[]{:S(2)}) collective-permute-start(bf16[2,2,2,32,2816]{4,3,0,1,2:T(8,128)(2,1)} %fusion.13), channel_id=1, source_target_pairs={{0,1},{1,0},{2,3},{3,2},{4,5},{5,4},{6,7},{7,6},{8,9},{9,8},{10,11... | collective-permute-start | bytes 4325384 | tf_op jit(solution)/shard_map/ppermute | solution.py:550
  637.2 34.8 %collective-permute-start.35 = (bf16[2,2,2,32,2816]{4,3,0,1,2:T(8,128)(2,1)}, bf16[2,2,2,32,2816]{4,3,0,1,2:T(8,128)(2,1)}, u32[]{:S(2)}, u32[]{:S(2)}) collective-permute-start(bf16[2,2,2,32,2816]{4,3,0,1,2:T(8,128)(2,1)} %fusion.12), channel_id=1, source_target_pairs={{0,4},{2,6},{4,0},{6,2},{8,12},{10,14},{12,8},{14,10},{16,20},{18,... | collective-permute-start | bytes 4325384 | tf_op jit(solution)/shard_map/ppermute | solution.py:550
  643.3 56.9 %collective-permute-start.15 = (bf16[2,2,2,32,3072]{4,3,0,1,2:T(8,128)(2,1)S(1)}, bf16[2,2,2,32,3072]{4,3,0,1,2:T(8,128)(2,1)}, u32[]{:S(2)}, u32[]{:S(2)}) collective-permute-start(bf16[2,2,2,32,3072]{4,3,0,1,2:T(8,128)(2,1)S(1)} %fusion.11), channel_id=1, source_target_pairs={{0,1},{1,0},{2,3},{3,2},{4,5},{5,4},{6,7},{7,6},{8,9},{9,8},{10,11... | collective-permute-start | bytes 4718600 | tf_op jit(solution)/shard_map/ppermute | solution.py:550
  648.1 57.4 %collective-permute-start.10 = (bf16[2,2,2,32,3072]{4,3,0,1,2:T(8,128)(2,1)S(1)}, bf16[2,2,2,32,3072]{4,3,0,1,2:T(8,128)(2,1)S(1)}, u32[]{:S(2)}, u32[]{:S(2)}) collective-permute-start(bf16[2,2,2,32,3072]{4,3,0,1,2:T(8,128)(2,1)S(1)} %fusion.10), channel_id=1, source_target_pairs={{0,4},{2,6},{4,0},{6,2},{8,12},{10,14},{12,8},{14,10},{16,20},{18,... | collective-permute-start | bytes 4718600 | tf_op jit(solution)/shard_map/ppermute | solution.py:550
  668.2 50.1 %collective-permute-start.41 = (bf16[2,2,32,2816]{3,2,0,1:T(8,128)(2,1)S(1)}, bf16[2,2,32,2816]{3,2,0,1:T(8,128)(2,1)S(1)}, u32[]{:S(2)}, u32[]{:S(2)}) collective-permute-start(bf16[2,2,32,2816]{3,2,0,1:T(8,128)(2,1)S(1)} %fusion.23), channel_id=1, source_target_pairs={{0,4},{2,6},{4,0},{6,2},{8,12},{10,14},{12,8},{14,10},{16,20},{18,... | collective-permute-start | bytes 2162696 | tf_op jit(solution)/shard_map/ppermute | solution.py:550
  674.0 46.7 %collective-permute-start.36 = (bf16[2,2,32,2816]{3,2,0,1:T(8,128)(2,1)S(1)}, bf16[2,2,32,2816]{3,2,0,1:T(8,128)(2,1)S(1)}, u32[]{:S(2)}, u32[]{:S(2)}) collective-permute-start(bf16[2,2,32,2816]{3,2,0,1:T(8,128)(2,1)S(1)} %fusion.22), channel_id=1, source_target_pairs={{0,1},{1,0},{2,3},{3,2},{4,5},{5,4},{6,7},{7,6},{8,9},{9,8},{10,11... | collective-permute-start | bytes 2162696 | tf_op jit(solution)/shard_map/ppermute | solution.py:550
  702.1 50.8 %collective-permute-start.16 = (bf16[2,2,32,3072]{3,2,0,1:T(8,128)(2,1)S(1)}, bf16[2,2,32,3072]{3,2,0,1:T(8,128)(2,1)S(1)}, u32[]{:S(2)}, u32[]{:S(2)}) collective-permute-start(bf16[2,2,32,3072]{3,2,0,1:T(8,128)(2,1)S(1)} %fusion.21), channel_id=1, source_target_pairs={{0,4},{2,6},{4,0},{6,2},{8,12},{10,14},{12,8},{14,10},{16,20},{18,... | collective-permute-start | bytes 2359304 | tf_op jit(solution)/shard_map/ppermute | solution.py:550
  706.1 48.1 %collective-permute-start.11 = (bf16[2,2,32,3072]{3,2,0,1:T(8,128)(2,1)S(1)}, bf16[2,2,32,3072]{3,2,0,1:T(8,128)(2,1)S(1)}, u32[]{:S(2)}, u32[]{:S(2)}) collective-permute-start(bf16[2,2,32,3072]{3,2,0,1:T(8,128)(2,1)S(1)} %fusion.20), channel_id=1, source_target_pairs={{0,1},{1,0},{2,3},{3,2},{4,5},{5,4},{6,7},{7,6},{8,9},{9,8},{10,11... | collective-permute-start | bytes 2359304 | tf_op jit(solution)/shard_map/ppermute | solution.py:550
  718.5 10.9 %collective-permute-start.42 = (bf16[2,32,2816]{2,1,0:T(8,128)(2,1)S(1)}, bf16[2,32,2816]{2,1,0:T(8,128)(2,1)S(1)}, u32[]{:S(2)}, u32[]{:S(2)}) collective-permute-start(bf16[2,32,2816]{2,1,0:T(8,128)(2,1)S(1)} %fusion.33), channel_id=1, source_target_pairs={{0,8},{2,10},{4,12},{6,14},{8,0},{10,2},{12,4},{14,6},{16,24},{18,... | collective-permute-start | bytes 1081352 | tf_op jit(solution)/shard_map/ppermute | solution.py:550
  720.9 19.5 %collective-permute-start.37 = (bf16[2,32,2816]{2,1,0:T(8,128)(2,1)S(1)}, bf16[2,32,2816]{2,1,0:T(8,128)(2,1)S(1)}, u32[]{:S(2)}, u32[]{:S(2)}) collective-permute-start(bf16[2,32,2816]{2,1,0:T(8,128)(2,1)S(1)} %fusion.32), channel_id=1, source_target_pairs={{0,8},{2,10},{4,12},{6,14},{8,0},{10,2},{12,4},{14,6},{16,24},{18,... | collective-permute-start | bytes 1081352 | tf_op jit(solution)/shard_map/ppermute | solution.py:550
  729.5 13.0 %collective-permute-start.43 = (bf16[32,2816]{1,0:T(8,128)(2,1)S(1)}, bf16[32,2816]{1,0:T(8,128)(2,1)S(1)}, u32[]{:S(2)}, u32[]{:S(2)}) collective-permute-start(bf16[32,2816]{1,0:T(8,128)(2,1)S(1)} %fusion.48), channel_id=1, source_target_pairs={{0,16},{2,18},{4,20},{6,22},{8,24},{10,26},{12,28},{14,30},{16,0},... | collective-permute-start | bytes 540680 | tf_op jit(solution)/shard_map/ppermute | solution.py:550
  740.5 11.5 %collective-permute-start.38 = (bf16[32,2816]{1,0:T(8,128)(2,1)S(1)}, bf16[32,2816]{1,0:T(8,128)(2,1)S(1)}, u32[]{:S(2)}, u32[]{:S(2)}) collective-permute-start(bf16[32,2816]{1,0:T(8,128)(2,1)S(1)} %fusion.47), channel_id=1, source_target_pairs={{0,16},{2,18},{4,20},{6,22},{8,24},{10,26},{12,28},{14,30},{16,0},... | collective-permute-start | bytes 540680 | tf_op jit(solution)/shard_map/ppermute | solution.py:550
  753.2 7.8 %collective-permute-start.17 = (bf16[2,32,3072]{2,1,0:T(8,128)(2,1)S(1)}, bf16[2,32,3072]{2,1,0:T(8,128)(2,1)S(1)}, u32[]{:S(2)}, u32[]{:S(2)}) collective-permute-start(bf16[2,32,3072]{2,1,0:T(8,128)(2,1)S(1)} %fusion.31), channel_id=1, source_target_pairs={{0,8},{2,10},{4,12},{6,14},{8,0},{10,2},{12,4},{14,6},{16,24},{18,... | collective-permute-start | bytes 1179656 | tf_op jit(solution)/shard_map/ppermute | solution.py:550
  754.5 10.8 %collective-permute-start.12 = (bf16[2,32,3072]{2,1,0:T(8,128)(2,1)S(1)}, bf16[2,32,3072]{2,1,0:T(8,128)(2,1)S(1)}, u32[]{:S(2)}, u32[]{:S(2)}) collective-permute-start(bf16[2,32,3072]{2,1,0:T(8,128)(2,1)S(1)} %fusion.30), channel_id=1, source_target_pairs={{0,8},{2,10},{4,12},{6,14},{8,0},{10,2},{12,4},{14,6},{16,24},{18,... | collective-permute-start | bytes 1179656 | tf_op jit(solution)/shard_map/ppermute | solution.py:550
  761.1 8.7 %collective-permute-start.18 = (bf16[32,3072]{1,0:T(8,128)(2,1)S(1)}, bf16[32,3072]{1,0:T(8,128)(2,1)S(1)}, u32[]{:S(2)}, u32[]{:S(2)}) collective-permute-start(bf16[32,3072]{1,0:T(8,128)(2,1)S(1)} %fusion.46), channel_id=1, source_target_pairs={{0,16},{2,18},{4,20},{6,22},{8,24},{10,26},{12,28},{14,30},{16,0},... | collective-permute-start | bytes 589832 | tf_op jit(solution)/shard_map/ppermute | solution.py:550
  765.3 8.7 %collective-permute-start.13 = (bf16[32,3072]{1,0:T(8,128)(2,1)S(1)}, bf16[32,3072]{1,0:T(8,128)(2,1)S(1)}, u32[]{:S(2)}, u32[]{:S(2)}) collective-permute-start(bf16[32,3072]{1,0:T(8,128)(2,1)S(1)} %fusion.45), channel_id=1, source_target_pairs={{0,16},{2,18},{4,20},{6,22},{8,24},{10,26},{12,28},{14,30},{16,0},... | collective-permute-start | bytes 589832 | tf_op jit(solution)/shard_map/ppermute | solution.py:550
  (93 other events, 1275.0 us)
Sparse Core Ops, SparseCore 0:
  10.9 126.7 all-gather.2
  140.6 67.2 all-gather.4

commit v2 on v1

--- a/solution.py
+++ b/solution.py
@@ -26,6 +26,27 @@
         (((left_dim,), (right_dim,)), ((), ())),
         preferred_element_type=jnp.float32,
     )
+
+
+def halves_of(values):
+    high = values.astype(jnp.bfloat16)
+    return high, (values - high.astype(jnp.float32)).astype(jnp.bfloat16)
+
+
+def mm3(left, right, left_dim=1, right_dim=0):
+    left_high, left_low = halves_of(left)
+    right_high, right_low = halves_of(right)
+    wide = right.shape[1 - right_dim]
+    lefts = jnp.concatenate([left_high, left_low], axis=left_dim)
+    rights = jnp.concatenate(
+        [
+            jnp.concatenate([right_high, right_high], axis=right_dim),
+            jnp.concatenate([right_low, jnp.zeros_like(right_low)], axis=right_dim),
+        ],
+        axis=1 - right_dim,
+    )
+    both = mm(lefts, rights, left_dim, right_dim)
+    return both[:, :wide] + both[:, wide:]
 
 
 def iotas(rows, columns):
@@ -52,8 +73,8 @@
 def unit_inverses(lowers, pair, levels, eye):
     inverses = [eye - jnp.where(pair, lower, 0.0) for lower in lowers]
     for level in levels:
-        parts = [mm(jnp.where(level, lower, 0.0), inv) for lower, inv in zip(lowers, inverses)]
-        inverses = [inv - mm(inv, part) for part, inv in zip(parts, inverses)]
+        parts = [mm3(jnp.where(level, lower, 0.0), inv) for lower, inv in zip(lowers, inverses)]
+        inverses = [inv - mm3(inv, part) for part, inv in zip(parts, inverses)]
     return inverses
 
 
@@ -122,8 +143,8 @@
         values = v_ref[:, here, :].reshape(SPAN, DV)
         queries = q_ref[here, :]
         link = link_matrix(rows, columns)
-        lower = jnp.where(strict, columns[:, 1:2] * twice(link) * mm(keys, keys, 1, 1), 0.0)
-        reading = link * mm(queries, keys, 1, 1)
+        lower = jnp.where(strict, columns[:, 1:2] * twice(link) * mm3(keys, keys, 1, 1), 0.0)
+        reading = link * mm3(queries, keys, 1, 1)
         lowers.append(lower)
         items.append((rows, columns, keys, values, queries, reading))
     inverses = unit_inverses(lowers, pair, levels, eye)
@@ -133,19 +154,19 @@
         inverse = inverses[chunk]
         here = slice(chunk * GROUP, (chunk + 1) * GROUP)
         beta, scale, tail = columns[:, 1:2], columns[:, 3:4], columns[:, 4:5]
-        key_part = mm(inverse, beta * scale * keys)
-        value_part = mm(inverse, beta * values)
+        key_part = mm3(inverse, beta * scale * keys)
+        value_part = mm3(inverse, beta * values)
         tail_keys = tail * keys
-        transfer = mm(key_part, tail_keys, 0, 0)
-        inject = mm(value_part, tail_keys, 0, 0)
+        transfer = mm3(key_part, tail_keys, 0, 0)
+        inject = mm3(value_part, tail_keys, 0, 0)
         x_out[0, chunk] = inverse.astype(x_out.dtype)
         w_out[0, chunk] = key_part.astype(w_out.dtype)
         u_out[0, chunk] = value_part.astype(u_out.dtype)
         t_out[0, chunk] = transfer.astype(t_out.dtype)
         i_out[0, chunk] = inject
-        ok_out[0, chunk] = (columns[:GROUP, 3:4] * queries - mm(reading, key_part)).astype(ok_out.dtype)
-        o_out[0, chunk] = mm(reading, value_part)
-        state = rows[3:4, GROUP - 1 : GROUP] * state - mm(state, transfer) + inject
+        ok_out[0, chunk] = (columns[:GROUP, 3:4] * queries - mm3(reading, key_part)).astype(ok_out.dtype)
+        o_out[0, chunk] = mm3(reading, value_part)
+        state = rows[3:4, GROUP - 1 : GROUP] * state - mm3(state, transfer) + inject
     state_out[0] = state
 
 
@@ -153,7 +174,7 @@
     chunks = t_in.shape[1]
     state = start_ref[0]
     for chunk in range(chunks):
-        state = vec_ref[0, chunk, 3:4, GROUP - 1 : GROUP] * state - mm(state, t_in[0, chunk])
+        state = vec_ref[0, chunk, 3:4, GROUP - 1 : GROUP] * state - mm3(state, t_in[0, chunk])
     state_out[0] = state
 
 
@@ -163,13 +184,13 @@
     states = []
     for chunk in range(chunks):
         states.append(state)
-        state = vec_ref[0, chunk, 3:4, GROUP - 1 : GROUP] * state - mm(state, t_in[0, chunk]) + i_in[0, chunk]
+        state = vec_ref[0, chunk, 3:4, GROUP - 1 : GROUP] * state - mm3(state, t_in[0, chunk]) + i_in[0, chunk]
     for chunk in range(chunks):
         here = slice(chunk * GROUP, (chunk + 1) * GROUP)
-        state = states[chunk].astype(jnp.bfloat16)
+        state = states[chunk]
         s_out[0, chunk] = state
-        u_out[0, chunk] = (u_in[0, chunk].astype(jnp.float32) - mm(w_in[0, chunk], state, 1, 1)).astype(u_out.dtype)
-        mixed = o_in[0, chunk] + mm(ok_in[0, chunk], state, 1, 1)
+        u_out[0, chunk] = (u_in[0, chunk].astype(jnp.float32) - mm3(w_in[0, chunk], state, 1, 1)).astype(u_out.dtype)
+        mixed = o_in[0, chunk] + mm3(ok_in[0, chunk], state, 1, 1)
         mixed_out[here, :] = mixed
         inv = lax.rsqrt(jnp.mean(mixed * mixed, axis=1, keepdims=True) + EPSILON)
         gate = silu_pair(gate_ref[here, :])[0]
@@ -194,15 +215,15 @@
         gain_grad = gain_grad + jnp.sum(d_scaled * unit, axis=0, keepdims=True)
         d_unit = d_scaled * gain
         d_mixed = inv * (d_unit - unit * jnp.mean(d_unit * unit, axis=1, keepdims=True))
-        d_mixed_low = d_mixed.astype(jnp.bfloat16)
+        d_mixed_low = d_mixed
         d_mixed_out[here, :] = d_mixed_low
-        local = mm(d_mixed_low, ok_in[0, chunk], 0, 0)
+        local = mm3(d_mixed_low, ok_in[0, chunk], 0, 0)
         local_out[0, chunk] = local
         locals_.append(local)
     gain_out[0] = jnp.broadcast_to(gain_grad, (8, DV))
     state = start_ref[0]
     for chunk in reversed(range(chunks)):
-        state = vec_ref[0, chunk, 3:4, GROUP - 1 : GROUP] * state - mm(state, t_in[0, chunk], 1, 1) + locals_[chunk]
+        state = vec_ref[0, chunk, 3:4, GROUP - 1 : GROUP] * state - mm3(state, t_in[0, chunk], 1, 1) + locals_[chunk]
     state_out[0] = state
 
 
@@ -241,7 +262,7 @@
     grad = exit_ref[0]
     for chunk in reversed(range(chunks)):
         exit_grads[chunk] = grad
-        grad = vec_ref[0, chunk, 3:4, GROUP - 1 : GROUP] * grad - mm(grad, t_in[0, chunk], 1, 1) + local_in[0, chunk]
+        grad = vec_ref[0, chunk, 3:4, GROUP - 1 : GROUP] * grad - mm3(grad, t_in[0, chunk], 1, 1) + local_in[0, chunk]
     for chunk in reversed(range(chunks)):
         here = slice(chunk * GROUP, (chunk + 1) * GROUP)
         rows, columns = chunk_vectors(vec_ref, chunk)
@@ -250,20 +271,20 @@
         values = v_ref[:, here, :].reshape(SPAN, DV)
         queries = q_ref[here, :]
         link = link_matrix(rows, columns)
-        link_gram = jnp.where(strict, twice(link) * mm(keys, keys, 1, 1), 0.0)
-        reading = link * mm(queries, keys, 1, 1)
+        link_gram = jnp.where(strict, twice(link) * mm3(keys, keys, 1, 1), 0.0)
+        reading = link * mm3(queries, keys, 1, 1)
         d_exit = exit_grads[chunk]
         solved = u_in[0, chunk]
         entry = s_in[0, chunk]
         d_mixed = d_mixed_in[here, :]
         tail_keys = tail * keys
-        d_solved = mm(reading, d_mixed, 0, 0) + mm(tail_keys, d_exit, 1, 1)
-        d_right = mm(x_in[0, chunk], d_solved, 0, 0)
-        d_lower = jnp.where(strict, -mm(d_right, solved, 1, 1), 0.0)
-        d_tail_keys = mm(solved, d_exit)
-        d_right_entry = mm(d_right, entry)
-        d_reading = mm(d_mixed, solved, 1, 1)
-        d_query_entry = mm(d_mixed, entry)
+        d_solved = mm3(reading, d_mixed, 0, 0) + mm3(tail_keys, d_exit, 1, 1)
+        d_right = mm3(x_in[0, chunk], d_solved, 0, 0)
+        d_lower = jnp.where(strict, -mm3(d_right, solved, 1, 1), 0.0)
+        d_tail_keys = mm3(solved, d_exit)
+        d_right_entry = mm3(d_right, entry)
+        d_reading = mm3(d_mixed, solved, 1, 1)
+        d_query_entry = mm3(d_mixed, entry)
         both_scale = -jnp.sum(d_right_entry * keys, axis=1, keepdims=True)
         lower_weight = d_lower * link_gram
         d_beta = (
@@ -279,10 +300,10 @@
         d_keys = (
             tail * d_tail_keys
             - beta * scale * d_right_entry
-            + mm(d_gram, keys)
-            + mm(d_query_gram, queries, 0, 0)
+            + mm3(d_gram, keys)
+            + mm3(d_query_gram, queries, 0, 0)
         )
-        d_queries = mm(d_query_gram, keys) + scale[:GROUP] * d_query_entry
+        d_queries = mm3(d_query_gram, keys) + scale[:GROUP] * d_query_entry
         d_values = beta * d_right
         none = jnp.zeros((GROUP, 1), jnp.float32)
         d_gap = jnp.sum(lower_moment, axis=1, keepdims=True) + jnp.concatenate(
@@ -528,6 +549,696 @@
     return [part.reshape((-1,) + part.shape[5:]) if part.ndim == 6 else part for part in outs]
 
 
+WIDE = 256
+RING = 4
+SPAN_TICKS = 2
+REDUCE_STAGES = 5
+CORE, NEAR, FAR, RINGS = 0, 1, 2, 3
+
+
+class Reduce:
+    def __init__(self, refs, lane, count):
+        (
+            self.own, self.first_send, self.first, self.near_kept, self.near_send, self.near,
+            self.far_kept, self.far_send, self.far, self.last_kept, self.last_send, self.last,
+            self.load_sem, self.send_sem, self.recv_sem,
+        ) = refs
+        self.lane, self.count = lane, count
+        self.z, self.x, self.core, self.y = place()
+        self.peers = peers()
+        self.x_first = lane == 0
+
+    def copy(self, source, target, slot_of, stage, index, device):
+        lane = self.lane
+        return pltpu.make_async_remote_copy(
+            src_ref=source, dst_ref=target,
+            send_sem=self.send_sem.at[lane, stage, lax.rem(index, 2)],
+            recv_sem=self.recv_sem.at[lane, stage, lax.rem(index, RING)],
+            device_id=device, device_id_type=MESH,
+        )
+
+    def core_copy(self, source, index):
+        return self.copy(source, self.first.at[self.lane, lax.rem(index, RING)], None, CORE, index, self.peers[ZS + 1])
+
+    def near_copy(self, index):
+        lane = self.lane
+        return self.copy(
+            self.near_send.at[lane, lax.rem(index, 2)], self.near.at[lane, lax.rem(index, RING)], None, NEAR, index,
+            self.peers[ZS - 1 if self.x_first else ZS],
+        )
+
+    def far_copy(self, index):
+        lane = self.lane
+        return self.copy(
+            self.far_send.at[lane, lax.rem(index, 2)], self.far.at[lane, lax.rem(index, RING)], None, FAR, index,
+            self.peers[ZS if self.x_first else ZS - 1],
+        )
+
+    def ring_copies(self, index):
+        lane = self.lane
+        return [
+            self.copy(
+                self.last_send.at[lane, lax.rem(index, 2), step], self.last.at[lane, lax.rem(index, RING), step],
+                None, RINGS + step, index, self.peers[step],
+            )
+            for step in range(ZS - 1)
+        ]
+
+    def load_copy(self, source, index):
+        slot = lax.rem(index, 2)
+        return pltpu.make_async_copy(source, self.own.at[self.lane, slot], self.load_sem.at[self.lane, slot])
+
+    def from_core(self, index, loaded):
+        lane, slot, ring = self.lane, lax.rem(index, 2), lax.rem(index, RING)
+        arrived = self.core_copy(self.first_send.at[lane, slot], index)
+        arrived.wait_recv()
+        arrived.wait_send()
+
+        @pl.when(loaded)
+        def _():
+            self.load_copy(self.first_send.at[lane, slot], index).wait()
+
+        def one(z, carry):
+            if self.x_first:
+                pick = lambda ref, half: ref[lane, slot, z, half]
+                pick_got = lambda half: self.first[lane, ring, z, half]
+                mine = self.x
+            else:
+                pick = lambda ref, half: ref[lane, slot, z, :, half]
+                pick_got = lambda half: self.first[lane, ring, z, :, half]
+                mine = self.y
+            kept = pick(self.own, mine).astype(jnp.float32) + pick_got(mine).astype(jnp.float32)
+            sent = pick(self.own, 1 - mine).astype(jnp.float32) + pick_got(1 - mine).astype(jnp.float32)
+            self.near_kept[lane, slot, z] = kept
+            self.near_send[lane, slot, z] = sent.astype(jnp.bfloat16)
+            return carry
+
+        lax.fori_loop(0, ZS, one, 0)
+        self.near_copy(index).start()
+
+    def from_near(self, index):
+        lane, slot, ring = self.lane, lax.rem(index, 2), lax.rem(index, RING)
+        arrived = self.near_copy(index)
+        arrived.wait_recv()
+        arrived.wait_send()
+        mine = self.y if self.x_first else self.x
+
+        def one(z, carry):
+            kept = self.near_kept[lane, slot, z, mine] + self.near[lane, ring, z, mine].astype(jnp.float32)
+            sent = self.near_kept[lane, slot, z, 1 - mine] + self.near[lane, ring, z, 1 - mine].astype(jnp.float32)
+            self.far_kept[lane, slot, z] = kept
+            self.far_send[lane, slot, z] = sent.astype(jnp.bfloat16)
+            return carry
+
+        lax.fori_loop(0, ZS, one, 0)
+        self.far_copy(index).start()
+
+    def from_far(self, index):
+        lane, slot, ring = self.lane, lax.rem(index, 2), lax.rem(index, RING)
+        arrived = self.far_copy(index)
+        arrived.wait_recv()
+        arrived.wait_send()
+
+        def total(z):
+            return self.far_kept[lane, slot, z] + self.far[lane, ring, z].astype(jnp.float32)
+
+        self.last_kept[lane, slot] = total(self.z)
+        for step, copy in enumerate(self.ring_copies(index)):
+            self.last_send[lane, slot, step] = total(lax.rem(self.z + 1 + step, ZS)).astype(jnp.bfloat16)
+            copy.start()
+
+    def from_ring(self, index):
+        lane, slot, ring = self.lane, lax.rem(index, 2), lax.rem(index, RING)
+        total = self.last_kept[lane, slot]
+        for step, copy in enumerate(self.ring_copies(index)):
+            copy.wait_recv()
+            copy.wait_send()
+            total = total + self.last[lane, ring, step].astype(jnp.float32)
+        return total
+
+
+def reduce_scratch(rows):
+    half = (2, 2, rows, WIDE)
+    lanes = 2
+    return [
+        pltpu.VMEM((lanes, 2, ZS) + half, jnp.bfloat16),
+        pltpu.VMEM((lanes, 2, ZS) + half, jnp.bfloat16),
+        pltpu.VMEM((lanes, RING, ZS) + half, jnp.bfloat16),
+        pltpu.VMEM((lanes, 2, ZS, 2, rows, WIDE), jnp.float32),
+        pltpu.VMEM((lanes, 2, ZS, 2, rows, WIDE), jnp.bfloat16),
+        pltpu.VMEM((lanes, RING, ZS, 2, rows, WIDE), jnp.bfloat16),
+        pltpu.VMEM((lanes, 2, ZS, rows, WIDE), jnp.float32),
+        pltpu.VMEM((lanes, 2, ZS, rows, WIDE), jnp.bfloat16),
+        pltpu.VMEM((lanes, RING, ZS, rows, WIDE), jnp.bfloat16),
+        pltpu.VMEM((lanes, 2, rows, WIDE), jnp.float32),
+        pltpu.VMEM((lanes, 2, ZS - 1, rows, WIDE), jnp.bfloat16),
+        pltpu.VMEM((lanes, RING, ZS - 1, rows, WIDE), jnp.bfloat16),
+        pltpu.SemaphoreType.DMA((lanes, 2)),
+        pltpu.SemaphoreType.DMA((lanes, RINGS + ZS - 1, 2)),
+        pltpu.SemaphoreType.DMA((lanes, RINGS + ZS - 1, RING)),
+    ]
+
+
+def at_columns(ref, core, first, row=0, rows=32):
+    return ref.at[:, :, core, :, pl.ds(row, rows), pl.ds(pl.multiple_of(first, WIDE), WIDE)]
+
+
+def make_mixer_back_kernel(length, gu_count, down_count, out_count, down_blocks):
+    chunks = length // GROUP
+    parts = 1 + 2 * NH
+    pairs = H // 2
+    gate_count = H * DV // WIDE
+    down_first = gu_count
+    out_first = down_first + down_count
+    gate_first = out_first + out_count
+    head_first = gate_first + gate_count
+    items = head_first + parts * pairs
+    count = items // 2
+    early_ticks = H // 2
+    ticks = count + (REDUCE_STAGES - 1) * SPAN_TICKS
+    head_ticks = 3
+    rows = 32
+
+    def kernel(
+        vec_ref, t_in, ok_in, mixed_in, gate_ref, gain_ref, d_gated_ref,
+        q_in, k0_in, k1_in, v0_in, v1_in, bq, bk0, bk1, bv0, bv1, tq, tk0, tk1, tv0, tv1, mask_ref,
+        x_in, u_in, s_in, normed_ref, gu_in, down_in, out_in,
+        gain_out, d_vec_out, gq_out, gk0_out, gk1_out, gv0_out, gv1_out, d_projected_out,
+        gu_out, down_out, out_out, mix_out,
+        d_mixed_ref, local_ref, all_ref, relay_send, relay_recv, edge_send, edge_recv, tail_ref,
+        ext_ref, pre_ref, q_ref, k_ref, v_ref, inv_ref, d_ref, z_ref,
+        relay_sems, edge_send_sem, edge_recv_sem, store_sem, *engine_refs,
+    ):
+        step = pl.program_id(0)
+        z, x, core, y = place()
+        y_peer = device_at(z, x, core, 1 - y)
+        lanes = [Reduce(engine_refs, lane, count) for lane in range(2)]
+        first_device = jnp.where(y == 0, 1.0, 0.0)
+
+        def source_of(item):
+            within = item - head_first
+            is_gate = item < head_first
+            part = jnp.where(is_gate, parts, lax.rem(within, parts))
+            column = jnp.where(is_gate, item - gate_first, within // parts) * WIDE
+            return part, column
+
+        def begin(lane, index):
+            engine = lanes[lane]
+            item = 2 * index + lane
+            slot = lax.rem(index, 2)
+
+            def from_hbm(ref, first, row):
+                engine.core_copy(at_columns(ref, 1 - core, first, row), index).start()
+                engine.load_copy(at_columns(ref, core, first, row), index).start()
+
+            @pl.when(item < down_first)
+            def _():
+                from_hbm(gu_in, item * WIDE, 0)
+
+            @pl.when((item >= down_first) & (item < out_first))
+            def _():
+                within = item - down_first
+                from_hbm(down_in, lax.rem(within, 4) * WIDE, pl.multiple_of((within // 4) * rows, rows))
+
+            @pl.when((item >= out_first) & (item < gate_first))
+            def _():
+                from_hbm(out_in, (item - out_first) * WIDE, 0)
+
+            @pl.when(item >= gate_first)
+            def _():
+                part, column = source_of(item)
+                right = all_ref[part, :, pl.ds(pl.multiple_of(column, WIDE), WIDE)]
+                for half, target in ((1 - core, engine.first_send), (core, engine.own)):
+                    left = normed_ref[:, :, half].reshape(-1, length)
+                    target[lane, slot] = mm(left, right).astype(jnp.bfloat16).reshape(ZS, 2, 2, rows, WIDE)
+                engine.core_copy(engine.first_send.at[lane, slot], index).start()
+
+        def end(lane, index):
+            item = 2 * index + lane
+            total = lanes[lane].from_ring(index)
+
+            def here(first):
+                return pl.ds(pl.multiple_of(first, WIDE), WIDE)
+
+            @pl.when(item < down_first)
+            def _():
+                gu_out[:, here(item * WIDE)] = total
+
+            @pl.when((item >= down_first) & (item < out_first))
+            def _():
+                within = item - down_first
+                down_out[within // 4, :, here(lax.rem(within, 4) * WIDE)] = total
+
+            @pl.when((item >= out_first) & (item < gate_first))
+            def _():
+                out_out[:, here((item - out_first) * WIDE)] = total
+
+            @pl.when(item >= gate_first)
+            def _():
+                part, column = source_of(item)
+                mix_out[:, here(part * (H * DK) + column)] = total
+
+        def tick(number):
+            for stage in reversed(range(REDUCE_STAGES)):
+                index = number - stage * SPAN_TICKS
+
+                @pl.when((index >= 0) & (index < count))
+                def _():
+                    for lane in range(2):
+                        engine = lanes[lane]
+                        if stage == 0:
+                            begin(lane, index)
+                        elif stage == 1:
+                            engine.from_core(index, 2 * index + lane < gate_first)
+                        elif stage == 2:
+                            engine.from_near(index)
+                        elif stage == 3:
+                            engine.from_far(index)
+                        else:
+                            end(lane, index)
+
+        def readout_back(head):
+            gain = gain_ref[0:1, :]
+            gain_grad = jnp.zeros((1, DV), jnp.float32)
+            column = pl.ds(pl.multiple_of(head * DV, DV), DV)
+            locals_ = []
+            for chunk in range(chunks):
+                here = slice(chunk * GROUP, (chunk + 1) * GROUP)
+                mixed = mixed_in[here, :]
+                inv = lax.rsqrt(jnp.mean(mixed * mixed, axis=1, keepdims=True) + EPSILON)
+                unit = mixed * inv
+                gate = gate_ref[here, :]
+                open_, sig = silu_pair(gate)
+                d_gated = d_gated_ref[here, :]
+                d_scaled = d_gated * open_
+                d_gate = d_gated * unit * gain * sig * (1.0 + gate * (1.0 - sig))
+                all_ref[parts, here, column] = d_gate.astype(jnp.bfloat16)
+                gain_grad = gain_grad + jnp.sum(d_scaled * unit, axis=0, keepdims=True)
+                d_unit = d_scaled * gain
+                d_mixed = inv * (d_unit - unit * jnp.mean(d_unit * unit, axis=1, keepdims=True))
+                d_mixed_ref[head, here] = d_mixed
+                local = mm3(d_mixed, ok_in[0, chunk], 0, 0)
+                local_ref[head, chunk] = local
+                locals_.append(local)
+            gain_out[0] = jnp.broadcast_to(gain_grad, (8, DV))
+            state = jnp.zeros((DV, DK), jnp.float32)
+            for chunk in reversed(range(chunks)):
+                state = (
+                    vec_ref[0, chunk, 3:4, GROUP - 1 : GROUP] * state
+                    - mm3(state, t_in[0, chunk], 1, 1)
+                    + locals_[chunk]
+                )
+            relay_send[head] = state.astype(jnp.bfloat16)
+
+        channels = (q_in, k0_in, k1_in, v0_in, v1_in)
+        taps = (tq, tk0, tk1, tv0, tv1)
+
+        def prepare(head):
+            for part, (channel, border, tap) in enumerate(zip(channels, (bq, bk0, bk1, bv0, bv1), taps)):
+                pre = conv_block(channel, border, tap, mask_ref, ext_ref.at[part])
+                pre_ref[part] = pre
+                value = silu_pair(pre)[0]
+                if part == 0:
+                    unit, inv = unit_rows(value)
+                    q_ref[...] = unit * DK ** (-0.5)
+                    inv_ref[0] = jnp.broadcast_to(inv, (length, DK))
+                elif part <= NH:
+                    unit, inv = unit_rows(value)
+                    k_ref[part - 1] = unit
+                    inv_ref[part] = jnp.broadcast_to(inv, (length, DK))
+                else:
+                    v_ref[part - 1 - NH] = value
+
+        def chain(head):
+            exit_grads = [None] * chunks
+            grad = first_device * relay_recv[head].astype(jnp.float32)
+            for chunk in reversed(range(chunks)):
+                exit_grads[chunk] = grad
+                grad = (
+                    vec_ref[0, chunk, 3:4, GROUP - 1 : GROUP] * grad
+                    - mm3(grad, t_in[0, chunk], 1, 1)
+                    + local_ref[head, chunk]
+                )
+            return exit_grads
+
+        def one_chunk(chunk, head, d_exit):
+            strict = order_masks()[0]
+            column_index = iotas(SPAN, 8)[1]
+            here = slice(chunk * GROUP, (chunk + 1) * GROUP)
+            rows_, columns = chunk_vectors(vec_ref, chunk)
+            beta, scale, tail = columns[:, 1:2], columns[:, 3:4], columns[:, 4:5]
+            keys = k_ref[:, here, :].reshape(SPAN, DK)
+            values = v_ref[:, here, :].reshape(SPAN, DV)
+            queries = q_ref[here, :]
+            link = link_matrix(rows_, columns)
+            link_gram = jnp.where(strict, twice(link) * mm3(keys, keys, 1, 1), 0.0)
+            reading = link * mm3(queries, keys, 1, 1)
+            solved = u_in[0, chunk]
+            entry = s_in[0, chunk]
+            d_mixed = d_mixed_ref[head, here]
+            tail_keys = tail * keys
+            d_solved = mm3(reading, d_mixed, 0, 0) + mm3(tail_keys, d_exit, 1, 1)
+            d_right = mm3(x_in[0, chunk], d_solved, 0, 0)
+            d_lower = jnp.where(strict, -mm3(d_right, solved, 1, 1), 0.0)
+            d_tail_keys = mm3(solved, d_exit)
+            d_right_entry = mm3(d_right, entry)
+            d_reading = mm3(d_mixed, solved, 1, 1)
+            d_query_entry = mm3(d_mixed, entry)
+            both_scale = -jnp.sum(d_right_entry * keys, axis=1, keepdims=True)
+            lower_weight = d_lower * link_gram
+            d_beta = (
+                jnp.sum(d_right * values, axis=1, keepdims=True)
+                + scale * both_scale
+                + jnp.sum(lower_weight, axis=1, keepdims=True)
+            )
+            lower_moment = lower_weight * beta
+            reading_moment = d_reading * reading
+            d_gram = beta * twice(link) * d_lower
+            d_gram = d_gram + jnp.transpose(d_gram)
+            d_query_gram = link * d_reading
+            d_keys = (
+                tail * d_tail_keys
+                - beta * scale * d_right_entry
+                + mm3(d_gram, keys)
+                + mm3(d_query_gram, queries, 0, 0)
+            )
+            d_queries = mm3(d_query_gram, keys) + scale[:GROUP] * d_query_entry
+            d_values = beta * d_right
+            none = jnp.zeros((GROUP, 1), jnp.float32)
+            d_gap = jnp.sum(lower_moment, axis=1, keepdims=True) + jnp.concatenate(
+                [jnp.sum(reading_moment, axis=1, keepdims=True), none], axis=0
+            )
+            last = jnp.sum(jnp.sum(d_exit * entry, axis=1, keepdims=True), axis=0, keepdims=True)
+            own_scale = jnp.sum(d_query_entry * queries, axis=1, keepdims=True)
+            own_scale = own_scale + jnp.where(iotas(GROUP, 1)[0] == GROUP - 1, last, 0.0)
+            d_scale = beta * both_scale + jnp.concatenate([own_scale, none], axis=0)
+            d_tail = jnp.sum(d_tail_keys * keys, axis=1, keepdims=True)
+            grads = jnp.where(
+                column_index == 0,
+                d_gap,
+                jnp.where(
+                    column_index == 1,
+                    d_beta,
+                    jnp.where(column_index == 3, d_scale, jnp.where(column_index == 4, d_tail, 0.0)),
+                ),
+            )
+            grads = jnp.transpose(grads)
+            sums = jnp.sum(lower_moment, axis=0, keepdims=True) + jnp.sum(reading_moment, axis=0, keepdims=True)
+            d_vec_out[0, chunk] = grads - jnp.where(iotas(8, SPAN)[0] == 0, sums, 0.0)
+            d_ref[0, here, :] = d_queries
+            for house in range(NH):
+                mine = slice(house * GROUP, (house + 1) * GROUP)
+                d_ref[1 + house, here, :] = d_keys[mine]
+                d_ref[1 + NH + house, here, :] = d_values[mine]
+
+        def finish_head(head):
+            tap_grads = (gq_out, gk0_out, gk1_out, gv0_out, gv1_out)
+            column = pl.ds(pl.multiple_of(head * DK, DK), DK)
+            z_ref[0:8, :] = jnp.zeros((8, DK), jnp.float32)
+            z_ref[8 + length : 16 + length, :] = jnp.zeros((8, DK), jnp.float32)
+            for part in range(parts):
+                grad = d_ref[part]
+                if part <= NH:
+                    unit = q_ref[...] * DK ** 0.5 if part == 0 else k_ref[part - 1]
+                    if part == 0:
+                        grad = grad * DK ** (-0.5)
+                    grad = inv_ref[part] * (grad - unit * jnp.sum(grad * unit, axis=1, keepdims=True))
+                pre = pre_ref[part]
+                sig = jax.nn.sigmoid(pre)
+                grad = grad * sig * (1.0 + pre * (1.0 - sig))
+                tap = taps[part]
+                total = grad * tap[0:1, :]
+                edge = jnp.zeros((8, DK), jnp.float32)
+                tap_rows = [jnp.sum(grad * channels[part][...], axis=0, keepdims=True)]
+                for index in range(1, 4):
+                    shifted = grad * mask_ref[index - 1]
+                    tap_rows.append(
+                        jnp.sum(shifted * ext_ref[part, 8 - index : 8 - index + length, :], axis=0, keepdims=True)
+                    )
+                    z_ref[8 : 8 + length, :] = shifted * tap[index : index + 1, :]
+                    total = total + z_ref[8 + index : 8 + index + length, :]
+                    edge = edge + z_ref[index : index + 8, :]
+                all_ref[part, :, column] = total.astype(jnp.bfloat16)
+                edge_send[lax.rem(head, 2), part] = edge
+                tail_ref[part] = total[length - 16 :, :]
+                tap_grads[part][...] = jnp.concatenate(tap_rows + [jnp.zeros((4, DK), jnp.float32)], axis=0)
+
+        @pl.when(step == 0)
+        def _():
+            meet(peers())
+
+        @pl.when((step < H) & (lax.rem(step, 2) == 0))
+        def _():
+            tick(step // 2)
+
+        @pl.when(step < H)
+        def _():
+            readout_back(step)
+
+        relay = pltpu.make_async_remote_copy(
+            src_ref=relay_send, dst_ref=relay_recv, send_sem=relay_sems.at[0], recv_sem=relay_sems.at[1],
+            device_id=y_peer, device_id_type=MESH,
+        )
+
+        @pl.when(step == H - 1)
+        def _():
+            relay.start()
+
+        @pl.when(step == H)
+        def _():
+            relay.wait()
+
+        def edge_copy(head):
+            slot = lax.rem(head, 2)
+            return pltpu.make_async_remote_copy(
+                src_ref=edge_send.at[slot], dst_ref=edge_recv.at[slot], send_sem=edge_send_sem.at[slot],
+                recv_sem=edge_recv_sem.at[slot], device_id=y_peer, device_id_type=MESH,
+            )
+
+        @pl.when(step > H)
+        def _():
+            head = step - H - 1
+            edge = edge_copy(head)
+            edge.wait()
+            here = pl.ds(pl.multiple_of(head * DK, DK), DK)
+            for part in range(parts):
+                fixed = tail_ref[part, 8:16] + first_device * edge_recv[lax.rem(head, 2), part]
+                both = jnp.concatenate([tail_ref[part, 0:8], fixed], axis=0)
+                all_ref[part, length - 16 : length, here] = both.astype(jnp.bfloat16)
+
+        head_tick = early_ticks + (step - H) * head_ticks
+
+        @pl.when((step >= H) & (step < 2 * H))
+        def _():
+            head = step - H
+            tick(head_tick)
+            prepare(head)
+            exit_grads = chain(head)
+            for chunk in reversed(range(chunks // 2, chunks)):
+                one_chunk(chunk, head, exit_grads[chunk])
+            tick(head_tick + 1)
+            for chunk in reversed(range(chunks // 2)):
+                one_chunk(chunk, head, exit_grads[chunk])
+            tick(head_tick + 2)
+            finish_head(head)
+            edge_copy(head).start()
+
+        @pl.when(step == 2 * H)
+        def _():
+            stores = [
+                pltpu.make_async_copy(
+                    all_ref.at[part], d_projected_out.at[:, pl.ds(part * H * DK, H * DK)], store_sem.at[part]
+                )
+                for part in range(parts + 1)
+            ]
+            for store in stores:
+                store.start()
+
+            def drain(number, carry):
+                tick(number)
+                return carry
+
+            lax.fori_loop(early_ticks + H * head_ticks, ticks, drain, 0)
+            for store in stores:
+                store.wait()
+
+    return kernel, ticks
+
+
+def mixer_back_call(
+    vec, transfer, out_keys, mixed, projected, gain, d_gated, border, taps, masks, inverse, solved, entries,
+    normed_t, grad_gu, grad_down, grad_out,
+):
+    length = projected.shape[0]
+    chunks = length // GROUP
+    parts = 1 + 2 * NH
+    rows = grad_gu.shape[4]
+    down_blocks = grad_down.shape[4] // rows
+    kernel, ticks = make_mixer_back_kernel(
+        length, grad_gu.shape[5] // WIDE, down_blocks * (grad_down.shape[5] // WIDE), grad_out.shape[5] // WIDE, down_blocks
+    )
+
+    def either(step):
+        return lax.rem(step, H)
+
+    def early(step):
+        return jnp.minimum(step, H - 1)
+
+    def late(step):
+        return jnp.clip(step - H, 0, H - 1)
+
+    def heads(shape, which):
+        rank = len(shape)
+        return pl.BlockSpec((1,) + shape, lambda step: (which(step),) + (0,) * rank)
+
+    def cols(count, first, which):
+        return pl.BlockSpec((count, DK), lambda step: (0, first + which(step)))
+
+    def whole(shape):
+        rank = len(shape)
+        return pl.BlockSpec(shape, lambda step: (0,) * rank)
+
+    square = (chunks, SPAN, DK)
+    anywhere = pl.BlockSpec(memory_space=pl.ANY)
+    in_specs = (
+        [
+            heads((chunks, 8, SPAN), either), heads(square, either), heads((chunks, GROUP, DK), early),
+            cols(length, 0, early), cols(length, parts * H, early), whole((8, DV)), cols(length, 0, early),
+        ]
+        + [cols(length, H * part, late) for part in range(parts)]
+        + [cols(8, H * part, late) for part in range(parts)] * 2
+        + [whole((3, length, DK))]
+        + [heads(square, late)] * 3
+        + [whole(normed_t.shape)]
+        + [anywhere] * 3
+    )
+    shard = (rows,)
+    out_shape = (
+        [per_head((8, DV)), per_head((chunks, 8, SPAN))]
+        + [jax.ShapeDtypeStruct((8, H * DK), jnp.float32)] * parts
+        + [
+            jax.ShapeDtypeStruct((length, (parts + 1) * H * DK), jnp.bfloat16),
+            jax.ShapeDtypeStruct((rows, grad_gu.shape[5]), jnp.float32),
+            jax.ShapeDtypeStruct((down_blocks, rows, grad_down.shape[5]), jnp.float32),
+            jax.ShapeDtypeStruct((rows, grad_out.shape[5]), jnp.float32),
+            jax.ShapeDtypeStruct((rows, (parts + 1) * H * DK), jnp.float32),
+        ]
+    )
+    out_specs = (
+        [heads((8, DV), early), heads((chunks, 8, SPAN), late)]
+        + [cols(8, 0, late)] * parts
+        + [anywhere]
+        + [whole(out.shape) for out in out_shape[-4:]]
+    )
+    tall = pltpu.VMEM((parts, length, DK), jnp.float32)
+    scratch = [
+        pltpu.VMEM((H, length, DV), jnp.float32),
+        pltpu.VMEM((H,) + square, jnp.float32),
+        pltpu.VMEM((parts + 1, length, H * DK), jnp.bfloat16),
+        pltpu.VMEM((H, DV, DK), jnp.bfloat16),
+        pltpu.VMEM((H, DV, DK), jnp.bfloat16),
+        pltpu.VMEM((2, parts, 8, DK), jnp.float32),
+        pltpu.VMEM((2, parts, 8, DK), jnp.float32),
+        pltpu.VMEM((parts, 16, DK), jnp.float32),
+        pltpu.VMEM((parts, length + 8, DK), jnp.float32),
+        tall,
+        pltpu.VMEM((length, DK), jnp.float32),
+        pltpu.VMEM((NH, length, DK), jnp.float32),
+        pltpu.VMEM((NH, length, DK), jnp.float32),
+        pltpu.VMEM((1 + NH, length, DK), jnp.float32),
+        tall,
+        pltpu.VMEM((length + 16, DK), jnp.float32),
+        pltpu.SemaphoreType.DMA((2,)),
+        pltpu.SemaphoreType.DMA((2,)),
+        pltpu.SemaphoreType.DMA((2,)),
+        pltpu.SemaphoreType.DMA((parts + 1,)),
+    ] + reduce_scratch(rows)
+    return pl.pallas_call(
+        kernel,
+        grid=(2 * H + 1,),
+        out_shape=out_shape,
+        in_specs=in_specs,
+        out_specs=out_specs,
+        scratch_shapes=scratch,
+        compiler_params=pltpu.CompilerParams(
+            dimension_semantics=("arbitrary",), collective_id=2, has_side_effects=True, vmem_limit_bytes=58 * 1024 * 1024
+        ),
+        cost_estimate=pl.CostEstimate(
+            flops=H * chunks * 14 * 2 * SPAN**3 * 4, bytes_accessed=100_000_000, transcendentals=0
+        ),
+    )(
+        vec, transfer, out_keys, mixed, projected, gain, d_gated,
+        *[projected] * parts, *[border] * parts, *[taps] * parts, masks,
+        inverse, solved, entries, normed_t, grad_gu, grad_down, grad_out,
+    )
+
+
+def total_kernel(packed_ref, sums_ref, packed_out, sums_out, first, near, far, last, kept, pair, ring, send, recv):
+    z, x, core, y = place()
+    targets = peers()
+    meet(targets)
+
+    def copy(source, target, slot, device):
+        made = pltpu.make_async_remote_copy(
+            src_ref=source, dst_ref=target, send_sem=send.at[slot], recv_sem=recv.at[slot],
+            device_id=device, device_id_type=MESH,
+        )
+        made.start()
+        return made
+
+    def swap(source, target, index, device):
+        pair[2 * index] = sums_out[...]
+        copies = [
+            copy(source, target, 2 * index, device),
+            copy(pair.at[2 * index], pair.at[2 * index + 1], 2 * index + 1, device),
+        ]
+        for made in copies:
+            made.wait()
+        sums_out[...] = sums_out[...] + pair[2 * index + 1]
+
+    sums_out[...] = sums_ref[...]
+    swap(packed_ref.at[:, :, 1 - core], first, 0, targets[ZS + 1])
+    kept[...] = packed_ref[:, :, core] + first[...]
+    swap(kept.at[:, 1 - x], near, 1, targets[ZS - 1])
+    kept[:, 0] = kept[:, x] + near[...]
+    swap(kept.at[:, 0, 1 - y], far, 2, targets[ZS])
+    kept[:, 0, 0] = kept[:, 0, y] + far[...]
+    ring[z] = sums_out[...]
+    copies = []
+    for step in range(ZS - 1):
+        other = lax.rem(z + 1 + step, ZS)
+        copies.append(copy(kept.at[other, 0, 0], last.at[step], 6 + 2 * step, targets[step]))
+        copies.append(copy(ring.at[z], ring.at[z], 7 + 2 * step, targets[step]))
+    for made in copies:
+        made.wait()
+    packed_out[...] = kept[z, 0, 0] + last[0] + last[1] + last[2]
+    sums_out[...] = ring[0] + ring[1] + ring[2] + ring[3]
+
+
+def total_call(packed, sums):
+    rows, wide = packed.shape[4], packed.shape[5]
+    held = pl.BlockSpec(memory_space=pltpu.VMEM)
+    return pl.pallas_call(
+        total_kernel,
+        out_shape=[jax.ShapeDtypeStruct((rows, wide), jnp.float32), jax.ShapeDtypeStruct(sums.shape, jnp.float32)],
+        in_specs=[held, held],
+        out_specs=[held, held],
+        scratch_shapes=[
+            pltpu.VMEM((ZS, 2, 2, rows, wide), jnp.float32),
+            pltpu.VMEM((ZS, 2, rows, wide), jnp.float32),
+            pltpu.VMEM((ZS, rows, wide), jnp.float32),
+            pltpu.VMEM((ZS - 1, rows, wide), jnp.float32),
+            pltpu.VMEM((ZS, 2, 2, rows, wide), jnp.float32),
+            pltpu.VMEM((6,) + sums.shape, jnp.float32),
+            pltpu.VMEM((ZS,) + sums.shape, jnp.float32),
+            pltpu.SemaphoreType.DMA((12,)),
+            pltpu.SemaphoreType.DMA((12,)),
+        ],
+        compiler_params=pltpu.CompilerParams(collective_id=3, has_side_effects=True, vmem_limit_bytes=LIMIT),
+        cost_estimate=pl.CostEstimate(flops=1000000, bytes_accessed=2_000_000, transcendentals=0),
+    )(packed, sums)
+
+
 def from_behind(block, axis, distance):
     devices = range(lax.axis_size(axis))
     route = [(i - distance, i) for i in devices if i - distance in devices]
@@ -662,12 +1373,12 @@
     chunks = length // GROUP
     square = (chunks, SPAN, DK)
     outs = [
-        (square, jnp.bfloat16),
-        (square, jnp.bfloat16),
         (square, jnp.float32),
-        (square, jnp.bfloat16),
         (square, jnp.float32),
-        ((chunks, GROUP, DK), jnp.bfloat16),
+        (square, jnp.float32),
+        (square, jnp.float32),
+        (square, jnp.float32),
+        ((chunks, GROUP, DK), jnp.float32),
         ((chunks, GROUP, DV), jnp.float32),
         ((DV, DK), jnp.float32),
     ]
@@ -711,8 +1422,8 @@
         [
             jax.ShapeDtypeStruct((length, H * DV), jnp.bfloat16),
             jax.ShapeDtypeStruct((length, H * DV), jnp.float32),
-            per_head((chunks, SPAN, DK), jnp.bfloat16),
-            per_head((chunks, SPAN, DK), jnp.bfloat16),
+            per_head((chunks, SPAN, DK)),
+            per_head((chunks, SPAN, DK)),
         ],
         [
             head_spec((chunks, 8, SPAN)), square, square, square, square, half, half,
@@ -732,7 +1443,7 @@
     return call(
         readout_back_kernel,
         [
-            jax.ShapeDtypeStruct((length, H * DV), jnp.bfloat16),
+            jax.ShapeDtypeStruct((length, H * DV), jnp.float32),
             jax.ShapeDtypeStruct((length, H * DV), jnp.bfloat16),
             per_head((chunks, SPAN, DK)),
             per_head((DV, DK)),
@@ -881,36 +1592,50 @@
     d_mlp_in = jnp.einsum("nf,df->nd", d_gate_low, gu_all, preferred_element_type=jnp.float32)
     d_hidden_norm, grad_norm_mlp = norm_mlp_back(d_mlp_in)
     d_hidden = d_result + d_hidden_norm
-    grad_gu = scatter_halves(grad_gu.astype(jnp.bfloat16))
-    grad_down = scatter_halves(grad_down.astype(jnp.bfloat16))
-
     d_mixer_low = d_hidden.astype(jnp.bfloat16)
     grad_out = jnp.einsum("nh,nd->hd", normed_out_low, d_mixer_low, preferred_element_type=jnp.float32)
-    grad_out = scatter_halves(grad_out.astype(jnp.bfloat16))
     d_normed_out = jnp.einsum("nd,hd->nh", d_mixer_low, out_all, preferred_element_type=jnp.float32)
-    d_mixed, d_out_gate, local, own_entry, gain_parts = readout_back_call(
-        vec, transfer, out_keys, mixed, projected, gain, d_normed_out, zero_state
-    )
+    if fast:
+        blocks = grad_down.astype(jnp.bfloat16).reshape(lax.axis_size("dp") * seqs, -1, width)
+        down_rows = blocks.shape[1]
+        blocks = jnp.pad(blocks, ((0, 0), (0, -down_rows % rows), (0, 0)))
+        backs = mixer_back_call(
+            vec, transfer, out_keys, mixed, projected, gain, d_normed_out, border, taps, masks, inverse, solved, entries,
+            normed_low.T.reshape(STACK + (rows, seg_len)),
+            grad_gu.astype(jnp.bfloat16).reshape(STACK + (rows, -1)),
+            blocks.reshape(STACK + (-1, width)),
+            grad_out.astype(jnp.bfloat16).reshape(STACK + (rows, -1)),
+        )
+        gain_parts, d_vec, tap_grads, d_projected = backs[0], backs[1], backs[2 : 2 + parts], backs[2 + parts]
+        grad_gu, grad_down, grad_out, grad_mix = backs[3 + parts :]
+        grad_down = grad_down.reshape(-1, width)[:down_rows]
+    else:
+        grad_gu = scatter_halves(grad_gu.astype(jnp.bfloat16))
+        grad_down = scatter_halves(grad_down.astype(jnp.bfloat16))
+        grad_out = scatter_halves(grad_out.astype(jnp.bfloat16))
+        d_mixed, d_out_gate, local, own_entry, gain_parts = readout_back_call(
+            vec, transfer, out_keys, mixed, projected, gain, d_normed_out, zero_state
+        )
+        exit_grad = zero_state
+        for turn in range(seqs - 1):
+            leaving = own_entry
+            if turn > 0:
+                leaving = leaving + jnp.einsum("hvl,hkl->hvk", exit_grad, device_transfer, precision=HIGHEST)
+            exit_grad = from_behind(leaving.astype(jnp.bfloat16), "seq", -1).astype(jnp.float32)
+        backs = backward_call(
+            projected, border, taps, masks, vec, transfer, inverse, solved, entries, d_mixed, local, exit_grad
+        )
+        d_columns, edges, tap_grads, d_vec = backs[:parts], backs[parts : 2 * parts], backs[2 * parts : 3 * parts], backs[-1]
+        edge = jnp.concatenate(edges, axis=1)
+        returned = from_behind(edge[9 - tap_count : 8].astype(jnp.bfloat16), "seq", -1).astype(jnp.float32)
+        fixed = (edge[17 - tap_count :] + returned).astype(jnp.bfloat16)
+        d_projected = jnp.concatenate(list(d_columns) + [d_out_gate], axis=1)
+        d_projected = lax.dynamic_update_slice(d_projected, fixed, (seg_len - tap_count + 1, 0))
+        grad_mix = jnp.einsum("nd,nc->dc", normed_low, d_projected, preferred_element_type=jnp.float32)
+        grad_mix = scatter_halves(grad_mix.astype(jnp.bfloat16))
     grad_norm_out = jnp.sum(gain_parts[:, 0, :], axis=0)
-    exit_grad = zero_state
-    for turn in range(seqs - 1):
-        leaving = own_entry
-        if turn > 0:
-            leaving = leaving + jnp.einsum("hvl,hkl->hvk", exit_grad, device_transfer, precision=HIGHEST)
-        exit_grad = from_behind(leaving.astype(jnp.bfloat16), "seq", -1).astype(jnp.float32)
-    backs = backward_call(
-        projected, border, taps, masks, vec, transfer, inverse, solved, entries, d_mixed, local, exit_grad
-    )
-    d_columns, edges, tap_grads, d_vec = backs[:parts], backs[parts : 2 * parts], backs[2 * parts : 3 * parts], backs[-1]
-    edge = jnp.concatenate(edges, axis=1)
-    returned = from_behind(edge[9 - tap_count : 8].astype(jnp.bfloat16), "seq", -1).astype(jnp.float32)
-    fixed = (edge[17 - tap_count :] + returned).astype(jnp.bfloat16)
-    d_projected = jnp.concatenate(list(d_columns) + [d_out_gate], axis=1)
-    d_projected = lax.dynamic_update_slice(d_projected, fixed, (seg_len - tap_count + 1, 0))
     d_gates_raw, grad_decay = vec_back(d_vec)
     d_gates_low = d_gates_raw.astype(jnp.bfloat16)
-    grad_mix = jnp.einsum("nd,nc->dc", normed_low, d_projected, preferred_element_type=jnp.float32)
-    grad_mix = scatter_halves(grad_mix.astype(jnp.bfloat16))
     grad_small = jnp.einsum("nd,nc->dc", normed_low, d_gates_low, preferred_element_type=jnp.float32)
     d_normed = jnp.einsum("nc,dc->nd", d_projected, mix_all, preferred_element_type=jnp.float32)
     d_normed = d_normed + jnp.einsum("nc,dc->nd", d_gates_low, small_all, preferred_element_type=jnp.float32)
@@ -922,13 +1647,18 @@
     conv_rows = grad_conv.reshape(tap_count, devices, -1).transpose(1, 0, 2).reshape(width, -1)
     packed = jnp.concatenate([grad_small, grad_norm_in[:, None], grad_norm_mlp[:, None], conv_rows], axis=1)
     packed = jnp.concatenate([packed, jnp.zeros((width, 128 - packed.shape[1]), jnp.float32)], axis=1)
-    packed = scatter_sum(packed, bit_orders()[0])
+    if fast:
+        sums = jnp.stack([grad_norm_out, jnp.pad(grad_decay, (0, DV - H))] + [jnp.zeros((DV,), jnp.float32)] * 6)
+        packed, sums = total_call(packed.reshape(STACK + (rows, -1)), sums)
+        grad_norm_out, grad_decay = sums[0], sums[1, :H]
+    else:
+        packed = scatter_sum(packed, bit_orders()[0])
+        sums = total_sum(jnp.concatenate([grad_norm_out, grad_decay]))
+        grad_norm_out, grad_decay = sums[:DV], sums[DV:]
     smalls = grad_small.shape[1]
     grad_small = packed[:, :smalls]
     grad_norm_in, grad_norm_mlp = packed[:, smalls], packed[:, smalls + 1]
     grad_conv = packed[:, smalls + 2 : smalls + 2 + conv_rows.shape[1]].reshape(tap_count, -1)
-    sums = total_sum(jnp.concatenate([grad_norm_out, grad_decay]))
-    grad_norm_out, grad_decay = sums[:DV], sums[DV:]
     return (
         block_output, input_grad, grad_norm_in, grad_mix, grad_small, grad_conv, grad_decay,
         grad_norm_out, grad_out, grad_norm_mlp, grad_gu, grad_down,

time: 789 us -> 579 us (0.73)
  waiting for transfers between devices: 190 us -> 3.47 us
  Pallas kernels: 267 us -> 411 us
  starting transfers between devices: 72.1 us -> 6.21 us
  local copies, waits for them, and re-layouts: 96.4 us -> 34.7 us
  other arithmetic: 43.8 us -> 13.4 us
  matrix products: 96.7 us -> 88.3 us
    ppermute x50 -> x0, waiting for transfers between devices: 184 us -> none  [exchange(): return lax.ppermute(block, axis, route)]
    pallas_call x2, Pallas kernels: 92.5 us -> 224 us  [the longest x1 209 us: mixer_back_call(): pl.pallas_call(kernel, grid=(2 * H + 1,), out_shape=out_shape, in_specs=i...]
    ppermute x50 -> x0, starting transfers between devices: 63.1 us -> none  [exchange(): return lax.ppermute(block, axis, route)]
    dynamic_slice x16 -> x0, local copies, waits for them, and re-layouts: 27.7 us -> none  [the longest x8 16 us: scatter_sum(): kept = lax.dynamic_index_in_dim(part, mine, place, keepdims=False)]
    add x50 -> x0, other arithmetic: 26.3 us -> none  [the longest x45 26.2 us: scatter_sum(): part = kept.astype(jnp.float32) + got.astype(jnp.float32)]
    slice x7 -> x1, local copies, waits for them, and re-layouts: 18.3 us -> 0.76 us  [on_device(): grad_down = grad_down.reshape(-1, width)[:down_rows]]
    unnamed x187 -> x75, local copies, waits for them, and re-layouts: 22.9 us -> 8.46 us
    dot_general x1, matrix products: 12.6 us -> 0.47 us  [on_device(): jnp.einsum('nd,nc->dc', normed_low, d_gates_low, preferred_element_type=j...]
  transfers between devices with their start and end apart: 56 -> 4, of which waited for: 34 -> 1; matrix products, arithmetic and copies ran while one was open for 22% -> 6% of each run, Pallas kernels for 32% -> 33%
where the time goes in v2:
time: 579 us; the launch traced here: 572 us
  Pallas kernels  411 us (71%)
  matrix products  88.3 us (15%)
  local copies, waits for them, and re-layouts  34.7 us (6%)
  between operations  15.2 us (3%)
  other arithmetic  13.4 us (2%)
  starting transfers between devices  6.21 us (1%)
    pallas_call x1, Pallas kernels, mixer_back_call(): pl.pallas_call(kernel, grid=(2 * H + 1,), out_shape=out_shape, in_specs=i...  209 us
    pallas_call x1, Pallas kernels, gather_project_call(): pl.pallas_call(gather_project_kernel, out_shape=[jax.ShapeDtypeStruct(ful...  115 us
    pallas_call x1, Pallas kernels, forward_call(): call(forward_kernel, [per_head(*out) for out in outs], conv_specs(length)...  54.4 us
    pallas_call x1, Pallas kernels, readout_call(): call(readout_kernel, [jax.ShapeDtypeStruct((length, H * DV), jnp.bfloat16...  17.9 us
    pallas_call x1, Pallas kernels, total_call(): pl.pallas_call(total_kernel, out_shape=[jax.ShapeDtypeStruct((rows, wide)...  14.5 us
    dot_general x1, matrix products, on_device(): jnp.einsum('nc,dc->nd', d_projected, mix_all, preferred_element_type=jnp....  14.2 us
    dot_general x1, matrix products, on_device(): jnp.einsum('nf,df->nd', d_gate_low, gu_all, preferred_element_type=jnp.fl...  13.9 us
    dot_general x1, matrix products, on_device(): jnp.einsum('nd,nf->df', mlp_in_low, d_gate_low, preferred_element_type=jn...  13.6 us
  transfers between devices with their start and end apart: 4, of which 1 were waited for; matrix products, arithmetic and copies ran while one was open for 6% of the time, Pallas kernels for 33%

profile of v2, /device:TPU:0, one launch (start us, length us, event | category | flops | bytes accessed | tf_op | source)
XLA Modules:
  0.0 572.5 jit_solution(15491796106461278576)
XLA Ops:
  8.7 0.8 reshape.247
  9.7 0.8 copy.183
  10.5 0.8 copy.184
  11.2 0.8 copy.185
  12.1 1.2 copy-done.2
  13.3 1.0 copy-done.10
  14.3 0.8 copy-done.11
  15.1 115.2 %shard_map.220 = (bf16[4,2,2,2,32,6144]{5,4,3,2,1,0:T(8,128)(2,1)}, bf16[4,2,2,2,32,1024]{5,4,3,2,1,0:T(8,128)(2,1)}, bf16[4,2,2,2,32,128]{5,4,3,2,1,0:T(8,128)(...) custom-call(bf16[512,1024]{1,0:T(8,128)(2,1)S(1)} %bitcast.151, ...), custom_call_target="tpu_custom_call" | custom-call | flops 6442450944 | bytes 60000000 | tf_op jit(solution)/shard_map/pallas_call | solution.py:523
  130.3 0.9 slice.91
  131.3 3.8 collective-permute-start
  137.6 2.3 convert_element_type.109
  139.9 1.8 copy.198
  141.9 0.7 pad_add_fusion
  143.6 1.0 slice_convert_fusion
  145.1 54.4 %shard_map.221 = (f32[8,8,128,128]{3,2,1,0:T(8,128)}, f32[8,8,128,128]{3,2,1,0:T(8,128)}, f32[8,8,128,128]{3,2,1,0:T(8,128)}, f32[8,8,128,128]{3,2,1,0:T(8,128)}...) custom-call(f32[512,6144]{1,0:T(8,128)} %get-tuple-element.45.q_in.k, ...), custom_call_target="tpu_custom_call" | custom-call | flops 21474836480 | bytes 33554432 | tf_op jit(solution)/shard_map/pallas_call | solution.py:1386
  199.5 0.7 convert_element_type.112
  200.2 2.4 collective-permute-start.1
  202.9 1.2 copy.226
  204.2 1.3 copy.200
  205.8 2.1 collective-permute-done.1
  207.9 1.0 convert_element_type.113.entry_ref
  208.9 17.9 %shard_map.222 = (bf16[512,1024]{1,0:T(8,128)(2,1)S(1)}, f32[512,1024]{1,0:T(8,128)S(1)}, f32[8,8,128,128]{3,2,1,0:T(8,128)}, f32[8,8,128,128]{3,2,1,0:T(8,128)}) custom-call(f32[8,8,8,128]{3,2,1,0:T(8,128)S(1)} %stack.46.vec_ref, f32[8,8,128,128]{3,2,1,0:T(8,128)} %get-tuple-element.47.w_in, f32[8,8,128,128]{3,2,1,0:T(8,128)} %get-tuple-element.48.u_in, ...), custom_call_target="tpu_custom_call" | custom-call | flops 4294967296 | bytes 33554432 | tf_op jit(solution)/shard_map/pallas_call | solution.py:1420
  226.8 2.6 multiply_reduce_fusion.2
  229.5 12.3 %fusion.58 = f32[512,5632]{1,0:T(8,128)} fusion(bf16[1024,5632]{1,0:T(8,128)(2,1)} %all-gather.3.cloned.1.call-done, f32[512,1024]{1,0:T(8,128)} %get-tuple-element.174, f32[1024]{0:T(1024)S(1)} %bitcast.161, f32[512]{0:T(512)S(1)} %fusion.48), kind=kOutput, calls=%fused_computation.139 | convolution fusion | flops 5907152896 | bytes 25171968 | tf_op jit(solution)/shard_map/dot_general | solution.py:1579
  241.8 13.1 %fusion.16 = (f32[512,2816]{1,0:T(8,128)}, f32[512,2816]{1,0:T(8,128)}, bf16[512,2816]{1,0:T(8,128)(2,1)}) fusion(f32[512,5632]{1,0:T(8,128)} %fusion.58, bf16[2816,1024]{1,0:T(8,128)(2,1)} %all-gather.5.cloned.1.call-done, bf16[1,512,1024]{2,1,0:T(8,128)(2,1)} %param.25), kind=kOutput, calls=%fused_computation.40 | convolution fusion | flops 2972975104 | bytes 32768000 | tf_op jit(solution)/shard_map/nd,fd->nf/dot_general | solution.py:1588
  255.0 13.6 %convolution_convert_fusion = bf16[1024,5632]{1,0:T(8,128)(2,1)} fusion(f32[512,2816]{1,0:T(8,128)} %get-tuple-element.155, f32[512,2816]{1,0:T(8,128)} %get-tuple-element.154, f32[512,1024]{1,0:T(8,128)S(1)} %copy-done.13, f32[1024]{0:T(1024)S(1)} %bitcast.162, f32[512]{0:T(512)S(1)} %fusion.48), kind=kOutput, calls=%fused_computation.1 | convolution fusion | flops 5918687232 | bytes 25171968 | tf_op jit(solution)/shard_map/nd,nf->df/dot_general | solution.py:1591
  268.5 13.9 %multiply_reduce_fusion = (f32[1024]{0:T(1024)S(1)}, f32[512]{0:T(512)S(1)}, f32[512,1024]{1,0:T(8,128)}) fusion(f32[512,1024]{1,0:T(8,128)} %get-tuple-element.174, f32[512]{0:T(512)S(1)} %fusion.48, f32[1024]{0:T(1024)S(1)} %bitcast.163, bf16[1024,5632]{1,0:T(8,128)(2,1)} %all-gather.3.cloned.1.call-done, f32[512,2816]{1,0:T(8,128)} %get-tuple-element.155, ...), kind=kOutput, calls=%fused_computation.23 | convolution fusion | flops 5914491392 | bytes 27275264 | tf_op jit(solution)/shard_map/nf,df->nd/dot_general | solution.py:1592
  282.5 3.1 fusion.3
  285.6 2.7 convolution_convert_fusion.2
  288.3 2.7 fusion.18.d_gated_ref
  291.0 3.4 convolution_convert_fusion.1
  294.4 3.3 pad.28
  297.7 209.2 %shard_map.223 = (f32[8,8,128]{2,1,0:T(8,128)}, f32[8,8,8,128]{3,2,1,0:T(8,128)}, f32[8,1024]{1,0:T(8,128)}, f32[8,1024]{1,0:T(8,128)}, f32[8,1024]{1,0:T(8,128)...) custom-call(f32[8,8,8,128]{3,2,1,0:T(8,128)} %copy-done.5, ...), custom_call_target="tpu_custom_call" | custom-call | flops 15032385536 | bytes 100000000 | tf_op jit(solution)/shard_map/pallas_call | solution.py:1156
  506.9 1.0 copy.201
  507.9 1.0 slice_reduce_fusion
  511.1 1.8 fusion.24
  512.9 0.8 slice_reduce_fusion.3
  514.3 14.2 %fusion.9 = (f32[1024]{0:T(1024)S(1)}, f32[512]{0:T(512)S(1)}, f32[512,1024]{1,0:T(8,128)}) fusion(f32[512]{0:T(512)S(1)} %fusion.49, bf16[1,512,1024]{2,1,0:T(8,128)(2,1)S(1)} %copy-done.3, f32[1024]{0:T(1024)S(1)} %bitcast.178, f32[512,1024]{1,0:T(8,128)} %fusion.24, bf16[512,6144]{1,0:T(8,128)(2,1)} %get-tuple-element.61, bf16[1024,6144]{1,0:T(8,128)(2,1)} %bitcast.185), kind=kOutput, calls=%fused_computation.22 | convolution fusion | flops 6446643712 | bytes 24129536 | tf_op jit(solution)/shard_map/nc,dc->nd/dot_general | solution.py:1640
  528.5 1.1 concatenate.60
  529.6 1.1 concatenate.61
  530.8 0.9 broadcast_in_dim.76
  531.7 1.9 concatenate.59.packed_ref
  533.5 14.5 %shard_map.224 = (f32[32,128]{1,0:T(8,128)S(1)}, f32[8,128]{1,0:T(8,128)S(1)}) custom-call(f32[4,2,2,2,32,128]{5,4,3,2,1,0:T(8,128)S(1)} %concatenate.59.packed_ref, f32[8,128]{1,0:T(8,128)S(1)} %maximum_maximum_fusion.sums_ref), custom_call_target="tpu_custom_call" | custom-call | flops 1000000 | bytes 2000000 | tf_op jit(solution)/shard_map/pallas_call | solution.py:1221
  551.2 0.8 slice.118
  552.0 3.9 fusion.11
  555.9 6.8 %fusion.10 = bf16[1,512,1024]{2,1,0:T(8,128)(2,1)} fusion(f32[512,1024]{1,0:T(8,128)S(1)} %copy-done.14, bf16[512,2816]{1,0:T(8,128)(2,1)S(1)} %copy-done.31, bf16[2816,1024]{1,0:T(8,128)(2,1)} %all-gather.5.cloned.1.call-done), kind=kOutput, calls=%fused_computation.30 | convolution fusion | flops 2953838592 | bytes 11796480 | tf_op jit(solution)/shard_map/dot_general | solution.py:1582
  562.8 0.9 copy.252
  564.3 0.9 copy.254
  (155 shorter events, 12.9 us)
Async XLA Ops:
  7.2 222.3 %all-gather.3.cloned.1.call-start = ((), (), s32[]{:S(2)}) async-start(), calls=%async_computation | async-start | bytes 11894784 | tf_op jit(solution)/shard_map/all_gather | solution.py:1504
  7.9 233.9 %all-gather.5.cloned.1.call-start = ((), (), s32[]{:S(2)}) async-start(), calls=%async_computation.1 | async-start | bytes 5947392 | tf_op jit(solution)/shard_map/all_gather | solution.py:1504
  12.1 1.2 copy-start.2
  13.3 1.0 copy-start.10
  14.3 0.8 copy-start.11
  15.1 119.9 %copy-start.25 = (s32[1,6]{1,0:T(1,128)S(1)}, s32[1,6]{1,0:T(1,128)}, u32[]{:S(2)}) copy-start(s32[1,6]{1,0:T(1,128)} %param.14) | copy-start | bytes 76
  15.1 120.7 %copy-start.27 = (bf16[8]{0:T(256)(128)(2,1)S(1)}, bf16[8]{0:T(256)(128)(2,1)}, u32[]{:S(2)}) copy-start(bf16[8]{0:T(256)(128)(2,1)} %param.19) | copy-start | bytes 52
  131.3 13.4 %collective-permute-start = (f32[3,5120]{1,0:T(4,128)S(1)}, f32[3,5120]{1,0:T(4,128)S(1)}, u32[]{:S(2)}, u32[]{:S(2)}) collective-permute-start(f32[3,5120]{1,0:T(4,128)S(1)} %slice.91), channel_id=1, source_target_pairs={{0,1},{2,3},{4,5},{6,7},{8,9},{10,11},{12,13},{14,15},{16,17},{18,... | collective-permute-start | bytes 184328 | tf_op jit(solution)/shard_map/ppermute | solution.py:1245
  143.6 65.3 %copy-start.5 = (f32[8,8,8,128]{3,2,1,0:T(8,128)}, f32[8,8,8,128]{3,2,1,0:T(8,128)S(1)}, u32[]{:S(2)}) copy-start(f32[8,8,8,128]{3,2,1,0:T(8,128)S(1)} %stack.46.vec_ref) | copy-start | bytes 786436
  144.6 54.8 %copy-start = (f32[8,5120]{1,0:T(8,128)}, f32[8,5120]{1,0:T(8,128)S(1)}, u32[]{:S(2)}) copy-start(f32[8,5120]{1,0:T(8,128)S(1)} %pad_convert_fusion.tq.tk0.tk1.tv0.tv1) | copy-start | bytes 491524
  144.7 54.8 %copy-start.1 = (f32[8,5120]{1,0:T(8,128)}, f32[8,5120]{1,0:T(8,128)S(1)}, u32[]{:S(2)}) copy-start(f32[8,5120]{1,0:T(8,128)S(1)} %concatenate.51.bq.bk0.bk1.bv0.bv1) | copy-start | bytes 491524
  145.0 54.5 %copy-start.4 = (f32[3,512,128]{2,1,0:T(8,128)}, f32[3,512,128]{2,1,0:T(8,128)S(1)}, u32[]{:S(2)}) copy-start(f32[3,512,128]{2,1,0:T(8,128)S(1)} %broadcast_in_dim.71.mask_ref) | copy-start | bytes 2359300
  145.0 57.6 %copy-start.3 = (bf16[1,512,1024]{2,1,0:T(8,128)(2,1)S(1)}, bf16[1,512,1024]{2,1,0:T(8,128)(2,1)}, u32[]{:S(2)}) copy-start(bf16[1,512,1024]{2,1,0:T(8,128)(2,1)} %param.13) | copy-start | bytes 3145732
  200.2 7.7 %collective-permute-start.1 = (bf16[8,128,128]{2,1,0:T(8,128)(2,1)}, bf16[8,128,128]{2,1,0:T(8,128)(2,1)}, u32[]{:S(2)}, u32[]{:S(2)}) collective-permute-start(bf16[8,128,128]{2,1,0:T(8,128)(2,1)} %convert_element_type.112), channel_id=1, source_target_pairs={{0,1},{2,3},{4,5},{6,7},{8,9},{10,11},{12,13},{14,15},{16,17},{18,... | collective-permute-start | bytes 786440 | tf_op jit(solution)/shard_map/ppermute | solution.py:1245
  202.9 6.0 %copy-start.26 = (bf16[128]{0:T(256)(128)(2,1)S(1)}, bf16[128]{0:T(256)(128)(2,1)}, u32[]{:S(2)}) copy-start(bf16[128]{0:T(256)(128)(2,1)} %param.20) | copy-start | bytes 772
  208.9 17.9 %copy-start.7 = (f32[8,128]{1,0:T(8,128)}, f32[8,128]{1,0:T(8,128)S(1)}, u32[]{:S(2)}) copy-start(f32[8,128]{1,0:T(8,128)S(1)} %broadcast_in_dim.73.gain_ref) | copy-start | bytes 12292
  208.9 17.9 %copy-start.28 = (bf16[4,2,2,2,32,1024]{5,4,3,2,1,0:T(8,128)(2,1)S(1)}, bf16[4,2,2,2,32,1024]{5,4,3,2,1,0:T(8,128)(2,1)}, u32[]{:S(2)}) copy-start(bf16[4,2,2,2,32,1024]{5,4,3,2,1,0:T(8,128)(2,1)} %get-tuple-element.55) | copy-start | bytes 6291460
  226.8 2.7 copy-start.6
  226.8 2.6 copy-start.8
  241.8 13.1 %copy-start.13 = (f32[512,1024]{1,0:T(8,128)S(1)}, f32[512,1024]{1,0:T(8,128)}, u32[]{:S(2)}) copy-start(f32[512,1024]{1,0:T(8,128)} %get-tuple-element.174) | copy-start | bytes 6291460
  282.5 3.1 copy-start.9
  285.6 2.7 copy-start.12
  285.6 2.7 copy-start.29
  288.3 2.7 copy-start.15
  288.3 2.7 copy-start.30
  510.6 3.1 copy-start.24
  510.6 3.1 copy-start.23
  510.6 3.1 copy-start.22
  510.6 3.2 copy-start.21
  510.6 3.2 copy-start.20
  530.8 20.4 %copy-start.18 = (f32[3,32,1024]{2,1,0:T(8,128)S(1)}, f32[3,32,1024]{2,1,0:T(8,128)}, u32[]{:S(2)}) copy-start(f32[3,32,1024]{2,1,0:T(8,128)} %get-tuple-element.75) | copy-start | bytes 1179652
  552.0 3.9 copy-start.14
  552.0 3.9 copy-start.31
  555.9 6.8 %copy-start.16 = (f32[32,6144]{1,0:T(8,128)S(1)}, f32[32,6144]{1,0:T(8,128)}, u32[]{:S(2)}) copy-start(f32[32,6144]{1,0:T(8,128)} %get-tuple-element.194) | copy-start | bytes 2359300
  555.9 7.7 %copy-start.19 = (f32[32,1024]{1,0:T(8,128)S(1)}, f32[32,1024]{1,0:T(8,128)}, u32[]{:S(2)}) copy-start(f32[32,1024]{1,0:T(8,128)} %get-tuple-element.199) | copy-start | bytes 393220
  562.8 1.5 copy-start.17
Sparse Core Ops, SparseCore 0:
  10.9 126.7 all-gather.2
  140.6 67.2 all-gather.4

commit v3 on v2

--- a/solution.py
+++ b/solution.py
@@ -70,6 +70,16 @@
     return strict, pair, levels, eye
 
 
+TOGETHER = 16
+
+
+def together(runs):
+    for first in range(0, len(runs), TOGETHER):
+        group = runs[first : first + TOGETHER]
+        while group:
+            group = [run for run in group if next(run, "done") != "done"]
+
+
 def unit_inverses(lowers, pair, levels, eye):
     inverses = [eye - jnp.where(pair, lower, 0.0) for lower in lowers]
     for level in levels:
@@ -83,13 +93,13 @@
     return values * sig, sig
 
 
-def conv_block(channel_ref, border_ref, tap_ref, mask_ref, ext_ref):
-    length = channel_ref.shape[0]
-    ext_ref[0:8, :] = border_ref[...]
-    ext_ref[8 : 8 + length, :] = channel_ref[...]
-    summed = channel_ref[...] * tap_ref[0:1, :]
+def conv_block(channels, border, taps, mask_ref, ext_ref):
+    length = channels.shape[0]
+    ext_ref[0:8, :] = border
+    ext_ref[8 : 8 + length, :] = channels
+    summed = channels * taps[0:1, :]
     for tap in range(1, 4):
-        summed = summed + ext_ref[8 - tap : 8 - tap + length, :] * tap_ref[tap : tap + 1, :] * mask_ref[tap - 1]
+        summed = summed + ext_ref[8 - tap : 8 - tap + length, :] * taps[tap : tap + 1, :] * mask_ref[tap - 1].astype(jnp.float32)
     return summed
 
 
@@ -128,7 +138,7 @@
     for channel, border, tap in (
         (q_in, bq, tq), (k0_in, bk0, tk0), (k1_in, bk1, tk1), (v0_in, bv0, tv0), (v1_in, bv1, tv1),
     ):
-        conv.append(silu_pair(conv_block(channel, border, tap, mask_ref, ext_ref))[0])
+        conv.append(silu_pair(conv_block(channel[...], border[...], tap[...], mask_ref, ext_ref))[0])
     q_ref[...] = unit_rows(conv[0])[0] * DK ** (-0.5)
     for step in range(NH):
         k_ref[step] = unit_rows(conv[1 + step])[0]
@@ -243,7 +253,7 @@
     channels = (q_in, k0_in, k1_in, v0_in, v1_in)
     taps = (tq, tk0, tk1, tv0, tv1)
     for part, (channel, border, tap) in enumerate(zip(channels, (bq, bk0, bk1, bv0, bv1), taps)):
-        pre = conv_block(channel, border, tap, mask_ref, ext_ref.at[part])
+        pre = conv_block(channel[...], border[...], tap[...], mask_ref, ext_ref.at[part])
         pre_ref[part] = pre
         value = silu_pair(pre)[0]
         if part == 0:
@@ -449,68 +459,197 @@
     return lambda z, x, core, y: ref.at[z, x, core, y, :, pl.ds(first, width)]
 
 
+class Spread:
+    def __init__(self, source, target, lane, width, sems, first=0):
+        self.first = first
+        self.source, self.target, self.lane, self.width = source, target, lane, width
+        self.send_sem, self.recv_sem, self.local_sem = sems
+        self.place, self.peers = place(), peers()
+
+    def here(self, index):
+        return pl.ds(pl.multiple_of((2 * (index - self.first) + self.lane) * self.width, self.width), self.width)
+
+    def block(self, index, stage):
+        z, x, core, y = self.place
+        every = slice(None)
+        here = self.here(index)
+        if stage == 0:
+            return self.target.at[z, x, core, y, :, here]
+        if stage == 1:
+            return self.target.at[:, x, core, y, :, here]
+        if stage == 2:
+            if self.lane == 0:
+                return self.target.at[:, :, core, y, :, here]
+            return self.target.at[:, x, core, :, :, here]
+        return self.target.at[:, :, core, :, :, here]
+
+    def copies(self, index, stage):
+        near, far = (ZS - 1, ZS) if self.lane == 0 else (ZS, ZS - 1)
+        slots = (0, 1, 2) if stage == 0 else ((near,), (far,), (ZS + 1,))[stage - 1]
+        target = self.block(index, stage)
+        source = self.source.at[:, self.here(index)] if stage == 0 else target
+        ring = lax.rem(index, RING)
+        return [
+            pltpu.make_async_remote_copy(
+                src_ref=source, dst_ref=target,
+                send_sem=self.send_sem.at[self.lane, slot, ring], recv_sem=self.recv_sem.at[self.lane, slot, ring],
+                device_id=self.peers[slot], device_id_type=MESH,
+            )
+            for slot in slots
+        ]
+
+    def own(self, index):
+        return pltpu.make_async_copy(
+            self.source.at[:, self.here(index)], self.block(index, 0), self.local_sem.at[self.lane, lax.rem(index, RING)]
+        )
+
+    def step(self, index, stage):
+        if stage > 0:
+            for copy in self.copies(index, stage - 1):
+                copy.wait_recv()
+                copy.wait_send()
+        if stage == 1:
+            self.own(index).wait()
+        if stage == 0:
+            self.own(index).start()
+        if stage < SPREAD_STAGES - 1:
+            for copy in self.copies(index, stage):
+                copy.start()
+
+
+SPREAD_STAGES = 5
+SPREAD_TICKS = 2
+SPREAD_FILL = (SPREAD_STAGES - 1) * SPREAD_TICKS
+FINE = 256
+
+
 def gather_project_kernel(
     x_ref, small_in, mix_in, out_in,
-    mix_out, out_out, small_out, normed_ref, projected_out, gates_ref,
+    mix_out, out_out, small_out, normed_ref, normed_t_ref, channels_out, gate_out, gates_ref, border_ref,
     mix_ref, small_ref, slab_ref,
-    send, recv, local, store_mix, store_slab, store_small,
+    small_send, small_recv, small_local, send, recv, local, store_mix, store_slab, store_small, edge_send, edge_recv,
 ):
+    parts, heads = channels_out.shape[0], channels_out.shape[1]
+    length = x_ref.shape[0]
+    block = 2 * FINE
+    count = mix_in.shape[1] // block
+    more = out_in.shape[1] // block
+    per_part, across = heads * DK // block, block // DK
+    z, x, core, y = place()
     sems = (send, recv, local)
-    chunk = 1024
-    half = chunk // 2
-    items = []
-
-    def add(source, first, width, ref, x_first):
-        items.append(
-            Gather(source.at[:, pl.ds(first, width)], columns_of(ref, first, width), x_first, sems, len(items))
+    small = Gather(small_in, lambda z, x, core, y: small_ref.at[z, x, core, y], True, (small_send, small_recv, small_local), 0)
+    mix_lanes = [Spread(mix_in, mix_ref, lane, FINE, sems) for lane in range(2)]
+    out_lanes = [Spread(out_in, out_out, lane, FINE, sems, count) for lane in range(2)]
+
+    def here(index):
+        return pl.ds(pl.multiple_of(index * block, block), block)
+
+    def slab_copies(index):
+        slot, first = lax.rem(index, 2), lax.rem(index, per_part) * across
+        return [
+            [
+                pltpu.make_async_copy(
+                    slab_ref.at[slot, :, half * DK : (half + 1) * DK], target.at[first + half], store_slab.at[slot, half]
+                )
+                for half in range(across)
+            ]
+            for target in (channels_out.at[jnp.minimum(index // per_part, parts - 1)], gate_out)
+        ]
+
+    def edge(index):
+        return pltpu.make_async_remote_copy(
+            src_ref=slab_ref.at[lax.rem(index, 2), length - 8 :, :], dst_ref=border_ref.at[:, here(index)],
+            send_sem=edge_send.at[lax.rem(index, 2)], recv_sem=edge_recv.at[index],
+            device_id=device_at(z, x, core, 1 - y), device_id_type=MESH,
         )
-        return items[-1]
-
-    ticks = []
-    chunks = mix_in.shape[1] // chunk
-    small = add(small_in, 0, small_in.shape[1], small_ref, True)
-    for index in range(chunks):
-        ticks.append([add(mix_in, index * chunk + part * half, half, mix_ref, part == 0) for part in range(2)])
-    ticks.append([add(out_in, part * half, half, out_out, part == 0) for part in range(2)])
-    ticks[0].insert(0, small)
+
+    def kept(index):
+        return pltpu.make_async_copy(
+            mix_ref.at[:, :, :, :, :, here(index)], mix_out.at[:, :, :, :, :, here(index)], store_mix.at[lax.rem(index, 2)]
+        )
+
+    def release(index):
+        for copy in slab_copies(index)[0]:
+            copy.wait()
+        kept(index).wait()
+
+        @pl.when(index < parts * per_part)
+        def _():
+            edge(index).wait_send()
+
+    def project(index):
+        @pl.when(index >= 2)
+        def _():
+            release(index - 2)
+
+        kept(index).start()
+        weights = mix_ref[:, :, :, :, :, here(index)].reshape(-1, block)
+        slab_ref[lax.rem(index, 2)] = mm(normed_ref[...], weights)
+        channels, gates = slab_copies(index)
+
+        @pl.when(index < parts * per_part)
+        def _():
+            for copy in channels:
+                copy.start()
+            edge(index).start()
+
+        @pl.when(index >= parts * per_part)
+        def _():
+            for copy in gates:
+                copy.start()
+
+    def tick(number):
+        for stage in reversed(range(SPREAD_STAGES)):
+            index = number - stage * SPREAD_TICKS
+
+            @pl.when((index >= 0) & (index < count))
+            def _():
+                for lane in mix_lanes:
+                    lane.step(index, stage)
+
+            @pl.when((index >= count) & (index < count + more))
+            def _():
+                for lane in out_lanes:
+                    lane.step(index, stage)
+
+        @pl.when((number >= SPREAD_FILL) & (number < count + SPREAD_FILL))
+        def _():
+            project(number - SPREAD_FILL)
+
     meet(peers())
-    steps = (Gather.begin, Gather.second, Gather.third, Gather.fourth, Gather.finish)
-    values = x_ref[...].astype(jnp.float32)
-    scaled = values * lax.rsqrt(jnp.mean(values * values, axis=1, keepdims=True) + EPSILON)
-    stores = []
-    for tick in range(len(ticks) + len(steps) - 1):
-        for step, action in reversed(list(enumerate(steps))):
-            if 0 <= tick - step < len(ticks):
-                for item in ticks[tick - step]:
-                    action(item)
-        done = tick - len(steps) + 1
-        if done == 0:
-            smalls = small_ref[...].reshape(-1, small_in.shape[1])
-            gain = jnp.transpose(smalls.astype(jnp.float32))[24:25, :]
-            normed_ref[...] = (scaled * gain).astype(jnp.bfloat16)
-            gates_ref[...] = mm(normed_ref[...], smalls)
-            stores.append(pltpu.make_async_copy(small_ref, small_out, store_small))
-            stores[-1].start()
-        if 0 <= done < chunks:
-            here = pl.ds(done * chunk, chunk)
-            keep = pltpu.make_async_copy(
-                mix_ref.at[:, :, :, :, :, here], mix_out.at[:, :, :, :, :, here], store_mix.at[done]
-            )
-            keep.start()
-            stores.append(keep)
-            weights = mix_ref[:, :, :, :, :, done * chunk : (done + 1) * chunk].reshape(-1, chunk)
-            slab = done % 2
-            if done >= 2:
-                slab_stores[done - 2].wait()
-            else:
-                slab_stores = [] if done == 0 else slab_stores
-            slab_ref[slab] = mm(normed_ref[...], weights)
-            slab_stores.append(
-                pltpu.make_async_copy(slab_ref.at[slab], projected_out.at[:, here], store_slab.at[slab])
-            )
-            slab_stores[-1].start()
-    for store in stores + slab_stores[-2:]:
-        store.wait()
+    small.begin()
+    for number in range(SPREAD_FILL):
+        tick(number)
+        if number == 0:
+            values = x_ref[...].astype(jnp.float32)
+            scaled = values * lax.rsqrt(jnp.mean(values * values, axis=1, keepdims=True) + EPSILON)
+        if number % SPREAD_TICKS == SPREAD_TICKS - 1:
+            (small.second, small.third, small.fourth, small.finish)[number // SPREAD_TICKS]()
+    smalls = small_ref[...].reshape(-1, small_in.shape[1])
+    gain = jnp.transpose(smalls.astype(jnp.float32))[24:25, :]
+    normed = (scaled * gain).astype(jnp.bfloat16)
+    normed_ref[...] = normed
+    keep_small = pltpu.make_async_copy(small_ref, small_out, store_small)
+    keep_small.start()
+
+    def loop(number, carry):
+        tick(number)
+        return carry
+
+    lax.fori_loop(SPREAD_FILL, 2 * SPREAD_FILL, loop, 0)
+    gates_ref[...] = mm(normed_ref[...], smalls)
+    flipped = jnp.transpose(normed_ref[...].astype(jnp.float32)).astype(jnp.bfloat16)
+    normed_t_ref[...] = flipped.reshape(normed_t_ref.shape)
+    lax.fori_loop(2 * SPREAD_FILL, count + more + SPREAD_FILL, loop, 0)
+    release(count - 2)
+    release(count - 1)
+    keep_small.wait()
+
+    def last(index, carry):
+        edge(index).wait_recv()
+        return carry
+
+    lax.fori_loop(0, parts * per_part, last, 0)
 
 
 def gather_project_call(x, small, mix, out):
@@ -518,8 +657,9 @@
     rows, width = mix.shape
     everywhere = pl.BlockSpec(memory_space=pl.ANY)
     held = pl.BlockSpec(memory_space=pltpu.VMEM)
-    items = 3 + 2 * (width // 1024)
     full = STACK + (rows,)
+    block = 2 * FINE
+    parts = width // (H * DK) - 1
     outs = pl.pallas_call(
         gather_project_kernel,
         out_shape=[
@@ -527,26 +667,266 @@
             jax.ShapeDtypeStruct(full + (out.shape[1],), jnp.bfloat16),
             jax.ShapeDtypeStruct(full + (small.shape[1],), jnp.bfloat16),
             jax.ShapeDtypeStruct(x.shape, jnp.bfloat16),
-            jax.ShapeDtypeStruct((length, width), jnp.float32),
+            jax.ShapeDtypeStruct(full + (length,), jnp.bfloat16),
+            jax.ShapeDtypeStruct((parts, H, length, DK), jnp.float32),
+            jax.ShapeDtypeStruct((H, length, DK), jnp.float32),
             jax.ShapeDtypeStruct((length, small.shape[1]), jnp.float32),
+            jax.ShapeDtypeStruct((8, parts * H * DK), jnp.float32),
         ],
         in_specs=[held, everywhere, everywhere, everywhere],
-        out_specs=[everywhere, everywhere, everywhere, held, everywhere, held],
+        out_specs=[everywhere, everywhere, everywhere, held, held, everywhere, everywhere, held, held],
         scratch_shapes=[
             pltpu.VMEM(full + (width,), jnp.bfloat16),
             pltpu.VMEM(full + (small.shape[1],), jnp.bfloat16),
-            pltpu.VMEM((2, length, 1024), jnp.float32),
-            pltpu.SemaphoreType.DMA((items, STAGES)),
-            pltpu.SemaphoreType.DMA((items, STAGES)),
-            pltpu.SemaphoreType.DMA((items,)),
-            pltpu.SemaphoreType.DMA((width // 1024,)),
+            pltpu.VMEM((2, length, block), jnp.float32),
+            pltpu.SemaphoreType.DMA((1, STAGES)),
+            pltpu.SemaphoreType.DMA((1, STAGES)),
+            pltpu.SemaphoreType.DMA((1,)),
+            pltpu.SemaphoreType.DMA((2, STAGES, RING)),
+            pltpu.SemaphoreType.DMA((2, STAGES, RING)),
+            pltpu.SemaphoreType.DMA((2, RING)),
             pltpu.SemaphoreType.DMA((2,)),
+            pltpu.SemaphoreType.DMA((2, block // DK)),
             pltpu.SemaphoreType.DMA,
+            pltpu.SemaphoreType.DMA((2,)),
+            pltpu.SemaphoreType.DMA((parts * H * DK // block,)),
         ],
         compiler_params=pltpu.CompilerParams(collective_id=1, has_side_effects=True, vmem_limit_bytes=LIMIT),
         cost_estimate=pl.CostEstimate(flops=2 * length * width * 1024, bytes_accessed=60_000_000, transcendentals=0),
     )(x, small, mix, out)
-    return [part.reshape((-1,) + part.shape[5:]) if part.ndim == 6 else part for part in outs]
+    return [part.reshape((-1,) + part.shape[5:]) if index < 3 else part for index, part in enumerate(outs)]
+
+
+PAIR = 2
+
+
+def mixer_kernel(
+    channel_ref, gate_ref, vec_ref, mask_ref, tap_ref, border_ref, gain_ref, shard_in,
+    xt_out, ok_out, us_out, gated_out, mixed_out, gathered_out,
+    w_ref, u_ref, t_ref, i_ref, k_read_ref, v_read_ref, relay_send, relay_recv,
+    ext_ref, q_ref, k_ref, v_ref,
+    relay_sems, send_sem, recv_sem, local_sem,
+):
+    step = pl.program_id(0)
+    steps = H // PAIR
+    parts = channel_ref.shape[0]
+    length = channel_ref.shape[2]
+    chunks = length // GROUP
+    z, x, core, y = place()
+    count = shard_in.shape[1] // (2 * WIDE)
+    lanes = [Spread(shard_in, gathered_out, lane, WIDE, (send_sem, recv_sem, local_sem)) for lane in range(2)]
+
+    def tick(number):
+        for stage in reversed(range(SPREAD_STAGES)):
+            index = number - stage * SPREAD_TICKS
+
+            @pl.when((index >= 0) & (index < count))
+            def _():
+                for lane in lanes:
+                    lane.step(index, stage)
+
+    def convolve(pair):
+        head = step * PAIR + pair
+        column = lambda part: pl.ds(pl.multiple_of((part * H + head) * DK, DK), DK)
+        for part in range(parts):
+            value = silu_pair(
+                conv_block(
+                    channel_ref[part, pair], border_ref[:, column(part)], tap_ref[:, column(part)], mask_ref,
+                    ext_ref.at[pair],
+                )
+            )[0]
+            if part == 0:
+                q_ref[pair] = unit_rows(value)[0] * DK ** (-0.5)
+            elif part <= NH:
+                k_ref[pair, part - 1] = unit_rows(value)[0]
+            else:
+                v_ref[pair, part - 1 - NH] = value
+            yield
+
+    def chunk_terms(pair, chunk, masks):
+        strict, same, levels, eye = masks
+        head = step * PAIR + pair
+        here = slice(chunk * GROUP, (chunk + 1) * GROUP)
+        rows = vec_ref[head, chunk]
+        columns = jnp.transpose(rows)
+        keys = k_ref[pair, :, here, :].reshape(SPAN, DK)
+        beta, scale, tail = columns[:, 1:2], columns[:, 3:4], columns[:, 4:5]
+        link = link_matrix(rows, columns)
+        lower = jnp.where(strict, beta * twice(link) * mm3(keys, keys, 1, 1), 0.0)
+        yield
+        inverse = eye - jnp.where(same, lower, 0.0)
+        for level in levels:
+            part = mm3(jnp.where(level, lower, 0.0), inverse)
+            yield
+            inverse = inverse - mm3(inverse, part)
+            yield
+        xt_out[pair, 0, chunk] = inverse
+
+    def chunk_rest(pair, chunk):
+        head = step * PAIR + pair
+        here = slice(chunk * GROUP, (chunk + 1) * GROUP)
+        rows = vec_ref[head, chunk]
+        columns = jnp.transpose(rows)
+        keys = k_ref[pair, :, here, :].reshape(SPAN, DK)
+        values = v_ref[pair, :, here, :].reshape(SPAN, DV)
+        queries = q_ref[pair, here, :]
+        beta, scale, tail = columns[:, 1:2], columns[:, 3:4], columns[:, 4:5]
+        inverse = xt_out[pair, 0, chunk]
+        reading = link_matrix(rows, columns) * mm3(queries, keys, 1, 1)
+        key_part = mm3(inverse, beta * scale * keys)
+        value_part = mm3(inverse, beta * values)
+        w_ref[head, chunk] = key_part
+        u_ref[head, chunk] = value_part
+        yield
+        tail_keys = tail * keys
+        transfer = mm3(key_part, tail_keys, 0, 0)
+        inject = mm3(value_part, tail_keys, 0, 0)
+        t_ref[head, chunk] = transfer
+        xt_out[pair, 1, chunk] = transfer
+        i_ref[head, chunk] = inject
+        yield
+        read_keys = scale[:GROUP] * queries - mm3(reading, key_part)
+        k_read_ref[head, chunk] = read_keys
+        ok_out[pair, chunk] = read_keys
+        v_read_ref[head, chunk] = mm3(reading, value_part)
+
+    def final_state(pair):
+        head = step * PAIR + pair
+        state = jnp.zeros((DV, DK), jnp.float32)
+        for chunk in range(chunks):
+            state = (
+                vec_ref[head, chunk, 3:4, GROUP - 1 : GROUP] * state - mm3(state, t_ref[head, chunk]) + i_ref[head, chunk]
+            )
+            yield
+        relay_send[head] = state.astype(jnp.bfloat16)
+
+    def readout(pair):
+        head = (step - steps) * PAIR + pair
+        state = jnp.where(y == 0, 0.0, 1.0) * relay_recv[head].astype(jnp.float32)
+        for chunk in range(chunks):
+            here = slice(chunk * GROUP, (chunk + 1) * GROUP)
+            us_out[pair, 1, chunk] = state
+            later = (
+                vec_ref[head, chunk, 3:4, GROUP - 1 : GROUP] * state - mm3(state, t_ref[head, chunk]) + i_ref[head, chunk]
+            )
+            us_out[pair, 0, chunk] = u_ref[head, chunk] - mm3(w_ref[head, chunk], state, 1, 1)
+            mixed = v_read_ref[head, chunk] + mm3(k_read_ref[head, chunk], state, 1, 1)
+            yield
+            mixed_out[pair, here, :] = mixed
+            inv = lax.rsqrt(jnp.mean(mixed * mixed, axis=1, keepdims=True) + EPSILON)
+            gate = silu_pair(gate_ref[pair, here, :])[0]
+            gated = mixed * inv * gain_ref[0:1, :] * gate
+            gated_out[here, pair * DV : (pair + 1) * DV] = gated.astype(gated_out.dtype)
+            state = later
+
+    relay = pltpu.make_async_remote_copy(
+        src_ref=relay_send, dst_ref=relay_recv, send_sem=relay_sems.at[0], recv_sem=relay_sems.at[1],
+        device_id=device_at(z, x, core, 1 - y), device_id_type=MESH,
+    )
+
+    @pl.when(step == 0)
+    def _():
+        meet(peers())
+
+    @pl.when(step < steps)
+    def _():
+        tick(step * 3)
+        together([convolve(pair) for pair in range(PAIR)])
+        masks = order_masks()
+        together([chunk_terms(pair, chunk, masks) for pair in range(PAIR) for chunk in range(chunks)])
+        tick(step * 3 + 1)
+        together([chunk_rest(pair, chunk) for pair in range(PAIR) for chunk in range(chunks)])
+        together([final_state(pair) for pair in range(PAIR)])
+        tick(step * 3 + 2)
+
+    @pl.when(step == steps - 1)
+    def _():
+        relay.start()
+
+    @pl.when(step == steps)
+    def _():
+        relay.wait()
+
+    @pl.when(step >= steps)
+    def _():
+        tick(steps * 3 + step - steps)
+        together([readout(pair) for pair in range(PAIR)])
+
+    @pl.when(step == 2 * steps - 1)
+    def _():
+        def drain(number, carry):
+            tick(number)
+            return carry
+
+        lax.fori_loop(steps * 4, max(count + SPREAD_FILL, steps * 4), drain, 0)
+
+
+def held_specs(count):
+    return [pl.BlockSpec(memory_space=pltpu.VMEM)] * count
+
+
+def mixer_call(channels, gate, vec, masks, taps, border, gain, shard):
+    parts, heads, length, width = channels.shape
+    chunks = length // GROUP
+    steps = H // PAIR
+
+    def early(step):
+        return jnp.minimum(step, steps - 1)
+
+    def late(step):
+        return jnp.maximum(step - steps, 0)
+
+    def heads_spec(shape, which):
+        rank = len(shape)
+        return pl.BlockSpec((PAIR,) + shape, lambda step: (which(step),) + (0,) * rank)
+
+    square = (chunks, SPAN, DK)
+    anywhere = pl.BlockSpec(memory_space=pl.ANY)
+    return pl.pallas_call(
+        mixer_kernel,
+        grid=(2 * steps,),
+        out_shape=[
+            per_head((2,) + square),
+            per_head((chunks, GROUP, DK)),
+            per_head((2,) + square),
+            jax.ShapeDtypeStruct((length, H * DV), jnp.bfloat16),
+            per_head((length, DV)),
+            jax.ShapeDtypeStruct(STACK + shard.shape, jnp.bfloat16),
+        ],
+        in_specs=[
+            pl.BlockSpec((parts, PAIR, length, DK), lambda step: (0, early(step), 0, 0)),
+            heads_spec((length, DV), late),
+        ]
+        + held_specs(5)
+        + [anywhere],
+        out_specs=[
+            heads_spec((2,) + square, early),
+            heads_spec((chunks, GROUP, DK), early),
+            heads_spec((2,) + square, late),
+            pl.BlockSpec((length, PAIR * DV), lambda step: (0, late(step))),
+            heads_spec((length, DV), late),
+            anywhere,
+        ],
+        scratch_shapes=[pltpu.VMEM((H,) + square, jnp.float32)] * 4
+        + [pltpu.VMEM((H, chunks, GROUP, DK), jnp.float32)] * 2
+        + [pltpu.VMEM((H, DV, DK), jnp.bfloat16)] * 2
+        + [
+            pltpu.VMEM((PAIR, length + 8, DK), jnp.float32),
+            pltpu.VMEM((PAIR, length, DK), jnp.float32),
+            pltpu.VMEM((PAIR, NH, length, DK), jnp.float32),
+            pltpu.VMEM((PAIR, NH, length, DK), jnp.float32),
+            pltpu.SemaphoreType.DMA((2,)),
+            pltpu.SemaphoreType.DMA((2, STAGES, RING)),
+            pltpu.SemaphoreType.DMA((2, STAGES, RING)),
+            pltpu.SemaphoreType.DMA((2, RING)),
+        ],
+        compiler_params=pltpu.CompilerParams(
+            dimension_semantics=("arbitrary",), collective_id=4, has_side_effects=True, vmem_limit_bytes=58 * 1024 * 1024
+        ),
+        cost_estimate=pl.CostEstimate(
+            flops=H * chunks * 24 * 2 * SPAN**3 * 4, bytes_accessed=80_000_000, transcendentals=0
+        ),
+    )(channels, gate, vec, masks, taps, border, gain, shard)
 
 
 WIDE = 256
@@ -559,14 +939,15 @@
 class Reduce:
     def __init__(self, refs, lane, count):
         (
-            self.own, self.first_send, self.first, self.near_kept, self.near_send, self.near,
+            self.both, self.first, self.near_kept, self.near_send, self.near,
             self.far_kept, self.far_send, self.far, self.last_kept, self.last_send, self.last,
-            self.load_sem, self.send_sem, self.recv_sem,
+            self.send_sem, self.recv_sem,
         ) = refs
         self.lane, self.count = lane, count
         self.z, self.x, self.core, self.y = place()
         self.peers = peers()
         self.x_first = lane == 0
+        self.columns = slice(lane * WIDE, (lane + 1) * WIDE)
 
     def copy(self, source, target, slot_of, stage, index, device):
         lane = self.lane
@@ -577,7 +958,8 @@
             device_id=device, device_id_type=MESH,
         )
 
-    def core_copy(self, source, index):
+    def core_copy(self, index):
+        source = self.both.at[lax.rem(index, 2), :, :, 1 - self.core, :, :, self.columns]
         return self.copy(source, self.first.at[self.lane, lax.rem(index, RING)], None, CORE, index, self.peers[ZS + 1])
 
     def near_copy(self, index):
@@ -604,31 +986,23 @@
             for step in range(ZS - 1)
         ]
 
-    def load_copy(self, source, index):
-        slot = lax.rem(index, 2)
-        return pltpu.make_async_copy(source, self.own.at[self.lane, slot], self.load_sem.at[self.lane, slot])
-
-    def from_core(self, index, loaded):
+    def from_core(self, index):
         lane, slot, ring = self.lane, lax.rem(index, 2), lax.rem(index, RING)
-        arrived = self.core_copy(self.first_send.at[lane, slot], index)
+        arrived = self.core_copy(index)
         arrived.wait_recv()
         arrived.wait_send()
 
-        @pl.when(loaded)
-        def _():
-            self.load_copy(self.first_send.at[lane, slot], index).wait()
-
         def one(z, carry):
             if self.x_first:
-                pick = lambda ref, half: ref[lane, slot, z, half]
+                pick = lambda half: self.both[slot, z, half, self.core, :, :, self.columns]
                 pick_got = lambda half: self.first[lane, ring, z, half]
                 mine = self.x
             else:
-                pick = lambda ref, half: ref[lane, slot, z, :, half]
+                pick = lambda half: self.both[slot, z, :, self.core, half, :, self.columns]
                 pick_got = lambda half: self.first[lane, ring, z, :, half]
                 mine = self.y
-            kept = pick(self.own, mine).astype(jnp.float32) + pick_got(mine).astype(jnp.float32)
-            sent = pick(self.own, 1 - mine).astype(jnp.float32) + pick_got(1 - mine).astype(jnp.float32)
+            kept = pick(mine).astype(jnp.float32) + pick_got(mine).astype(jnp.float32)
+            sent = pick(1 - mine).astype(jnp.float32) + pick_got(1 - mine).astype(jnp.float32)
             self.near_kept[lane, slot, z] = kept
             self.near_send[lane, slot, z] = sent.astype(jnp.bfloat16)
             return carry
@@ -681,8 +1055,7 @@
     half = (2, 2, rows, WIDE)
     lanes = 2
     return [
-        pltpu.VMEM((lanes, 2, ZS) + half, jnp.bfloat16),
-        pltpu.VMEM((lanes, 2, ZS) + half, jnp.bfloat16),
+        pltpu.VMEM((2,) + STACK + (rows, lanes * WIDE), jnp.bfloat16),
         pltpu.VMEM((lanes, RING, ZS) + half, jnp.bfloat16),
         pltpu.VMEM((lanes, 2, ZS, 2, rows, WIDE), jnp.float32),
         pltpu.VMEM((lanes, 2, ZS, 2, rows, WIDE), jnp.bfloat16),
@@ -693,110 +1066,121 @@
         pltpu.VMEM((lanes, 2, rows, WIDE), jnp.float32),
         pltpu.VMEM((lanes, 2, ZS - 1, rows, WIDE), jnp.bfloat16),
         pltpu.VMEM((lanes, RING, ZS - 1, rows, WIDE), jnp.bfloat16),
-        pltpu.SemaphoreType.DMA((lanes, 2)),
         pltpu.SemaphoreType.DMA((lanes, RINGS + ZS - 1, 2)),
         pltpu.SemaphoreType.DMA((lanes, RINGS + ZS - 1, RING)),
     ]
 
 
-def at_columns(ref, core, first, row=0, rows=32):
-    return ref.at[:, :, core, :, pl.ds(row, rows), pl.ds(pl.multiple_of(first, WIDE), WIDE)]
-
-
-def make_mixer_back_kernel(length, gu_count, down_count, out_count, down_blocks):
+def make_back_kernel(length, width, hidden):
     chunks = length // GROUP
     parts = 1 + 2 * NH
-    pairs = H // 2
-    gate_count = H * DV // WIDE
-    down_first = gu_count
-    out_first = down_first + down_count
-    gate_first = out_first + out_count
-    head_first = gate_first + gate_count
-    items = head_first + parts * pairs
-    count = items // 2
-    early_ticks = H // 2
+    blocks = hidden // WIDE
+    halves = width // WIDE // 2
+    down_first = blocks
+    out_first = down_first + 3 * halves
+    gate_first = out_first + halves
+    head_first = gate_first + halves
+    count = head_first + parts * (H // 2) // 2
     ticks = count + (REDUCE_STAGES - 1) * SPAN_TICKS
-    head_ticks = 3
     rows = 32
+    shard = hidden // 32
+    early = blocks + 2
+    late = early + H
+    last = late + H
+    early_tick = blocks
+    late_tick = early_tick + H // 2
 
     def kernel(
-        vec_ref, t_in, ok_in, mixed_in, gate_ref, gain_ref, d_gated_ref,
-        q_in, k0_in, k1_in, v0_in, v1_in, bq, bk0, bk1, bv0, bv1, tq, tk0, tk1, tv0, tv1, mask_ref,
-        x_in, u_in, s_in, normed_ref, gu_in, down_in, out_in,
-        gain_out, d_vec_out, gq_out, gk0_out, gk1_out, gv0_out, gv1_out, d_projected_out,
-        gu_out, down_out, out_out, mix_out,
+        xt_in, ok_in, mixed_in, gate_ref, channel_ref, us_in, wg_ref, wu_ref, wd_ref,
+        vec_ref, mask_ref, tap_ref, border_ref, gain_ref, out_ref, mlp_gain_ref,
+        x_in, gated_in, cot_in, mix_in, normed_in,
+        d_projected_out, y_out, d_hidden_out, d_normed_out,
+        gain_out, d_vec_out, tap_out, mlp_gain_out, gu_out, down_out, out_out, mix_out,
         d_mixed_ref, local_ref, all_ref, relay_send, relay_recv, edge_send, edge_recv, tail_ref,
-        ext_ref, pre_ref, q_ref, k_ref, v_ref, inv_ref, d_ref, z_ref,
-        relay_sems, edge_send_sem, edge_recv_sem, store_sem, *engine_refs,
+        ext_ref, pre_ref, q_ref, k_ref, inv_ref, d_ref, z_ref,
+        cot_ref, left_ref, act_t_ref, right_ref, d_mixer_ref,
+        relay_sems, edge_send_sem, edge_recv_sem, store_sem, load_sem, out_sem, mix_sem, *engine_refs,
     ):
         step = pl.program_id(0)
         z, x, core, y = place()
         y_peer = device_at(z, x, core, 1 - y)
         lanes = [Reduce(engine_refs, lane, count) for lane in range(2)]
         first_device = jnp.where(y == 0, 1.0, 0.0)
-
-        def source_of(item):
-            within = item - head_first
-            is_gate = item < head_first
+        halves_of_width = width // 2 // WIDE
+
+        def wide(first):
+            return pl.ds(pl.multiple_of(first, WIDE), WIDE)
+
+        def down_item(lane, index):
+            within = index - down_first
+            return lane * halves_of_width + within // 3, lax.rem(within, 3)
+
+        def mix_item(lane, index):
+            within = 2 * (index - head_first) + lane
+            is_gate = index < head_first
             part = jnp.where(is_gate, parts, lax.rem(within, parts))
-            column = jnp.where(is_gate, item - gate_first, within // parts) * WIDE
+            column = jnp.where(is_gate, 2 * (index - gate_first) + lane, within // parts) * WIDE
             return part, column
 
-        def begin(lane, index):
-            engine = lanes[lane]
-            item = 2 * index + lane
+        def begin(index):
             slot = lax.rem(index, 2)
-
-            def from_hbm(ref, first, row):
-                engine.core_copy(at_columns(ref, 1 - core, first, row), index).start()
-                engine.load_copy(at_columns(ref, core, first, row), index).start()
-
-            @pl.when(item < down_first)
+            is_down = (index >= down_first) & (index < out_first)
+
+            def product(left):
+                made = mm(left.reshape(-1, length), right_ref[...]).astype(jnp.bfloat16)
+                lanes[0].both[slot] = made.reshape(STACK + (rows, 2 * WIDE))
+
+            def pair(column):
+                return pl.ds(pl.multiple_of(column * 2 * WIDE, 2 * WIDE), 2 * WIDE)
+
+            @pl.when(is_down)
             def _():
-                from_hbm(gu_in, item * WIDE, 0)
-
-            @pl.when((item >= down_first) & (item < out_first))
+                for lane in range(2):
+                    right_ref[:, lane * WIDE : (lane + 1) * WIDE] = cot_ref[:, wide(down_item(lane, index)[0] * WIDE)]
+                here = pl.ds(pl.multiple_of(down_item(0, index)[1] * rows, rows), rows)
+                product(act_t_ref[:, :, :, :, here, :])
+
+            @pl.when((index >= out_first) & (index < gate_first))
             def _():
-                within = item - down_first
-                from_hbm(down_in, lax.rem(within, 4) * WIDE, pl.multiple_of((within // 4) * rows, rows))
-
-            @pl.when((item >= out_first) & (item < gate_first))
+                right_ref[...] = d_mixer_ref[:, pair(index - out_first)]
+
+            @pl.when((index >= gate_first) & (index < head_first))
             def _():
-                from_hbm(out_in, (item - out_first) * WIDE, 0)
-
-            @pl.when(item >= gate_first)
+                right_ref[...] = all_ref[parts, :, pair(index - gate_first)]
+
+            @pl.when(index >= head_first)
             def _():
-                part, column = source_of(item)
-                right = all_ref[part, :, pl.ds(pl.multiple_of(column, WIDE), WIDE)]
-                for half, target in ((1 - core, engine.first_send), (core, engine.own)):
-                    left = normed_ref[:, :, half].reshape(-1, length)
-                    target[lane, slot] = mm(left, right).astype(jnp.bfloat16).reshape(ZS, 2, 2, rows, WIDE)
-                engine.core_copy(engine.first_send.at[lane, slot], index).start()
+                for lane in range(2):
+                    part, column = mix_item(lane, index)
+                    right_ref[:, lane * WIDE : (lane + 1) * WIDE] = all_ref[part, :, wide(column)]
+
+            @pl.when(jnp.logical_not(is_down))
+            def _():
+                product(left_ref[jnp.where(index < down_first, 0, jnp.where(index < gate_first, 1, 2))])
+
+            for engine in lanes:
+                engine.core_copy(index).start()
 
         def end(lane, index):
-            item = 2 * index + lane
             total = lanes[lane].from_ring(index)
 
-            def here(first):
-                return pl.ds(pl.multiple_of(first, WIDE), WIDE)
-
-            @pl.when(item < down_first)
+            @pl.when(index < down_first)
             def _():
-                gu_out[:, here(item * WIDE)] = total
-
-            @pl.when((item >= down_first) & (item < out_first))
+                gu_out[:, wide(lane * hidden + index * WIDE)] = total
+
+            @pl.when((index >= down_first) & (index < out_first))
             def _():
-                within = item - down_first
-                down_out[within // 4, :, here(lax.rem(within, 4) * WIDE)] = total
-
-            @pl.when((item >= out_first) & (item < gate_first))
+                column, block = down_item(lane, index)
+                down_out[block, :, wide(column * WIDE)] = total
+
+            @pl.when((index >= out_first) & (index < gate_first))
             def _():
-                out_out[:, here((item - out_first) * WIDE)] = total
-
-            @pl.when(item >= gate_first)
+                out_out[:, wide((2 * (index - out_first) + lane) * WIDE)] = total
+
+            @pl.when(index >= gate_first)
             def _():
-                part, column = source_of(item)
-                mix_out[:, here(part * (H * DK) + column)] = total
+                part, column = mix_item(lane, index)
+                mix_out[:, wide(part * (H * DK) + column)] = total
 
         def tick(number):
             for stage in reversed(range(REDUCE_STAGES)):
@@ -804,32 +1188,144 @@
 
                 @pl.when((index >= 0) & (index < count))
                 def _():
-                    for lane in range(2):
-                        engine = lanes[lane]
-                        if stage == 0:
-                            begin(lane, index)
-                        elif stage == 1:
-                            engine.from_core(index, 2 * index + lane < gate_first)
+                    if stage == 0:
+                        begin(index)
+                    for lane, engine in enumerate(lanes):
+                        if stage == 1:
+                            engine.from_core(index)
                         elif stage == 2:
                             engine.from_near(index)
                         elif stage == 3:
                             engine.from_far(index)
-                        else:
+                        elif stage == 4:
                             end(lane, index)
+
+        def transposed(values):
+            flipped = jnp.transpose(values.astype(jnp.float32)).astype(jnp.bfloat16)
+            return flipped.reshape(STACK + (rows, length))
+
+        def head_slices():
+            return [slice(head * DV, (head + 1) * DV) for head in range(H)]
+
+        def joined(ref, first):
+            quarter = length // SPAN
+            return jnp.concatenate(
+                [ref[head, first * quarter : (first + 1) * quarter].reshape(length, DV) for head in range(H)], axis=1
+            )
+
+        def split(ref, first, values):
+            quarter = length // SPAN
+            for head, here in enumerate(head_slices()):
+                ref[head, first * quarter : (first + 1) * quarter] = values[:, here].reshape(quarter, SPAN, DV)
+
+        def enter_mlp():
+            loads = [
+                pltpu.make_async_copy(source, target, load_sem.at[index])
+                for index, (source, target) in enumerate(
+                    ((gated_in, all_ref.at[1]), (x_in, all_ref.at[0]), (cot_in, cot_ref), (normed_in, left_ref.at[2]))
+                )
+            ]
+            for load in loads:
+                load.start()
+            for load in loads:
+                load.wait()
+            split(local_ref, 1, mm(all_ref[1], out_ref[...]))
+            quarter = length // SPAN
+
+            def one(index, carry):
+                here = pl.ds(pl.multiple_of(index * SPAN, SPAN), SPAN)
+                mixed_rows = jnp.concatenate([local_ref[head, quarter + index] for head in range(H)], axis=1)
+                hidden_rows = all_ref[0, here].astype(jnp.float32) + mixed_rows
+                inv = lax.rsqrt(jnp.mean(hidden_rows * hidden_rows, axis=1, keepdims=True) + EPSILON)
+                all_ref[3, here] = (hidden_rows * inv * mlp_gain_ref[0:1, :]).astype(jnp.bfloat16)
+                for head, columns in enumerate(head_slices()):
+                    local_ref[head, index] = hidden_rows[:, columns]
+                    local_ref[head, quarter + index] = hidden_rows[:, columns]
+                return carry
+
+            lax.fori_loop(0, quarter, one, 0)
+            d_mixed_ref[...] = jnp.zeros_like(d_mixed_ref)
+            left_ref[0] = transposed(all_ref[3])
+            left_ref[1] = transposed(all_ref[1])
+            act_t_ref[:, :, :, :, shard:, :] = jnp.zeros(STACK + (act_t_ref.shape[4] - shard, length), jnp.float32)
+
+        def mlp_block(block):
+            mlp_in = all_ref[3]
+            gate = mm(mlp_in, wg_ref[...])
+            up = mm(mlp_in, wu_ref[...])
+            open_, sig = silu_pair(gate)
+            act = (open_ * up).astype(jnp.bfloat16)
+            d_act = mm(cot_ref[...], wd_ref[...], 1, 1)
+            d_gate = (d_act * up * sig * (1.0 + gate * (1.0 - sig))).astype(jnp.bfloat16)
+            d_up = (d_act * open_).astype(jnp.bfloat16)
+            right_ref[:, :WIDE] = d_gate
+            right_ref[:, WIDE:] = d_up
+            split(local_ref, 0, joined(local_ref, 0) + mm(act, wd_ref[...]))
+            d_in = mm(d_gate, wg_ref[...], 1, 1) + mm(d_up, wu_ref[...], 1, 1)
+            for head, here in enumerate(head_slices()):
+                d_mixed_ref[head] = d_mixed_ref[head] + d_in[:, here]
+            act_t = jnp.transpose(act.astype(jnp.float32))
+            for group in range(WIDE // 8):
+                place_ = block * (WIDE // 8) + group
+                owner, row = place_ // (shard // 8), lax.rem(place_, shard // 8) * 8
+                act_t_ref[
+                    owner // 8, lax.rem(owner // 4, 2), lax.rem(owner // 2, 2), lax.rem(owner, 2),
+                    pl.ds(pl.multiple_of(row, 8), 8), :,
+                ] = act_t[group * 8 : (group + 1) * 8]
+
+        y_store = pltpu.make_async_copy(all_ref.at[0], y_out, out_sem.at[0])
+
+        def leave_mlp():
+            quarter = length // SPAN
+
+            def tile(ref, first, index):
+                return jnp.concatenate([ref[head, first * quarter + index] for head in range(H)], axis=1)
+
+            def one(index, gain_grad):
+                here = pl.ds(pl.multiple_of(index * SPAN, SPAN), SPAN)
+                all_ref[0, here] = tile(local_ref, 0, index).astype(jnp.bfloat16)
+                hidden_rows = tile(local_ref, 1, index)
+                d_in = jnp.concatenate([d_mixed_ref[head, here] for head in range(H)], axis=1)
+                inv = lax.rsqrt(jnp.mean(hidden_rows * hidden_rows, axis=1, keepdims=True) + EPSILON)
+                unit = hidden_rows * inv
+                d_unit = d_in * mlp_gain_ref[0:1, :]
+                d_norm = inv * (d_unit - unit * jnp.mean(d_unit * unit, axis=1, keepdims=True))
+                d_hidden = cot_ref[here].astype(jnp.float32) + d_norm
+                for head, columns in enumerate(head_slices()):
+                    local_ref[head, quarter + index] = d_hidden[:, columns]
+                d_mixer_ref[here] = d_hidden.astype(jnp.bfloat16)
+                return gain_grad + jnp.sum(d_in * unit, axis=0, keepdims=True)
+
+            gain_grad = lax.fori_loop(0, quarter, one, jnp.zeros((1, width), jnp.float32))
+            mlp_gain_out[...] = jnp.broadcast_to(gain_grad, (8, width))
+            y_store.start()
+            stores = [
+                pltpu.make_async_copy(
+                    local_ref.at[head, quarter : 2 * quarter], d_hidden_out.at[:, :, here], out_sem.at[1 + head]
+                )
+                for head, here in enumerate(head_slices())
+            ]
+            for store in stores:
+                store.start()
+            d_normed_rows = mm(d_mixer_ref[...], out_ref[...], 1, 1)
+            for head, here in enumerate(head_slices()):
+                d_mixed_ref[head] = d_normed_rows[:, here]
+            for store in stores:
+                store.wait()
 
         def readout_back(head):
             gain = gain_ref[0:1, :]
             gain_grad = jnp.zeros((1, DV), jnp.float32)
             column = pl.ds(pl.multiple_of(head * DV, DV), DV)
-            locals_ = []
-            for chunk in range(chunks):
+            state = jnp.zeros((DV, DK), jnp.float32)
+            for chunk in reversed(range(chunks)):
                 here = slice(chunk * GROUP, (chunk + 1) * GROUP)
-                mixed = mixed_in[here, :]
+                mixed = mixed_in[0, here, :]
                 inv = lax.rsqrt(jnp.mean(mixed * mixed, axis=1, keepdims=True) + EPSILON)
                 unit = mixed * inv
-                gate = gate_ref[here, :]
+                gate = gate_ref[0, here, :]
                 open_, sig = silu_pair(gate)
-                d_gated = d_gated_ref[here, :]
+                d_gated = d_mixed_ref[head, here]
                 d_scaled = d_gated * open_
                 d_gate = d_gated * unit * gain * sig * (1.0 + gate * (1.0 - sig))
                 all_ref[parts, here, column] = d_gate.astype(jnp.bfloat16)
@@ -839,71 +1335,75 @@
                 d_mixed_ref[head, here] = d_mixed
                 local = mm3(d_mixed, ok_in[0, chunk], 0, 0)
                 local_ref[head, chunk] = local
-                locals_.append(local)
-            gain_out[0] = jnp.broadcast_to(gain_grad, (8, DV))
-            state = jnp.zeros((DV, DK), jnp.float32)
-            for chunk in reversed(range(chunks)):
                 state = (
-                    vec_ref[0, chunk, 3:4, GROUP - 1 : GROUP] * state
-                    - mm3(state, t_in[0, chunk], 1, 1)
-                    + locals_[chunk]
+                    vec_ref[head, chunk, 3:4, GROUP - 1 : GROUP] * state
+                    - mm3(state, xt_in[0, 1, chunk], 1, 1)
+                    + local
                 )
+            gain_out[head] = jnp.broadcast_to(gain_grad, (8, DV))
             relay_send[head] = state.astype(jnp.bfloat16)
 
-        channels = (q_in, k0_in, k1_in, v0_in, v1_in)
-        taps = (tq, tk0, tk1, tv0, tv1)
+        def head_columns(part, head):
+            return pl.ds(pl.multiple_of((part * H + head) * DK, DK), DK)
 
         def prepare(head):
-            for part, (channel, border, tap) in enumerate(zip(channels, (bq, bk0, bk1, bv0, bv1), taps)):
-                pre = conv_block(channel, border, tap, mask_ref, ext_ref.at[part])
+            for part in range(parts):
+                here = head_columns(part, head)
+                pre = conv_block(channel_ref[part], border_ref[:, here], tap_ref[:, here], mask_ref, ext_ref.at[part])
+                yield
                 pre_ref[part] = pre
+                if part > NH:
+                    continue
                 value = silu_pair(pre)[0]
                 if part == 0:
                     unit, inv = unit_rows(value)
                     q_ref[...] = unit * DK ** (-0.5)
-                    inv_ref[0] = jnp.broadcast_to(inv, (length, DK))
-                elif part <= NH:
+                    inv_ref[:, 0:1] = inv
+                else:
                     unit, inv = unit_rows(value)
                     k_ref[part - 1] = unit
-                    inv_ref[part] = jnp.broadcast_to(inv, (length, DK))
-                else:
-                    v_ref[part - 1 - NH] = value
-
-        def chain(head):
-            exit_grads = [None] * chunks
+                    inv_ref[:, part : part + 1] = inv
+
+        def chain(head, exit_grads):
             grad = first_device * relay_recv[head].astype(jnp.float32)
             for chunk in reversed(range(chunks)):
                 exit_grads[chunk] = grad
                 grad = (
-                    vec_ref[0, chunk, 3:4, GROUP - 1 : GROUP] * grad
-                    - mm3(grad, t_in[0, chunk], 1, 1)
+                    vec_ref[head, chunk, 3:4, GROUP - 1 : GROUP] * grad
+                    - mm3(grad, xt_in[0, 1, chunk], 1, 1)
                     + local_ref[head, chunk]
                 )
-            return exit_grads
+                yield
 
         def one_chunk(chunk, head, d_exit):
             strict = order_masks()[0]
             column_index = iotas(SPAN, 8)[1]
             here = slice(chunk * GROUP, (chunk + 1) * GROUP)
-            rows_, columns = chunk_vectors(vec_ref, chunk)
+            rows_ = vec_ref[head, chunk]
+            columns = jnp.transpose(rows_)
             beta, scale, tail = columns[:, 1:2], columns[:, 3:4], columns[:, 4:5]
             keys = k_ref[:, here, :].reshape(SPAN, DK)
-            values = v_ref[:, here, :].reshape(SPAN, DV)
+            values = silu_pair(pre_ref[1 + NH :, here, :].reshape(SPAN, DV))[0]
             queries = q_ref[here, :]
             link = link_matrix(rows_, columns)
             link_gram = jnp.where(strict, twice(link) * mm3(keys, keys, 1, 1), 0.0)
             reading = link * mm3(queries, keys, 1, 1)
-            solved = u_in[0, chunk]
-            entry = s_in[0, chunk]
+            yield
+            solved = us_in[0, 0, chunk]
+            entry = us_in[0, 1, chunk]
             d_mixed = d_mixed_ref[head, here]
             tail_keys = tail * keys
             d_solved = mm3(reading, d_mixed, 0, 0) + mm3(tail_keys, d_exit, 1, 1)
-            d_right = mm3(x_in[0, chunk], d_solved, 0, 0)
+            yield
+            d_right = mm3(xt_in[0, 0, chunk], d_solved, 0, 0)
+            yield
             d_lower = jnp.where(strict, -mm3(d_right, solved, 1, 1), 0.0)
+            yield
             d_tail_keys = mm3(solved, d_exit)
             d_right_entry = mm3(d_right, entry)
             d_reading = mm3(d_mixed, solved, 1, 1)
             d_query_entry = mm3(d_mixed, entry)
+            yield
             both_scale = -jnp.sum(d_right_entry * keys, axis=1, keepdims=True)
             lower_weight = d_lower * link_gram
             d_beta = (
@@ -915,6 +1415,7 @@
             reading_moment = d_reading * reading
             d_gram = beta * twice(link) * d_lower
             d_gram = d_gram + jnp.transpose(d_gram)
+            yield
             d_query_gram = link * d_reading
             d_keys = (
                 tail * d_tail_keys
@@ -924,6 +1425,7 @@
             )
             d_queries = mm3(d_query_gram, keys) + scale[:GROUP] * d_query_entry
             d_values = beta * d_right
+            yield
             none = jnp.zeros((GROUP, 1), jnp.float32)
             d_gap = jnp.sum(lower_moment, axis=1, keepdims=True) + jnp.concatenate(
                 [jnp.sum(reading_moment, axis=1, keepdims=True), none], axis=0
@@ -944,7 +1446,7 @@
             )
             grads = jnp.transpose(grads)
             sums = jnp.sum(lower_moment, axis=0, keepdims=True) + jnp.sum(reading_moment, axis=0, keepdims=True)
-            d_vec_out[0, chunk] = grads - jnp.where(iotas(8, SPAN)[0] == 0, sums, 0.0)
+            d_vec_out[head, chunk] = grads - jnp.where(iotas(8, SPAN)[0] == 0, sums, 0.0)
             d_ref[0, here, :] = d_queries
             for house in range(NH):
                 mine = slice(house * GROUP, (house + 1) * GROUP)
@@ -952,7 +1454,6 @@
                 d_ref[1 + NH + house, here, :] = d_values[mine]
 
         def finish_head(head):
-            tap_grads = (gq_out, gk0_out, gk1_out, gv0_out, gv1_out)
             column = pl.ds(pl.multiple_of(head * DK, DK), DK)
             z_ref[0:8, :] = jnp.zeros((8, DK), jnp.float32)
             z_ref[8 + length : 16 + length, :] = jnp.zeros((8, DK), jnp.float32)
@@ -962,16 +1463,17 @@
                     unit = q_ref[...] * DK ** 0.5 if part == 0 else k_ref[part - 1]
                     if part == 0:
                         grad = grad * DK ** (-0.5)
-                    grad = inv_ref[part] * (grad - unit * jnp.sum(grad * unit, axis=1, keepdims=True))
+                    grad = inv_ref[:, part : part + 1] * (grad - unit * jnp.sum(grad * unit, axis=1, keepdims=True))
                 pre = pre_ref[part]
                 sig = jax.nn.sigmoid(pre)
                 grad = grad * sig * (1.0 + pre * (1.0 - sig))
-                tap = taps[part]
+                here = head_columns(part, head)
+                tap = tap_ref[:, here]
                 total = grad * tap[0:1, :]
                 edge = jnp.zeros((8, DK), jnp.float32)
-                tap_rows = [jnp.sum(grad * channels[part][...], axis=0, keepdims=True)]
+                tap_rows = [jnp.sum(grad * channel_ref[part], axis=0, keepdims=True)]
                 for index in range(1, 4):
-                    shifted = grad * mask_ref[index - 1]
+                    shifted = grad * mask_ref[index - 1].astype(jnp.float32)
                     tap_rows.append(
                         jnp.sum(shifted * ext_ref[part, 8 - index : 8 - index + length, :], axis=0, keepdims=True)
                     )
@@ -981,32 +1483,40 @@
                 all_ref[part, :, column] = total.astype(jnp.bfloat16)
                 edge_send[lax.rem(head, 2), part] = edge
                 tail_ref[part] = total[length - 16 :, :]
-                tap_grads[part][...] = jnp.concatenate(tap_rows + [jnp.zeros((4, DK), jnp.float32)], axis=0)
+                tap_out[:, here] = jnp.concatenate(tap_rows + [jnp.zeros((4, DK), jnp.float32)], axis=0)
 
         @pl.when(step == 0)
         def _():
             meet(peers())
-
-        @pl.when((step < H) & (lax.rem(step, 2) == 0))
+            enter_mlp()
+
+        @pl.when((step >= 1) & (step <= blocks))
         def _():
-            tick(step // 2)
-
-        @pl.when(step < H)
+            mlp_block(step - 1)
+
+        @pl.when(step == blocks + 1)
         def _():
-            readout_back(step)
+            leave_mlp()
+
+        early_head = step - early
+
+        @pl.when((step >= early) & (step < late))
+        def _():
+            readout_back(early_head)
 
         relay = pltpu.make_async_remote_copy(
             src_ref=relay_send, dst_ref=relay_recv, send_sem=relay_sems.at[0], recv_sem=relay_sems.at[1],
             device_id=y_peer, device_id_type=MESH,
         )
 
-        @pl.when(step == H - 1)
+        @pl.when(step == late - 1)
         def _():
             relay.start()
 
-        @pl.when(step == H)
+        @pl.when(step == late)
         def _():
             relay.wait()
+            y_store.wait()
 
         def edge_copy(head):
             slot = lax.rem(head, 2)
@@ -1015,36 +1525,45 @@
                 recv_sem=edge_recv_sem.at[slot], device_id=y_peer, device_id_type=MESH,
             )
 
-        @pl.when(step > H)
-        def _():
-            head = step - H - 1
-            edge = edge_copy(head)
-            edge.wait()
+        def fix_edges(head):
+            edge_copy(head).wait()
             here = pl.ds(pl.multiple_of(head * DK, DK), DK)
             for part in range(parts):
                 fixed = tail_ref[part, 8:16] + first_device * edge_recv[lax.rem(head, 2), part]
                 both = jnp.concatenate([tail_ref[part, 0:8], fixed], axis=0)
                 all_ref[part, length - 16 : length, here] = both.astype(jnp.bfloat16)
 
-        head_tick = early_ticks + (step - H) * head_ticks
-
-        @pl.when((step >= H) & (step < 2 * H))
+        @pl.when((step >= late) & (step < last))
         def _():
-            head = step - H
-            tick(head_tick)
-            prepare(head)
-            exit_grads = chain(head)
-            for chunk in reversed(range(chunks // 2, chunks)):
-                one_chunk(chunk, head, exit_grads[chunk])
-            tick(head_tick + 1)
-            for chunk in reversed(range(chunks // 2)):
-                one_chunk(chunk, head, exit_grads[chunk])
-            tick(head_tick + 2)
+            head = step - late
+            exit_grads = [None] * chunks
+            together([chain(head, exit_grads), prepare(head)])
+
+            @pl.when(head > 0)
+            def _():
+                fix_edges(head - 1)
+
+            tick(late_tick + jnp.minimum(2 * head, head + 5))
+            together([one_chunk(chunk, head, exit_grads[chunk]) for chunk in reversed(range(chunks))])
+
             finish_head(head)
             edge_copy(head).start()
 
-        @pl.when(step == 2 * H)
+        late_head = step - late
+        in_mlp = (step >= 1) & (step <= blocks)
+        in_early = (step >= early) & (step < late) & (lax.rem(early_head, 2) == 0)
+        in_late = (late_head >= 0) & (late_head < 5)
+        number = jnp.where(
+            in_mlp, step - 1, jnp.where(in_early, early_tick + early_head // 2, late_tick + 2 * late_head + 1)
+        )
+
+        @pl.when(in_mlp | in_early | in_late)
         def _():
+            tick(number)
+
+        @pl.when(step == last)
+        def _():
+            fix_edges(H - 1)
             stores = [
                 pltpu.make_async_copy(
                     all_ref.at[part], d_projected_out.at[:, pl.ds(part * H * DK, H * DK)], store_sem.at[part]
@@ -1053,83 +1572,102 @@
             ]
             for store in stores:
                 store.start()
-
-            def drain(number, carry):
-                tick(number)
+            loads = mix_in.shape[5] // length
+
+            def load(index):
+                here = pl.ds(pl.multiple_of(index * length, length), length)
+                slot = lax.rem(index, 2)
+                return pltpu.make_async_copy(mix_in.at[:, :, :, :, :, here], left_ref.at[slot], mix_sem.at[slot])
+
+            load(0).start()
+            load(1).start()
+            d_mixed_ref[...] = jnp.zeros_like(d_mixed_ref)
+            per_part = H * DK // length
+
+            def drain(index, carry):
+                tick(late_tick + H + 5 + index)
+                load(index).wait()
+                here = pl.ds(pl.multiple_of(lax.rem(index, per_part) * length, length), length)
+                left = all_ref[index // per_part, :, here]
+                added = mm(left, left_ref[lax.rem(index, 2)].reshape(-1, length), 1, 1)
+                for head, place_ in enumerate(head_slices()):
+                    d_mixed_ref[head] = d_mixed_ref[head] + added[:, place_]
+
+                @pl.when(index + 2 < loads)
+                def _():
+                    load(index + 2).start()
+
                 return carry
 
-            lax.fori_loop(early_ticks + H * head_ticks, ticks, drain, 0)
+            lax.fori_loop(0, loads, drain, 0)
+            assert late_tick + H + 5 + loads >= ticks
+            for head, here in enumerate(head_slices()):
+                stores.append(
+                    pltpu.make_async_copy(d_mixed_ref.at[head], d_normed_out.at[:, here], out_sem.at[head])
+                )
+                stores[-1].start()
             for store in stores:
                 store.wait()
 
     return kernel, ticks
 
 
-def mixer_back_call(
-    vec, transfer, out_keys, mixed, projected, gain, d_gated, border, taps, masks, inverse, solved, entries,
-    normed_t, grad_gu, grad_down, grad_out,
+def back_call(
+    xt, out_keys, mixed, gate, channels, us, gu, down, vec, masks, taps, border, gain, out, mlp_gain,
+    x, gated, cot, mix, normed_t,
 ):
-    length = projected.shape[0]
+    parts, heads, length, width = channels.shape
     chunks = length // GROUP
-    parts = 1 + 2 * NH
-    rows = grad_gu.shape[4]
-    down_blocks = grad_down.shape[4] // rows
-    kernel, ticks = make_mixer_back_kernel(
-        length, grad_gu.shape[5] // WIDE, down_blocks * (grad_down.shape[5] // WIDE), grad_out.shape[5] // WIDE, down_blocks
-    )
+    model, hidden = gu.shape[0], down.shape[0]
+    rows, blocks = 32, hidden // WIDE
+    padded = -(-(hidden // 32) // rows) * rows
+    kernel, ticks = make_back_kernel(length, model, hidden)
+    first = blocks + 2
 
     def either(step):
-        return lax.rem(step, H)
+        return lax.rem(jnp.maximum(step - first, 0), H)
 
     def early(step):
-        return jnp.minimum(step, H - 1)
+        return jnp.clip(step - first, 0, H - 1)
 
     def late(step):
-        return jnp.clip(step - H, 0, H - 1)
-
-    def heads(shape, which):
+        return jnp.clip(step - first - H, 0, H - 1)
+
+    def block(step):
+        return jnp.clip(step - 1, 0, blocks - 1)
+
+    def heads_spec(shape, which):
         rank = len(shape)
         return pl.BlockSpec((1,) + shape, lambda step: (which(step),) + (0,) * rank)
-
-    def cols(count, first, which):
-        return pl.BlockSpec((count, DK), lambda step: (0, first + which(step)))
-
-    def whole(shape):
-        rank = len(shape)
-        return pl.BlockSpec(shape, lambda step: (0,) * rank)
 
     square = (chunks, SPAN, DK)
     anywhere = pl.BlockSpec(memory_space=pl.ANY)
     in_specs = (
         [
-            heads((chunks, 8, SPAN), either), heads(square, either), heads((chunks, GROUP, DK), early),
-            cols(length, 0, early), cols(length, parts * H, early), whole((8, DV)), cols(length, 0, early),
+            heads_spec((2,) + square, either), heads_spec((chunks, GROUP, DK), early), heads_spec((length, DV), early),
+            heads_spec((length, DV), early),
+            pl.BlockSpec((parts, None, length, DK), lambda step: (0, late(step), 0, 0)), heads_spec((2,) + square, late),
+            pl.BlockSpec((model, WIDE), lambda step: (0, block(step))),
+            pl.BlockSpec((model, WIDE), lambda step: (0, blocks + block(step))),
+            pl.BlockSpec((WIDE, model), lambda step: (block(step), 0)),
         ]
-        + [cols(length, H * part, late) for part in range(parts)]
-        + [cols(8, H * part, late) for part in range(parts)] * 2
-        + [whole((3, length, DK))]
-        + [heads(square, late)] * 3
-        + [whole(normed_t.shape)]
-        + [anywhere] * 3
+        + held_specs(7)
+        + [anywhere] * 5
     )
-    shard = (rows,)
-    out_shape = (
-        [per_head((8, DV)), per_head((chunks, 8, SPAN))]
-        + [jax.ShapeDtypeStruct((8, H * DK), jnp.float32)] * parts
-        + [
-            jax.ShapeDtypeStruct((length, (parts + 1) * H * DK), jnp.bfloat16),
-            jax.ShapeDtypeStruct((rows, grad_gu.shape[5]), jnp.float32),
-            jax.ShapeDtypeStruct((down_blocks, rows, grad_down.shape[5]), jnp.float32),
-            jax.ShapeDtypeStruct((rows, grad_out.shape[5]), jnp.float32),
-            jax.ShapeDtypeStruct((rows, (parts + 1) * H * DK), jnp.float32),
-        ]
-    )
-    out_specs = (
-        [heads((8, DV), early), heads((chunks, 8, SPAN), late)]
-        + [cols(8, 0, late)] * parts
-        + [anywhere]
-        + [whole(out.shape) for out in out_shape[-4:]]
-    )
+    out_shape = [
+        jax.ShapeDtypeStruct((length, (parts + 1) * H * DK), jnp.bfloat16),
+        jax.ShapeDtypeStruct((length, model), jnp.bfloat16),
+        jax.ShapeDtypeStruct((length // SPAN, SPAN, model), jnp.float32),
+        jax.ShapeDtypeStruct((length, model), jnp.float32),
+        per_head((8, DV)),
+        per_head((chunks, 8, SPAN)),
+        jax.ShapeDtypeStruct((8, parts * H * DK), jnp.float32),
+        jax.ShapeDtypeStruct((8, model), jnp.float32),
+        jax.ShapeDtypeStruct((rows, gu.shape[1]), jnp.float32),
+        jax.ShapeDtypeStruct((padded // rows, rows, model), jnp.float32),
+        jax.ShapeDtypeStruct((rows, model), jnp.float32),
+        jax.ShapeDtypeStruct((rows, (parts + 1) * H * DK), jnp.float32),
+    ]
     tall = pltpu.VMEM((parts, length, DK), jnp.float32)
     scratch = [
         pltpu.VMEM((H, length, DV), jnp.float32),
@@ -1144,32 +1682,38 @@
         tall,
         pltpu.VMEM((length, DK), jnp.float32),
         pltpu.VMEM((NH, length, DK), jnp.float32),
-        pltpu.VMEM((NH, length, DK), jnp.float32),
-        pltpu.VMEM((1 + NH, length, DK), jnp.float32),
+        pltpu.VMEM((length, DK), jnp.float32),
         tall,
         pltpu.VMEM((length + 16, DK), jnp.float32),
+        pltpu.VMEM((length, model), jnp.bfloat16),
+        pltpu.VMEM((3,) + STACK + (rows, length), jnp.bfloat16),
+        pltpu.VMEM(STACK + (padded, length), jnp.float32),
+        pltpu.VMEM((length, 2 * WIDE), jnp.bfloat16),
+        pltpu.VMEM((length, model), jnp.bfloat16),
         pltpu.SemaphoreType.DMA((2,)),
         pltpu.SemaphoreType.DMA((2,)),
         pltpu.SemaphoreType.DMA((2,)),
         pltpu.SemaphoreType.DMA((parts + 1,)),
+        pltpu.SemaphoreType.DMA((4,)),
+        pltpu.SemaphoreType.DMA((1 + H,)),
+        pltpu.SemaphoreType.DMA((2,)),
     ] + reduce_scratch(rows)
     return pl.pallas_call(
         kernel,
-        grid=(2 * H + 1,),
+        grid=(first + 2 * H + 1,),
         out_shape=out_shape,
         in_specs=in_specs,
-        out_specs=out_specs,
+        out_specs=[anywhere] * 4 + held_specs(len(out_shape) - 4),
         scratch_shapes=scratch,
         compiler_params=pltpu.CompilerParams(
-            dimension_semantics=("arbitrary",), collective_id=2, has_side_effects=True, vmem_limit_bytes=58 * 1024 * 1024
+            dimension_semantics=("arbitrary",), collective_id=2, has_side_effects=True, vmem_limit_bytes=255 * 256 * 1024
         ),
         cost_estimate=pl.CostEstimate(
             flops=H * chunks * 14 * 2 * SPAN**3 * 4, bytes_accessed=100_000_000, transcendentals=0
         ),
     )(
-        vec, transfer, out_keys, mixed, projected, gain, d_gated,
-        *[projected] * parts, *[border] * parts, *[taps] * parts, masks,
-        inverse, solved, entries, normed_t, grad_gu, grad_down, grad_out,
+        xt, out_keys, mixed, gate, channels, us, gu, gu, down, vec, masks, taps, border, gain, out, mlp_gain,
+        x, gated, cot, mix, normed_t,
     )
 
 
@@ -1521,7 +2065,7 @@
             [w_small, norm_in[:, None], norm_mlp[:, None], conv_w.reshape(tap_count, rows, -1).transpose(1, 2, 0).reshape(rows, -1)], axis=1
         )
         small = jnp.concatenate([small, jnp.zeros((rows, DK - small.shape[1]), small.dtype)], axis=1)
-        mix_all, out_all, small_pack, normed_low, projected, gates_raw = gather_project_call(
+        mix_all, out_all, small_pack, normed_low, normed_t, channels, gate, gates_raw, border = gather_project_call(
             block_input.reshape(seg_len, width), small, w_mix, w_out
         )
         small_all = small_pack[:, :smalls]
@@ -1540,9 +2084,13 @@
         normed_low = normed.astype(jnp.bfloat16)
         projected = jnp.dot(normed_low, mix_all, preferred_element_type=jnp.float32)
         gates_raw = jnp.dot(normed_low, small_all, preferred_element_type=jnp.float32)
-    gu_all, down_all = gather(w_gu), gather(w_down)
-    border = from_behind(projected[seg_len - tap_count + 1 :, : parts * key_width], "seq", 1)
-    border = jnp.concatenate([jnp.zeros((9 - tap_count, parts * key_width), jnp.float32), border], axis=0)
+    if fast:
+        down_own = w_down + (gates_raw[0, 0] * 0.0).astype(w_down.dtype)
+        down_all = gather(down_own)
+    else:
+        gu_all, down_all = gather(w_gu), gather(w_down)
+        border = from_behind(projected[seg_len - tap_count + 1 :, : parts * key_width], "seq", 1)
+        border = jnp.concatenate([jnp.zeros((9 - tap_count, parts * key_width), jnp.float32), border], axis=0)
     positions = lax.axis_index("seq") * seg_len + jnp.arange(1 - tap_count, seg_len, dtype=jnp.int32)
     seg_ext = jnp.sum((positions[:, None] >= doc_starts[0][None, :]).astype(jnp.int32), axis=1)
     seg_ext = jnp.where(positions < 0, -1, seg_ext)
@@ -1551,65 +2099,70 @@
         [seg_ext[tap_count - 1 - tap : tap_count - 1 - tap + seg_len] == seg_now for tap in range(1, tap_count)]
     ).astype(jnp.float32)
     masks = jnp.broadcast_to(masks[:, :, None], (tap_count - 1, seg_len, DK))
+    if fast:
+        masks = masks.astype(jnp.bfloat16)
     taps = jnp.concatenate([conv_all.astype(jnp.float32), jnp.zeros((8 - tap_count, parts * key_width), jnp.float32)], axis=0)
     vec, vec_back = jax.vjp(
         partial(gate_vectors, seg_now, seg_ext[tap_count - 2]), gates_raw, decay_log.astype(jnp.float32)
     )
-    zero_state = jnp.zeros((H, DV, DK), jnp.float32)
-    inverse, key_part, value_part, transfer, inject, out_keys, out_values, final_state = forward_call(
-        projected, border, taps, masks, vec, zero_state
-    )
-    entry = zero_state
-    device_transfer = None
-    if seqs > 2:
-        eye = jnp.broadcast_to(jnp.eye(DK, dtype=jnp.float32), (H, DK, DK))
-        device_transfer = chain_call(vec, transfer, eye)
-    for turn in range(seqs - 1):
-        leaving = final_state
-        if turn > 0:
-            leaving = leaving + jnp.einsum("hvk,hkl->hvl", entry, device_transfer, precision=HIGHEST)
-        entry = from_behind(leaving.astype(jnp.bfloat16), "seq", 1).astype(jnp.float32)
     gain = jnp.broadcast_to(norm_out.astype(jnp.float32)[None, :], (8, DV))
-    normed_out_low, mixed, solved, entries = readout_call(
-        vec, key_part, value_part, transfer, inject, out_keys, out_values, entry, projected, gain
-    )
-    hidden = residual_in + jnp.dot(normed_out_low, out_all, preferred_element_type=jnp.float32)
-    mlp_in, norm_mlp_back = jax.vjp(rms_scale, hidden, norm_mlp_all)
-    mlp_in_low = mlp_in.astype(jnp.bfloat16)
-    gate_up = jnp.dot(mlp_in_low, gu_all, preferred_element_type=jnp.float32)
-    activated, act_back = jax.vjp(swiglu, gate_up)
-    activated_low = activated.astype(jnp.bfloat16)
-    result = hidden + jnp.dot(activated_low, down_all, preferred_element_type=jnp.float32)
-    block_output = result.astype(jnp.bfloat16).reshape(block_input.shape)
-
-    d_result_low = cotangent.reshape(seg_len, width)
-    d_result = d_result_low.astype(jnp.float32)
-    grad_down = jnp.einsum("nf,nd->fd", activated_low, d_result_low, preferred_element_type=jnp.float32)
-    d_activated = jnp.einsum("nd,fd->nf", d_result_low, down_all, preferred_element_type=jnp.float32)
-    (d_gate_up,) = act_back(d_activated)
-    d_gate_low = d_gate_up.astype(jnp.bfloat16)
-    grad_gu = jnp.einsum("nd,nf->df", mlp_in_low, d_gate_low, preferred_element_type=jnp.float32)
-    d_mlp_in = jnp.einsum("nf,df->nd", d_gate_low, gu_all, preferred_element_type=jnp.float32)
-    d_hidden_norm, grad_norm_mlp = norm_mlp_back(d_mlp_in)
-    d_hidden = d_result + d_hidden_norm
-    d_mixer_low = d_hidden.astype(jnp.bfloat16)
-    grad_out = jnp.einsum("nh,nd->hd", normed_out_low, d_mixer_low, preferred_element_type=jnp.float32)
-    d_normed_out = jnp.einsum("nd,hd->nh", d_mixer_low, out_all, preferred_element_type=jnp.float32)
     if fast:
-        blocks = grad_down.astype(jnp.bfloat16).reshape(lax.axis_size("dp") * seqs, -1, width)
-        down_rows = blocks.shape[1]
-        blocks = jnp.pad(blocks, ((0, 0), (0, -down_rows % rows), (0, 0)))
-        backs = mixer_back_call(
-            vec, transfer, out_keys, mixed, projected, gain, d_normed_out, border, taps, masks, inverse, solved, entries,
-            normed_low.T.reshape(STACK + (rows, seg_len)),
-            grad_gu.astype(jnp.bfloat16).reshape(STACK + (rows, -1)),
-            blocks.reshape(STACK + (-1, width)),
-            grad_out.astype(jnp.bfloat16).reshape(STACK + (rows, -1)),
+        xt, out_keys, us, normed_out_low, mixed, gu_all = mixer_call(channels, gate, vec, masks, taps, border, gain, w_gu)
+        gu_all = gu_all.reshape(width, -1)
+    else:
+        zero_state = jnp.zeros((H, DV, DK), jnp.float32)
+        inverse, key_part, value_part, transfer, inject, out_keys, out_values, final_state = forward_call(
+            projected, border, taps, masks, vec, zero_state
         )
-        gain_parts, d_vec, tap_grads, d_projected = backs[0], backs[1], backs[2 : 2 + parts], backs[2 + parts]
-        grad_gu, grad_down, grad_out, grad_mix = backs[3 + parts :]
-        grad_down = grad_down.reshape(-1, width)[:down_rows]
+        entry = zero_state
+        device_transfer = None
+        if seqs > 2:
+            eye = jnp.broadcast_to(jnp.eye(DK, dtype=jnp.float32), (H, DK, DK))
+            device_transfer = chain_call(vec, transfer, eye)
+        for turn in range(seqs - 1):
+            leaving = final_state
+            if turn > 0:
+                leaving = leaving + jnp.einsum("hvk,hkl->hvl", entry, device_transfer, precision=HIGHEST)
+            entry = from_behind(leaving.astype(jnp.bfloat16), "seq", 1).astype(jnp.float32)
+        normed_out_low, mixed, solved, entries = readout_call(
+            vec, key_part, value_part, transfer, inject, out_keys, out_values, entry, projected, gain
+        )
+    if fast:
+        mlp_gain = jnp.broadcast_to(norm_mlp_all[None, :], (8, width))
+        backs = back_call(
+            xt, out_keys, mixed, gate, channels, us, gu_all, down_all, vec, masks, taps, border, gain,
+            out_all, mlp_gain,
+            block_input.reshape(seg_len, width), normed_out_low, cotangent.reshape(seg_len, width), mix_all.reshape(STACK + (rows, -1)), normed_t,
+        )
+        d_projected, block_output, d_hidden, d_normed, gain_parts, d_vec, grad_conv, mlp_gain_parts = backs[:8]
+        grad_gu, grad_down, grad_out, grad_mix = backs[8:]
+        block_output = block_output.reshape(block_input.shape)
+        d_hidden = d_hidden.reshape(seg_len, width)
+        grad_norm_mlp = mlp_gain_parts[0]
+        grad_down = grad_down.reshape(-1, width)[: w_down.shape[0]]
     else:
+        hidden = residual_in + jnp.dot(normed_out_low, out_all, preferred_element_type=jnp.float32)
+        mlp_in, norm_mlp_back = jax.vjp(rms_scale, hidden, norm_mlp_all)
+        mlp_in_low = mlp_in.astype(jnp.bfloat16)
+        gate_up = jnp.dot(mlp_in_low, gu_all, preferred_element_type=jnp.float32)
+        activated, act_back = jax.vjp(swiglu, gate_up)
+        activated_low = activated.astype(jnp.bfloat16)
+        result = hidden + jnp.dot(activated_low, down_all, preferred_element_type=jnp.float32)
+        block_output = result.astype(jnp.bfloat16).reshape(block_input.shape)
+
+        d_result_low = cotangent.reshape(seg_len, width)
+        d_result = d_result_low.astype(jnp.float32)
+        grad_down = jnp.einsum("nf,nd->fd", activated_low, d_result_low, preferred_element_type=jnp.float32)
+        d_activated = jnp.einsum("nd,fd->nf", d_result_low, down_all, preferred_element_type=jnp.float32)
+        (d_gate_up,) = act_back(d_activated)
+        d_gate_low = d_gate_up.astype(jnp.bfloat16)
+        grad_gu = jnp.einsum("nd,nf->df", mlp_in_low, d_gate_low, preferred_element_type=jnp.float32)
+        d_mlp_in = jnp.einsum("nf,df->nd", d_gate_low, gu_all, preferred_element_type=jnp.float32)
+        d_hidden_norm, grad_norm_mlp = norm_mlp_back(d_mlp_in)
+        d_hidden = d_result + d_hidden_norm
+        d_mixer_low = d_hidden.astype(jnp.bfloat16)
+        grad_out = jnp.einsum("nh,nd->hd", normed_out_low, d_mixer_low, preferred_element_type=jnp.float32)
+        d_normed_out = jnp.einsum("nd,hd->nh", d_mixer_low, out_all, preferred_element_type=jnp.float32)
         grad_gu = scatter_halves(grad_gu.astype(jnp.bfloat16))
         grad_down = scatter_halves(grad_down.astype(jnp.bfloat16))
         grad_out = scatter_halves(grad_out.astype(jnp.bfloat16))
@@ -1633,16 +2186,18 @@
         d_projected = lax.dynamic_update_slice(d_projected, fixed, (seg_len - tap_count + 1, 0))
         grad_mix = jnp.einsum("nd,nc->dc", normed_low, d_projected, preferred_element_type=jnp.float32)
         grad_mix = scatter_halves(grad_mix.astype(jnp.bfloat16))
+        grad_conv = jnp.concatenate(tap_grads, axis=1)
     grad_norm_out = jnp.sum(gain_parts[:, 0, :], axis=0)
     d_gates_raw, grad_decay = vec_back(d_vec)
     d_gates_low = d_gates_raw.astype(jnp.bfloat16)
     grad_small = jnp.einsum("nd,nc->dc", normed_low, d_gates_low, preferred_element_type=jnp.float32)
-    d_normed = jnp.einsum("nc,dc->nd", d_projected, mix_all, preferred_element_type=jnp.float32)
+    if not fast:
+        d_normed = jnp.einsum("nc,dc->nd", d_projected, mix_all, preferred_element_type=jnp.float32)
     d_normed = d_normed + jnp.einsum("nc,dc->nd", d_gates_low, small_all, preferred_element_type=jnp.float32)
     d_input_norm, grad_norm_in = norm_in_back(d_normed)
     input_grad = (d_hidden + d_input_norm).astype(jnp.bfloat16).reshape(block_input.shape)
 
-    grad_conv = jnp.concatenate(tap_grads, axis=1)[:tap_count]
+    grad_conv = grad_conv[:tap_count]
     devices = lax.axis_size("dp") * seqs
     conv_rows = grad_conv.reshape(tap_count, devices, -1).transpose(1, 0, 2).reshape(width, -1)
     packed = jnp.concatenate([grad_small, grad_norm_in[:, None], grad_norm_mlp[:, None], conv_rows], axis=1)

time: 579 us -> 483 us (0.83); the launches traced: 572 us -> 483 us
  matrix products: 88.3 us -> 3.36 us
  Pallas kernels: 411 us -> 421 us
  starting transfers between devices: 6.21 us -> 0.04 us
    dot_general x10 -> x0, matrix products: 85.3 us -> none  [the longest x1 14.2 us: on_device(): jnp.einsum('nc,dc->nd', d_projected, mix_all, preferred_element_type=jnp....]
    pallas_call x3 -> x2, Pallas kernels: 281 us -> 324 us  [the longest x1 227 us: back_call(): pl.pallas_call(kernel, grid=(first + 2 * H + 1,), out_shape=out_shape, in...]
    pallas_call x1, Pallas kernels: 115 us -> 81.5 us  [gather_project_call(): pl.pallas_call(gather_project_kernel, out_shape=[jax.ShapeDtypeStruct(ful...]
    ppermute x2 -> x0, starting transfers between devices: 6.13 us -> none  [from_behind(): return lax.ppermute(block, axis, route)]
  transfers between devices with their start and end apart: 4 -> 1, of which waited for: 1 -> 0; matrix products, arithmetic and copies ran while one was open for 6% -> 2% of each run, Pallas kernels for 33% -> 20%
where the time goes in v3:
time: 483 us
  Pallas kernels  421 us (87%)
  local copies, waits for them, and re-layouts  33.5 us (7%)
  between operations  15.4 us (3%)
  other arithmetic  10.1 us (2%)
    pallas_call x1, Pallas kernels, back_call(): pl.pallas_call(kernel, grid=(first + 2 * H + 1,), out_shape=out_shape, in...  227 us
    pallas_call x1, Pallas kernels, mixer_call(): pl.pallas_call(mixer_kernel, grid=(2 * steps,), out_shape=[per_head((2,)...  96.7 us
    pallas_call x1, Pallas kernels, gather_project_call(): pl.pallas_call(gather_project_kernel, out_shape=[jax.ShapeDtypeStruct(ful...  81.5 us
    pallas_call x1, Pallas kernels, total_call(): pl.pallas_call(total_kernel, out_shape=[jax.ShapeDtypeStruct((rows, wide)...  15.3 us
    unnamed x54, local copies, waits for them, and re-layouts  11.1 us
  transfers between devices with their start and end apart: 1, of which 0 were waited for; matrix products, arithmetic and copies ran while one was open for 2% of the time, Pallas kernels for 20%

profile of v3, /device:TPU:0, one launch (start us, length us, event | category | flops | bytes accessed | tf_op | source)
XLA Modules:
  0.0 483.2 jit_solution(7967135416967295375)
XLA Ops:
  7.2 0.8 reshape.218
  8.2 0.8 copy.178
  9.0 0.8 copy.179
  9.8 0.8 copy.180
  10.7 1.0 copy-done.8
  11.6 0.8 copy-done.9
  12.5 81.5 %shard_map.220 = (bf16[4,2,2,2,32,6144]{5,4,3,2,1,0:T(8,128)(2,1)}, bf16[4,2,2,2,32,1024]{5,4,3,2,1,0:T(8,128)(2,1)}, bf16[4,2,2,2,32,128]{5,4,3,2,1,0:T(8,128)(...) custom-call(bf16[512,1024]{1,0:T(8,128)(2,1)} %bitcast.128, ...), custom_call_target="tpu_custom_call" | custom-call | flops 6442450944 | bytes 60000000 | tf_op jit(solution)/shard_map/pallas_call | solution.py:663
  94.0 1.0 copy-done.4
  95.0 1.0 copy-done.5
  96.0 0.7 copy-done.7
  96.6 0.6 slice.93
  97.9 0.7 broadcast_add_fusion
  98.8 0.6 slice.84
  99.7 0.6 fusion.24
  101.1 1.3 convert_element_type.85
  103.9 0.7 pad_add_fusion
  105.3 1.0 stack.46.vec_ref
  106.6 0.7 pad_convert_fusion.tap_ref
  107.3 1.0 broadcast_in_dim.67.mask_ref
  108.3 0.6 broadcast_in_dim.68.gain_ref
  108.9 96.7 %shard_map.221 = (f32[8,2,8,128,128]{4,3,2,1,0:T(8,128)}, f32[8,8,64,128]{3,2,1,0:T(8,128)}, f32[8,2,8,128,128]{4,3,2,1,0:T(8,128)}, bf16[512,1024]{1,0:T(8,128)...) custom-call(f32[5,8,512,128]{3,2,1,0:T(8,128)} %get-tuple-element.40.channel_ref, ...), custom_call_target="tpu_custom_call" | custom-call | flops 25769803776 | bytes 80000000 | tf_op jit(solution)/shard_map/pallas_call | solution.py:885
  205.6 0.6 broadcast_in_dim.69.mlp_gain_ref
  206.2 227.3 %shard_map.222 = (bf16[512,6144]{1,0:T(8,128)(2,1)}, bf16[512,1024]{1,0:T(8,128)(2,1)}, f32[4,128,1024]{2,1,0:T(8,128)}, f32[512,1024]{1,0:T(8,128)}, f32[8,8,12...) custom-call(f32[8,2,8,128,128]{4,3,2,1,0:T(8,128)} %get-tuple-elemen, ...), custom_call_target="tpu_custom_call" | custom-call | flops 15032385536 | bytes 100000000 | tf_op jit(solution)/shard_map/pallas_call | solution.py:1701
  433.5 1.0 copy.195
  434.6 1.1 slice_reduce_fusion
  436.5 1.4 fusion.11
  437.9 0.8 slice_reduce_fusion.3
  439.3 0.5 fusion.40
  439.8 0.9 copy-done.12
  440.6 2.2 fusion.5
  442.8 1.1 concatenate.52
  444.4 0.8 slice_reduce_fusion.4
  445.2 1.1 concatenate.53
  446.4 0.9 broadcast_in_dim.71
  447.2 1.9 concatenate.51.packed_ref
  449.1 15.3 %shard_map.223 = (f32[32,128]{1,0:T(8,128)S(1)}, f32[8,128]{1,0:T(8,128)S(1)}) custom-call(f32[4,2,2,2,32,128]{5,4,3,2,1,0:T(8,128)S(1)} %concatenate.51.packed_ref, f32[8,128]{1,0:T(8,128)S(1)} %maximum_maximum_fusion.sums_ref), custom_call_target="tpu_custom_call" | custom-call | flops 1000000 | bytes 2000000 | tf_op jit(solution)/shard_map/pallas_call | solution.py:1765
  464.5 0.7 slice_reduce_fusion.1
  465.2 0.5 slice_bitcast_fusion.3
  465.7 0.5 slice_bitcast_fusion.4
  466.2 0.7 reshape.236
  466.9 0.7 copy.211
  467.6 0.8 slice.112
  468.3 3.8 fusion.1
  472.2 1.0 copy.243
  473.2 0.5 copy-done.14
  473.7 0.9 copy.244
  474.6 0.7 copy.245
  475.2 0.9 copy.246
  (109 shorter events, 6.0 us)
Async XLA Ops:
  7.2 198.4 %all-gather.2.cloned.1.call-start = ((), (), s32[]{:S(2)}) async-start(), calls=%async_computation | async-start | bytes 5947392 | tf_op jit(solution)/shard_map/all_gather | solution.py:2048
  10.6 1.0 copy-start.8
  11.6 0.8 copy-start.9
  12.5 85.4 %copy-start.17 = (bf16[88,1024]{1,0:T(8,128)(2,1)S(1)}, bf16[88,1024]{1,0:T(8,128)(2,1)}, u32[]{:S(2)}) copy-start(bf16[88,1024]{1,0:T(8,128)(2,1)} %param.24) | copy-start | bytes 540676
  12.5 86.1 %copy-start.20 = (s32[1,6]{1,0:T(1,128)S(1)}, s32[1,6]{1,0:T(1,128)}, u32[]{:S(2)}) copy-start(s32[1,6]{1,0:T(1,128)} %param.14) | copy-start | bytes 76
  12.5 87.0 %copy-start.22 = (bf16[8]{0:T(256)(128)(2,1)S(1)}, bf16[8]{0:T(256)(128)(2,1)}, u32[]{:S(2)}) copy-start(bf16[8]{0:T(256)(128)(2,1)} %param.19) | copy-start | bytes 52
  94.0 1.0 copy-start.4
  95.0 1.0 copy-start.5
  95.9 0.7 copy-start.7
  96.6 5.8 %copy-start.2 = (f32[512,128]{1,0:T(8,128)}, f32[512,128]{1,0:T(8,128)S(1)}, u32[]{:S(2)}) copy-start(f32[512,128]{1,0:T(8,128)S(1)} %get-tuple-element.42) | copy-start | bytes 786436
  96.6 6.3 %copy-start = (bf16[4,2,2,2,32,128]{5,4,3,2,1,0:T(8,128)(2,1)}, bf16[4,2,2,2,32,128]{5,4,3,2,1,0:T(8,128)(2,1)S(1)}, u32[]{:S(2)}) copy-start(bf16[4,2,2,2,32,128]{5,4,3,2,1,0:T(8,128)(2,1)S(1)} %get-tuple-element.43) | copy-start | bytes 786436
  102.9 3.4 copy-start.10
  103.1 5.2 %copy-start.21 = (bf16[128]{0:T(256)(128)(2,1)S(1)}, bf16[128]{0:T(256)(128)(2,1)}, u32[]{:S(2)}) copy-start(bf16[128]{0:T(256)(128)(2,1)} %param.20) | copy-start | bytes 772
  433.5 5.5 %copy-start.3 = (f32[512,128]{1,0:T(8,128)S(1)}, f32[512,128]{1,0:T(8,128)}, u32[]{:S(2)}) copy-start(f32[512,128]{1,0:T(8,128)} %copy-done.2) | copy-start | bytes 786436
  434.6 4.7 copy-start.6
  436.5 3.3 copy-start.1
  436.5 3.3 copy-start.11
  439.0 1.6 copy-start.12
  440.6 3.3 copy-start.19
  446.4 21.2 %copy-start.16 = (f32[3,32,1024]{2,1,0:T(8,128)S(1)}, f32[3,32,1024]{2,1,0:T(8,128)}, u32[]{:S(2)}) copy-start(f32[3,32,1024]{2,1,0:T(8,128)} %get-tuple-element.67) | copy-start | bytes 1179652
  468.3 3.9 copy-start.13
  472.2 1.5 copy-start.14
  472.2 2.4 copy-start.18
  472.2 3.0 copy-start.15
Sparse Core Ops, SparseCore 0:
  98.7 85.2 all-gather.1

commit v4 on v3

--- a/solution.py
+++ b/solution.py
@@ -524,10 +524,10 @@
 
 
 def gather_project_kernel(
-    x_ref, small_in, mix_in, out_in,
-    mix_out, out_out, small_out, normed_ref, normed_t_ref, channels_out, gate_out, gates_ref, border_ref,
+    x_ref, small_in, mix_in, out_in, down_in,
+    mix_out, out_out, down_out, small_out, normed_ref, normed_t_ref, channels_out, gate_out, gates_ref, border_ref, gains_ref,
     mix_ref, small_ref, slab_ref,
-    small_send, small_recv, small_local, send, recv, local, store_mix, store_slab, store_small, edge_send, edge_recv,
+    small_send, small_recv, small_local, send, recv, local, store_mix, store_slab, store_small, store_down, edge_send, edge_recv,
 ):
     parts, heads = channels_out.shape[0], channels_out.shape[1]
     length = x_ref.shape[0]
@@ -626,11 +626,13 @@
         if number % SPREAD_TICKS == SPREAD_TICKS - 1:
             (small.second, small.third, small.fourth, small.finish)[number // SPREAD_TICKS]()
     smalls = small_ref[...].reshape(-1, small_in.shape[1])
-    gain = jnp.transpose(smalls.astype(jnp.float32))[24:25, :]
-    normed = (scaled * gain).astype(jnp.bfloat16)
+    gains_ref[...] = jnp.transpose(smalls.astype(jnp.float32))[24:32, :]
+    normed = (scaled * gains_ref[0:1, :]).astype(jnp.bfloat16)
     normed_ref[...] = normed
     keep_small = pltpu.make_async_copy(small_ref, small_out, store_small)
     keep_small.start()
+    keep_down = pltpu.make_async_copy(down_in, down_out, store_down)
+    keep_down.start()
 
     def loop(number, carry):
         tick(number)
@@ -644,6 +646,7 @@
     release(count - 2)
     release(count - 1)
     keep_small.wait()
+    keep_down.wait()
 
     def last(index, carry):
         edge(index).wait_recv()
@@ -652,7 +655,7 @@
     lax.fori_loop(0, parts * per_part, last, 0)
 
 
-def gather_project_call(x, small, mix, out):
+def gather_project_call(x, small, mix, out, down):
     length = x.shape[0]
     rows, width = mix.shape
     everywhere = pl.BlockSpec(memory_space=pl.ANY)
@@ -665,6 +668,7 @@
         out_shape=[
             jax.ShapeDtypeStruct(full + (width,), jnp.bfloat16),
             jax.ShapeDtypeStruct(full + (out.shape[1],), jnp.bfloat16),
+            jax.ShapeDtypeStruct(down.shape, jnp.bfloat16),
             jax.ShapeDtypeStruct(full + (small.shape[1],), jnp.bfloat16),
             jax.ShapeDtypeStruct(x.shape, jnp.bfloat16),
             jax.ShapeDtypeStruct(full + (length,), jnp.bfloat16),
@@ -672,9 +676,10 @@
             jax.ShapeDtypeStruct((H, length, DK), jnp.float32),
             jax.ShapeDtypeStruct((length, small.shape[1]), jnp.float32),
             jax.ShapeDtypeStruct((8, parts * H * DK), jnp.float32),
+            jax.ShapeDtypeStruct((8, x.shape[1]), jnp.float32),
         ],
-        in_specs=[held, everywhere, everywhere, everywhere],
-        out_specs=[everywhere, everywhere, everywhere, held, held, everywhere, everywhere, held, held],
+        in_specs=[held, everywhere, everywhere, everywhere, everywhere],
+        out_specs=[everywhere, everywhere, everywhere, everywhere, held, held, everywhere, everywhere, held, held, held],
         scratch_shapes=[
             pltpu.VMEM(full + (width,), jnp.bfloat16),
             pltpu.VMEM(full + (small.shape[1],), jnp.bfloat16),
@@ -688,13 +693,14 @@
             pltpu.SemaphoreType.DMA((2,)),
             pltpu.SemaphoreType.DMA((2, block // DK)),
             pltpu.SemaphoreType.DMA,
+            pltpu.SemaphoreType.DMA,
             pltpu.SemaphoreType.DMA((2,)),
             pltpu.SemaphoreType.DMA((parts * H * DK // block,)),
         ],
         compiler_params=pltpu.CompilerParams(collective_id=1, has_side_effects=True, vmem_limit_bytes=LIMIT),
         cost_estimate=pl.CostEstimate(flops=2 * length * width * 1024, bytes_accessed=60_000_000, transcendentals=0),
-    )(x, small, mix, out)
-    return [part.reshape((-1,) + part.shape[5:]) if index < 3 else part for index, part in enumerate(outs)]
+    )(x, small, mix, out, down)
+    return [part.reshape((-1,) + part.shape[5:]) if index in (0, 1, 3) else part for index, part in enumerate(outs)]
 
 
 PAIR = 2
@@ -830,14 +836,18 @@
 
     @pl.when(step < steps)
     def _():
-        tick(step * 3)
+        def early_tick(number, carry):
+            tick(number)
+            return carry
+
+        lax.fori_loop(jnp.where(step == 0, 0, step * 3 + 1), step * 3 + 2, early_tick, 0)
         together([convolve(pair) for pair in range(PAIR)])
         masks = order_masks()
         together([chunk_terms(pair, chunk, masks) for pair in range(PAIR) for chunk in range(chunks)])
-        tick(step * 3 + 1)
+        tick(step * 3 + 2)
         together([chunk_rest(pair, chunk) for pair in range(PAIR) for chunk in range(chunks)])
         together([final_state(pair) for pair in range(PAIR)])
-        tick(step * 3 + 2)
+        tick(step * 3 + 3)
 
     @pl.when(step == steps - 1)
     def _():
@@ -849,7 +859,7 @@
 
     @pl.when(step >= steps)
     def _():
-        tick(steps * 3 + step - steps)
+        tick(steps * 3 + 1 + step - steps)
         together([readout(pair) for pair in range(PAIR)])
 
     @pl.when(step == 2 * steps - 1)
@@ -858,7 +868,7 @@
             tick(number)
             return carry
 
-        lax.fori_loop(steps * 4, max(count + SPREAD_FILL, steps * 4), drain, 0)
+        lax.fori_loop(steps * 4 + 1, max(count + SPREAD_FILL, steps * 4 + 1), drain, 0)
 
 
 def held_specs(count):
@@ -1246,8 +1256,6 @@
             lax.fori_loop(0, quarter, one, 0)
             d_mixed_ref[...] = jnp.zeros_like(d_mixed_ref)
             left_ref[0] = transposed(all_ref[3])
-            left_ref[1] = transposed(all_ref[1])
-            act_t_ref[:, :, :, :, shard:, :] = jnp.zeros(STACK + (act_t_ref.shape[4] - shard, length), jnp.float32)
 
         def mlp_block(block):
             mlp_in = all_ref[3]
@@ -1420,10 +1428,10 @@
             d_keys = (
                 tail * d_tail_keys
                 - beta * scale * d_right_entry
-                + mm3(d_gram, keys)
-                + mm3(d_query_gram, queries, 0, 0)
+                + mm(d_gram, keys)
+                + mm(d_query_gram, queries, 0, 0)
             )
-            d_queries = mm3(d_query_gram, keys) + scale[:GROUP] * d_query_entry
+            d_queries = mm(d_query_gram, keys) + scale[:GROUP] * d_query_entry
             d_values = beta * d_right
             yield
             none = jnp.zeros((GROUP, 1), jnp.float32)
@@ -1494,6 +1502,11 @@
         def _():
             mlp_block(step - 1)
 
+            @pl.when(step == 2)
+            def _():
+                left_ref[1] = transposed(all_ref[1])
+                act_t_ref[:, :, :, :, shard:, :] = jnp.zeros(STACK + (act_t_ref.shape[4] - shard, length), jnp.float32)
+
         @pl.when(step == blocks + 1)
         def _():
             leave_mlp()
@@ -1584,28 +1597,40 @@
             d_mixed_ref[...] = jnp.zeros_like(d_mixed_ref)
             per_part = H * DK // length
 
-            def drain(index, carry):
-                tick(late_tick + H + 5 + index)
-                load(index).wait()
-                here = pl.ds(pl.multiple_of(lax.rem(index, per_part) * length, length), length)
-                left = all_ref[index // per_part, :, here]
-                added = mm(left, left_ref[lax.rem(index, 2)].reshape(-1, length), 1, 1)
-                for head, place_ in enumerate(head_slices()):
-                    d_mixed_ref[head] = d_mixed_ref[head] + added[:, place_]
-
-                @pl.when(index + 2 < loads)
+            d_normed_stores = [
+                pltpu.make_async_copy(d_mixed_ref.at[head], d_normed_out.at[:, here], out_sem.at[head])
+                for head, here in enumerate(head_slices())
+            ]
+
+            def drain(turn, carry):
+                tick(late_tick + H + 5 + turn)
+
+                @pl.when(turn < loads // 2)
                 def _():
-                    load(index + 2).start()
+                    for slot in range(2):
+                        index = 2 * turn + slot
+                        load(index).wait()
+                        here = pl.ds(pl.multiple_of(lax.rem(index, per_part) * length, length), length)
+                        left = all_ref[index // per_part, :, here]
+                        added = mm(left, left_ref[slot].reshape(-1, length), 1, 1)
+                        for head, place_ in enumerate(head_slices()):
+                            d_mixed_ref[head] = d_mixed_ref[head] + added[:, place_]
+
+                        @pl.when(index + 2 < loads)
+                        def _():
+                            load(index + 2).start()
+
+                @pl.when(turn == loads // 2)
+                def _():
+                    for store in d_normed_stores:
+                        store.start()
 
                 return carry
 
-            lax.fori_loop(0, loads, drain, 0)
-            assert late_tick + H + 5 + loads >= ticks
-            for head, here in enumerate(head_slices()):
-                stores.append(
-                    pltpu.make_async_copy(d_mixed_ref.at[head], d_normed_out.at[:, here], out_sem.at[head])
-                )
-                stores[-1].start()
+            turns = ticks - (late_tick + H + 5)
+            assert turns > loads // 2
+            lax.fori_loop(0, turns, drain, 0)
+            stores.extend(d_normed_stores)
             for store in stores:
                 store.wait()
 
@@ -1717,7 +1742,9 @@
     )
 
 
-def total_kernel(packed_ref, sums_ref, packed_out, sums_out, first, near, far, last, kept, pair, ring, send, recv):
+def total_kernel(
+    packed_ref, sums_ref, packed_out, sums_out, first, near, far, last, kept, low, pair, ring, send, recv
+):
     z, x, core, y = place()
     targets = peers()
     meet(targets)
@@ -1741,21 +1768,25 @@
         sums_out[...] = sums_out[...] + pair[2 * index + 1]
 
     sums_out[...] = sums_ref[...]
-    swap(packed_ref.at[:, :, 1 - core], first, 0, targets[ZS + 1])
-    kept[...] = packed_ref[:, :, core] + first[...]
-    swap(kept.at[:, 1 - x], near, 1, targets[ZS - 1])
-    kept[:, 0] = kept[:, x] + near[...]
-    swap(kept.at[:, 0, 1 - y], far, 2, targets[ZS])
-    kept[:, 0, 0] = kept[:, 0, y] + far[...]
+    low[...] = packed_ref[:, :, 1 - core].astype(jnp.bfloat16)
+    swap(low, first, 0, targets[ZS + 1])
+    kept[...] = packed_ref[:, :, core] + first[...].astype(jnp.float32)
+    low[:, 0] = kept[:, 1 - x].astype(jnp.bfloat16)
+    swap(low.at[:, 0], near, 1, targets[ZS - 1])
+    kept[:, 0] = kept[:, x] + near[...].astype(jnp.float32)
+    low[:, 0, 0] = kept[:, 0, 1 - y].astype(jnp.bfloat16)
+    swap(low.at[:, 0, 0], far, 2, targets[ZS])
+    kept[:, 0, 0] = kept[:, 0, y] + far[...].astype(jnp.float32)
+    low[:, 0, 0] = kept[:, 0, 0].astype(jnp.bfloat16)
     ring[z] = sums_out[...]
     copies = []
     for step in range(ZS - 1):
         other = lax.rem(z + 1 + step, ZS)
-        copies.append(copy(kept.at[other, 0, 0], last.at[step], 6 + 2 * step, targets[step]))
+        copies.append(copy(low.at[other, 0, 0], last.at[step], 6 + 2 * step, targets[step]))
         copies.append(copy(ring.at[z], ring.at[z], 7 + 2 * step, targets[step]))
     for made in copies:
         made.wait()
-    packed_out[...] = kept[z, 0, 0] + last[0] + last[1] + last[2]
+    packed_out[...] = kept[z, 0, 0] + sum(last[step].astype(jnp.float32) for step in range(ZS - 1))
     sums_out[...] = ring[0] + ring[1] + ring[2] + ring[3]
 
 
@@ -1768,11 +1799,12 @@
         in_specs=[held, held],
         out_specs=[held, held],
         scratch_shapes=[
+            pltpu.VMEM((ZS, 2, 2, rows, wide), jnp.bfloat16),
+            pltpu.VMEM((ZS, 2, rows, wide), jnp.bfloat16),
+            pltpu.VMEM((ZS, rows, wide), jnp.bfloat16),
+            pltpu.VMEM((ZS - 1, rows, wide), jnp.bfloat16),
             pltpu.VMEM((ZS, 2, 2, rows, wide), jnp.float32),
-            pltpu.VMEM((ZS, 2, rows, wide), jnp.float32),
-            pltpu.VMEM((ZS, rows, wide), jnp.float32),
-            pltpu.VMEM((ZS - 1, rows, wide), jnp.float32),
-            pltpu.VMEM((ZS, 2, 2, rows, wide), jnp.float32),
+            pltpu.VMEM((ZS, 2, 2, rows, wide), jnp.bfloat16),
             pltpu.VMEM((6,) + sums.shape, jnp.float32),
             pltpu.VMEM((ZS,) + sums.shape, jnp.float32),
             pltpu.SemaphoreType.DMA((12,)),
@@ -2065,13 +2097,12 @@
             [w_small, norm_in[:, None], norm_mlp[:, None], conv_w.reshape(tap_count, rows, -1).transpose(1, 2, 0).reshape(rows, -1)], axis=1
         )
         small = jnp.concatenate([small, jnp.zeros((rows, DK - small.shape[1]), small.dtype)], axis=1)
-        mix_all, out_all, small_pack, normed_low, normed_t, channels, gate, gates_raw, border = gather_project_call(
-            block_input.reshape(seg_len, width), small, w_mix, w_out
+        mix_all, out_all, down_own, small_pack, normed_low, normed_t, channels, gate, gates_raw, border, gains = gather_project_call(
+            block_input.reshape(seg_len, width), small, w_mix, w_out, w_down
         )
         small_all = small_pack[:, :smalls]
         gates_raw = gates_raw[:, :smalls]
-        norm_in_all = small_pack[:, smalls].astype(jnp.float32)
-        norm_mlp_all = small_pack[:, smalls + 1].astype(jnp.float32)
+        norm_in_all, norm_mlp_all = gains[0], gains[1]
         per_row = conv_w.shape[1] // rows
         conv_all = small_pack[:, smalls + 2 : smalls + 2 + per_row * tap_count]
         conv_all = conv_all.reshape(-1, tap_count).transpose(1, 0)
@@ -2085,7 +2116,6 @@
         projected = jnp.dot(normed_low, mix_all, preferred_element_type=jnp.float32)
         gates_raw = jnp.dot(normed_low, small_all, preferred_element_type=jnp.float32)
     if fast:
-        down_own = w_down + (gates_raw[0, 0] * 0.0).astype(w_down.dtype)
         down_all = gather(down_own)
     else:
         gu_all, down_all = gather(w_gu), gather(w_down)

time: 483 us -> 473 us (0.979)
  Pallas kernels: 421 us -> 413 us
    unnamed x54 -> x52, local copies, waits for them, and re-layouts: 11.1 us -> 11.6 us
  transfers between devices with their start and end apart: 1 -> 1, of which waited for: 0 -> 0; matrix products, arithmetic and copies ran while one was open for 2% -> 2% of each run, Pallas kernels for 20% -> 19%
where the time goes in v4:
time: 473 us
  Pallas kernels  413 us (87%)
  local copies, waits for them, and re-layouts  33.5 us (7%)
  between operations  14.7 us (3%)
  other arithmetic  9.17 us (2%)
    pallas_call x1, Pallas kernels, back_call(): pl.pallas_call(kernel, grid=(first + 2 * H + 1,), out_shape=out_shape, in...  225 us
    pallas_call x1, Pallas kernels, mixer_call(): pl.pallas_call(mixer_kernel, grid=(2 * steps,), out_shape=[per_head((2,)...  91.9 us
    pallas_call x1, Pallas kernels, gather_project_call(): pl.pallas_call(gather_project_kernel, out_shape=[jax.ShapeDtypeStruct(ful...  81.5 us
    pallas_call x1, Pallas kernels, total_call(): pl.pallas_call(total_kernel, out_shape=[jax.ShapeDtypeStruct((rows, wide)...  13.7 us
    unnamed x52, local copies, waits for them, and re-layouts  11.6 us
  transfers between devices with their start and end apart: 1, of which 0 were waited for; matrix products, arithmetic and copies ran while one was open for 2% of the time, Pallas kernels for 19%

profile of v4, /device:TPU:0, one launch (start us, length us, event | category | flops | bytes accessed | tf_op | source)
XLA Modules:
  0.0 473.3 jit_solution(17981094040031895743)
XLA Ops:
  7.2 0.8 reshape.201
  8.2 0.8 copy.170
  9.0 0.8 copy.171
  9.8 0.8 copy.172
  10.7 1.0 copy-done.8
  11.6 0.9 copy-done.9
  12.6 0.8 copy-done.10
  13.4 81.5 %shard_map.220 = (bf16[4,2,2,2,32,6144]{5,4,3,2,1,0:T(8,128)(2,1)}, bf16[4,2,2,2,32,1024]{5,4,3,2,1,0:T(8,128)(2,1)}, bf16[88,1024]{1,0:T(8,128)(2,1)}, bf16[4,2...) custom-call(bf16[512,1024]{1,0:T(8,128)(2,1)} %bitcast.126, ...), custom_call_target="tpu_custom_call" | custom-call | flops 6442450944 | bytes 60000000 | tf_op jit(solution)/shard_map/pallas_call | solution.py:666
  94.9 1.0 copy-done.2
  95.9 1.0 copy-done.5
  96.9 0.7 copy-done.7
  97.8 0.6 slice.80
  98.7 0.6 fusion.24
  100.2 1.3 convert_element_type.59
  101.5 0.5 copy.185
  102.3 0.7 pad_add_fusion
  103.7 1.0 stack.46.vec_ref
  105.0 0.7 pad_convert_fusion.tap_ref
  105.7 1.0 broadcast_in_dim.67.mask_ref
  106.7 0.6 broadcast_in_dim.68.gain_ref
  107.3 91.9 %shard_map.221 = (f32[8,2,8,128,128]{4,3,2,1,0:T(8,128)}, f32[8,8,64,128]{3,2,1,0:T(8,128)}, f32[8,2,8,128,128]{4,3,2,1,0:T(8,128)}, bf16[512,1024]{1,0:T(8,128)...) custom-call(f32[5,8,512,128]{3,2,1,0:T(8,128)} %get-tuple-element.42.channel_ref, ...), custom_call_target="tpu_custom_call" | custom-call | flops 25769803776 | bytes 80000000 | tf_op jit(solution)/shard_map/pallas_call | solution.py:895
  199.3 0.6 broadcast_in_dim.70.mlp_gain_ref
  199.9 225.4 %shard_map.222 = (bf16[512,6144]{1,0:T(8,128)(2,1)}, bf16[512,1024]{1,0:T(8,128)(2,1)}, f32[4,128,1024]{2,1,0:T(8,128)}, f32[512,1024]{1,0:T(8,128)}, f32[8,8,12...) custom-call(f32[8,2,8,128,128]{4,3,2,1,0:T(8,128)} %get-tuple-elemen, ...), custom_call_target="tpu_custom_call" | custom-call | flops 15032385536 | bytes 100000000 | tf_op jit(solution)/shard_map/pallas_call | solution.py:1726
  425.3 1.0 copy.186
  426.4 1.1 slice_reduce_fusion
  428.3 1.4 fusion.11
  429.7 0.8 slice_reduce_fusion.3
  431.0 0.5 fusion.41
  431.5 0.9 copy-done.13
  432.4 2.2 fusion.5
  434.6 1.1 concatenate.52
  436.2 0.8 slice_reduce_fusion.4
  436.9 1.1 concatenate.53
  438.1 0.9 broadcast_in_dim.72
  439.0 1.9 concatenate.51.packed_ref
  440.9 13.7 %shard_map.223 = (f32[32,128]{1,0:T(8,128)S(1)}, f32[8,128]{1,0:T(8,128)S(1)}) custom-call(f32[4,2,2,2,32,128]{5,4,3,2,1,0:T(8,128)S(1)} %concatenate.51.packed_ref, f32[8,128]{1,0:T(8,128)S(1)} %maximum_maximum_fusion.sums_ref), custom_call_target="tpu_custom_call" | custom-call | flops 1000000 | bytes 2000000 | tf_op jit(solution)/shard_map/pallas_call | solution.py:1796
  454.7 0.7 slice_reduce_fusion.1
  455.4 0.5 slice_bitcast_fusion.3
  455.9 0.5 slice_bitcast_fusion.4
  456.4 0.7 reshape.219
  457.1 0.7 copy.201
  457.7 0.8 slice.105
  458.5 3.8 fusion.1
  462.4 1.0 copy.229
  463.3 0.5 copy-done.15
  463.9 0.9 copy.230
  464.8 0.7 copy.231
  465.4 0.9 copy.232
  (105 shorter events, 4.9 us)
Async XLA Ops:
  7.2 192.1 %all-gather.2.cloned.1.call-start = ((), (), s32[]{:S(2)}) async-start(), calls=%async_computation | async-start | bytes 5947392 | tf_op jit(solution)/shard_map/all_gather | solution.py:2080
  10.6 1.0 copy-start.8
  11.6 0.9 copy-start.9
  12.6 0.8 copy-start.10
  13.4 84.2 %copy-start.20 = (s32[1,6]{1,0:T(1,128)S(1)}, s32[1,6]{1,0:T(1,128)}, u32[]{:S(2)}) copy-start(s32[1,6]{1,0:T(1,128)} %param.14) | copy-start | bytes 76
  13.4 85.0 %copy-start.22 = (bf16[8]{0:T(256)(128)(2,1)S(1)}, bf16[8]{0:T(256)(128)(2,1)}, u32[]{:S(2)}) copy-start(bf16[8]{0:T(256)(128)(2,1)} %param.19) | copy-start | bytes 52
  94.9 1.0 copy-start.2
  95.9 1.0 copy-start.5
  96.9 0.7 copy-start.7
  97.5 3.9 copy-start
  97.5 3.9 copy-start.3
  100.1 4.6 copy-start.11
  101.4 5.3 %copy-start.21 = (bf16[128]{0:T(256)(128)(2,1)S(1)}, bf16[128]{0:T(256)(128)(2,1)}, u32[]{:S(2)}) copy-start(bf16[128]{0:T(256)(128)(2,1)} %param.20) | copy-start | bytes 772
  425.3 5.5 %copy-start.1 = (f32[512,128]{1,0:T(8,128)S(1)}, f32[512,128]{1,0:T(8,128)}, u32[]{:S(2)}) copy-start(f32[512,128]{1,0:T(8,128)} %copy-done) | copy-start | bytes 786436
  426.4 4.7 copy-start.6
  428.2 3.3 copy-start.4
  428.3 3.3 copy-start.12
  430.8 1.6 copy-start.13
  432.4 3.3 copy-start.19
  438.1 19.6 %copy-start.17 = (f32[3,32,1024]{2,1,0:T(8,128)S(1)}, f32[3,32,1024]{2,1,0:T(8,128)}, u32[]{:S(2)}) copy-start(f32[3,32,1024]{2,1,0:T(8,128)} %get-tuple-element.71) | copy-start | bytes 1179652
  458.5 3.9 copy-start.14
  462.4 1.5 copy-start.15
  462.4 2.4 copy-start.18
  462.4 3.0 copy-start.16
Sparse Core Ops, SparseCore 0:
  97.7 84.7 all-gather.1

commit v5 on v4

--- a/solution.py
+++ b/solution.py
@@ -17,6 +17,7 @@
 EPSILON = 1e-06
 HIGHEST = lax.Precision.HIGHEST
 LIMIT = 50 * 1024 * 1024
+MOST = 255 * 256 * 1024
 
 
 def mm(left, right, left_dim=1, right_dim=0):
@@ -1395,24 +1396,31 @@
             queries = q_ref[here, :]
             link = link_matrix(rows_, columns)
             link_gram = jnp.where(strict, twice(link) * mm3(keys, keys, 1, 1), 0.0)
+            yield
             reading = link * mm3(queries, keys, 1, 1)
             yield
             solved = us_in[0, 0, chunk]
             entry = us_in[0, 1, chunk]
             d_mixed = d_mixed_ref[head, here]
             tail_keys = tail * keys
-            d_solved = mm3(reading, d_mixed, 0, 0) + mm3(tail_keys, d_exit, 1, 1)
+            d_solved = mm3(reading, d_mixed, 0, 0)
+            yield
+            d_solved = d_solved + mm3(tail_keys, d_exit, 1, 1)
             yield
             d_right = mm3(xt_in[0, 0, chunk], d_solved, 0, 0)
             yield
             d_lower = jnp.where(strict, -mm3(d_right, solved, 1, 1), 0.0)
             yield
             d_tail_keys = mm3(solved, d_exit)
+            yield
             d_right_entry = mm3(d_right, entry)
+            yield
             d_reading = mm3(d_mixed, solved, 1, 1)
+            yield
             d_query_entry = mm3(d_mixed, entry)
             yield
             both_scale = -jnp.sum(d_right_entry * keys, axis=1, keepdims=True)
+            yield
             lower_weight = d_lower * link_gram
             d_beta = (
                 jnp.sum(d_right * values, axis=1, keepdims=True)
@@ -1420,6 +1428,7 @@
                 + jnp.sum(lower_weight, axis=1, keepdims=True)
             )
             lower_moment = lower_weight * beta
+            yield
             reading_moment = d_reading * reading
             d_gram = beta * twice(link) * d_lower
             d_gram = d_gram + jnp.transpose(d_gram)
@@ -1731,7 +1740,7 @@
         out_specs=[anywhere] * 4 + held_specs(len(out_shape) - 4),
         scratch_shapes=scratch,
         compiler_params=pltpu.CompilerParams(
-            dimension_semantics=("arbitrary",), collective_id=2, has_side_effects=True, vmem_limit_bytes=255 * 256 * 1024
+            dimension_semantics=("arbitrary",), collective_id=2, has_side_effects=True, vmem_limit_bytes=MOST
         ),
         cost_estimate=pl.CostEstimate(
             flops=H * chunks * 14 * 2 * SPAN**3 * 4, bytes_accessed=100_000_000, transcendentals=0

time: 473 us -> 471 us (level)
  transfers between devices with their start and end apart: 1 -> 1, of which waited for: 0 -> 0; matrix products, arithmetic and copies ran while one was open for 2% -> 2% of each run, Pallas kernels for 19% -> 20%
where the time goes in v5:
time: 471 us
  Pallas kernels  410 us (87%)
  local copies, waits for them, and re-layouts  33.5 us (7%)
  between operations  14.7 us (3%)
  other arithmetic  9.17 us (2%)
    pallas_call x1, Pallas kernels, back_call(): pl.pallas_call(kernel, grid=(first + 2 * H + 1,), out_shape=out_shape, in...  223 us
    pallas_call x1, Pallas kernels, mixer_call(): pl.pallas_call(mixer_kernel, grid=(2 * steps,), out_shape=[per_head((2,)...  91.9 us
    pallas_call x1, Pallas kernels, gather_project_call(): pl.pallas_call(gather_project_kernel, out_shape=[jax.ShapeDtypeStruct(ful...  81.5 us
    pallas_call x1, Pallas kernels, total_call(): pl.pallas_call(total_kernel, out_shape=[jax.ShapeDtypeStruct((rows, wide)...  13.7 us
    unnamed x52, local copies, waits for them, and re-layouts  11.6 us
  transfers between devices with their start and end apart: 1, of which 0 were waited for; matrix products, arithmetic and copies ran while one was open for 2% of the time, Pallas kernels for 20%

profile of v5, /device:TPU:0, one launch (start us, length us, event | category | flops | bytes accessed | tf_op | source)
XLA Modules:
  0.0 470.8 jit_solution(5706636811677036891)
XLA Ops:
  7.2 0.8 reshape.201
  8.2 0.8 copy.170
  9.0 0.8 copy.171
  9.8 0.8 copy.172
  10.7 1.0 copy-done.8
  11.6 0.9 copy-done.9
  12.6 0.8 copy-done.10
  13.4 81.5 %shard_map.220 = (bf16[4,2,2,2,32,6144]{5,4,3,2,1,0:T(8,128)(2,1)}, bf16[4,2,2,2,32,1024]{5,4,3,2,1,0:T(8,128)(2,1)}, bf16[88,1024]{1,0:T(8,128)(2,1)}, bf16[4,2...) custom-call(bf16[512,1024]{1,0:T(8,128)(2,1)} %bitcast.126, ...), custom_call_target="tpu_custom_call" | custom-call | flops 6442450944 | bytes 60000000 | tf_op jit(solution)/shard_map/pallas_call | solution.py:667
  94.9 1.0 copy-done.2
  95.9 1.0 copy-done.5
  96.9 0.7 copy-done.7
  97.8 0.6 slice.80
  98.7 0.6 fusion.24
  100.2 1.3 convert_element_type.59
  101.5 0.5 copy.185
  102.3 0.7 pad_add_fusion
  103.7 1.0 stack.46.vec_ref
  105.0 0.7 pad_convert_fusion.tap_ref
  105.7 1.0 broadcast_in_dim.67.mask_ref
  106.7 0.6 broadcast_in_dim.68.gain_ref
  107.3 91.9 %shard_map.221 = (f32[8,2,8,128,128]{4,3,2,1,0:T(8,128)}, f32[8,8,64,128]{3,2,1,0:T(8,128)}, f32[8,2,8,128,128]{4,3,2,1,0:T(8,128)}, bf16[512,1024]{1,0:T(8,128)...) custom-call(f32[5,8,512,128]{3,2,1,0:T(8,128)} %get-tuple-element.42.channel_ref, ...), custom_call_target="tpu_custom_call" | custom-call | flops 25769803776 | bytes 80000000 | tf_op jit(solution)/shard_map/pallas_call | solution.py:896
  199.3 0.6 broadcast_in_dim.70.mlp_gain_ref
  199.9 222.9 %shard_map.222 = (bf16[512,6144]{1,0:T(8,128)(2,1)}, bf16[512,1024]{1,0:T(8,128)(2,1)}, f32[4,128,1024]{2,1,0:T(8,128)}, f32[512,1024]{1,0:T(8,128)}, f32[8,8,12...) custom-call(f32[8,2,8,128,128]{4,3,2,1,0:T(8,128)} %get-tuple-elemen, ...), custom_call_target="tpu_custom_call" | custom-call | flops 15032385536 | bytes 100000000 | tf_op jit(solution)/shard_map/pallas_call | solution.py:1735
  422.8 1.0 copy.186
  423.9 1.1 slice_reduce_fusion
  425.8 1.4 fusion.11
  427.2 0.8 slice_reduce_fusion.3
  428.6 0.5 fusion.41
  429.1 0.8 copy-done.13
  429.9 2.2 fusion.5
  432.1 1.1 concatenate.52
  433.7 0.8 slice_reduce_fusion.4
  434.4 1.1 concatenate.53
  435.7 0.9 broadcast_in_dim.72
  436.5 1.9 concatenate.51.packed_ref
  438.4 13.7 %shard_map.223 = (f32[32,128]{1,0:T(8,128)S(1)}, f32[8,128]{1,0:T(8,128)S(1)}) custom-call(f32[4,2,2,2,32,128]{5,4,3,2,1,0:T(8,128)S(1)} %concatenate.51.packed_ref, f32[8,128]{1,0:T(8,128)S(1)} %maximum_maximum_fusion.sums_ref), custom_call_target="tpu_custom_call" | custom-call | flops 1000000 | bytes 2000000 | tf_op jit(solution)/shard_map/pallas_call | solution.py:1805
  452.2 0.7 slice_reduce_fusion.1
  452.9 0.5 slice_bitcast_fusion.3
  453.4 0.5 slice_bitcast_fusion.4
  453.9 0.7 reshape.219
  454.6 0.7 copy.201
  455.2 0.8 slice.105
  456.0 3.8 fusion.1
  459.9 1.0 copy.229
  460.8 0.5 copy-done.15
  461.4 0.9 copy.230
  462.2 0.7 copy.231
  462.9 0.9 copy.232
  (105 shorter events, 4.9 us)
Async XLA Ops:
  7.2 192.1 %all-gather.2.cloned.1.call-start = ((), (), s32[]{:S(2)}) async-start(), calls=%async_computation | async-start | bytes 5947392 | tf_op jit(solution)/shard_map/all_gather | solution.py:2089
  10.6 1.0 copy-start.8
  11.6 0.9 copy-start.9
  12.6 0.8 copy-start.10
  13.4 84.2 %copy-start.20 = (s32[1,6]{1,0:T(1,128)S(1)}, s32[1,6]{1,0:T(1,128)}, u32[]{:S(2)}) copy-start(s32[1,6]{1,0:T(1,128)} %param.14) | copy-start | bytes 76
  13.4 85.0 %copy-start.22 = (bf16[8]{0:T(256)(128)(2,1)S(1)}, bf16[8]{0:T(256)(128)(2,1)}, u32[]{:S(2)}) copy-start(bf16[8]{0:T(256)(128)(2,1)} %param.19) | copy-start | bytes 52
  94.9 1.0 copy-start.2
  95.9 1.0 copy-start.5
  96.9 0.7 copy-start.7
  97.5 3.9 copy-start
  97.5 3.9 copy-start.3
  100.1 4.6 copy-start.11
  101.4 5.3 %copy-start.21 = (bf16[128]{0:T(256)(128)(2,1)S(1)}, bf16[128]{0:T(256)(128)(2,1)}, u32[]{:S(2)}) copy-start(bf16[128]{0:T(256)(128)(2,1)} %param.20) | copy-start | bytes 772
  422.8 5.5 %copy-start.1 = (f32[512,128]{1,0:T(8,128)S(1)}, f32[512,128]{1,0:T(8,128)}, u32[]{:S(2)}) copy-start(f32[512,128]{1,0:T(8,128)} %copy-done) | copy-start | bytes 786436
  423.9 4.7 copy-start.6
  425.8 3.3 copy-start.4
  425.8 3.3 copy-start.12
  428.3 1.6 copy-start.13
  429.9 3.3 copy-start.19
  435.7 19.6 %copy-start.17 = (f32[3,32,1024]{2,1,0:T(8,128)S(1)}, f32[3,32,1024]{2,1,0:T(8,128)}, u32[]{:S(2)}) copy-start(f32[3,32,1024]{2,1,0:T(8,128)} %get-tuple-element.71) | copy-start | bytes 1179652
  456.0 3.9 copy-start.14
  459.9 1.5 copy-start.15
  459.9 2.4 copy-start.18
  459.9 3.0 copy-start.16
Sparse Core Ops, SparseCore 0:
  97.7 84.7 all-gather.1
